TPU v7x, 128 devices: a whole 4x4x4 slice. The times are simulated.
128 devices in a mesh: node: 8 (over y, core), group: 16 (over x, z).
Axes of the slice: x: 4, y: 4, z: 4, core: 2. Of those that a mesh axis runs over, the one named last changes fastest.
Arguments:
- queries: bfloat16 [512, 8192], P('group'), may hold values from -12 to 12
- new_entry: bfloat16 [512, 2048], P('group'), may hold values from -8 to 8
- block_lists: int32 [512, 64], P('group'), may hold values from 0 to 6143, as said below
- list_lengths: int32 [512], P('group'), may hold values from 61 to 64, as said below
- block_fill: int32 [6144], P(('node', 'group')), may hold values from 1 to 16
- cache_pool: bfloat16 [6144, 16, 2048], P(('node', 'group')), may hold values from -3.5 to 3.5
Outputs:
- attended: bfloat16 [512, 8192], P('group')
Inputs may be any that keep to these rules, and one draw needn't show every extreme that they name: `block_lists`: each rollout's list holds 40 blocks shared by all rollouts, then 20 blocks of one of 8 branches, then 4 blocks of its own; no id repeats within a list. `list_lengths`: entries of a list at or past its length are ignored.
All inputs are finite; a program needn't handle non-finite values.
Results may differ from a plain program's by a relative error of at most 0.0095.
Values may be sent and summed in bfloat16 or wider, within the bound.
No kernel may reach another device: no remote copies, remote signals or barrier semaphores. Data moves between devices by JAX's collectives and lax.ppermute only.
A program may use at most 128 MiB of HBM per device.

v0:
```python
import math

import jax
import jax.numpy as jnp
from jax import lax
from jax.sharding import PartitionSpec as P

HEADS = 64
KV_HEADS = 8
HEAD_DIM = 128
BLK_TOKENS = 16


def combined_all(value, axis, join):
    pieces = jax.tree.map(lambda part: lax.all_gather(part, axis), value)
    head = jax.tree.map(lambda part: part[0], pieces)
    tail = jax.tree.map(lambda part: part[1:], pieces)
    so_far, _ = lax.scan(lambda so_far, piece: (join(so_far, piece), None), head, tail)
    return so_far


def merge_pair(first, second):
    peak_first, total_first, accum_first = first
    peak_second, total_second, accum_second = second
    peak = jnp.maximum(peak_first, peak_second)
    weight_first = jnp.exp(peak_first - peak)
    weight_second = jnp.exp(peak_second - peak)
    total = weight_first * total_first + weight_second * total_second
    accum = weight_first[..., None] * accum_first + weight_second[..., None] * accum_second
    return (peak, total, accum)


def fold_sources(parts):
    peaks, totals, accums = parts
    peak = jnp.max(peaks, axis=0)
    weight = jnp.exp(peaks - peak[None])
    return (peak, jnp.sum(weight * totals, axis=0), jnp.sum(weight[..., None] * accums, axis=0))


def local_partials(rows_query, rows_lists, rows_length, cache_pool, block_fill, first_block):
    width = KV_HEADS * HEAD_DIM
    group_size = HEADS // KV_HEADS
    scale = 1.0 / math.sqrt(HEAD_DIM)
    blocks_here = cache_pool.shape[0]
    tokens_here = blocks_here * BLK_TOKENS
    flat = cache_pool.reshape(tokens_here, 2 * width)
    keys = flat[:, :width].reshape(tokens_here, KV_HEADS, HEAD_DIM)
    values = flat[:, width:].reshape(tokens_here, KV_HEADS, HEAD_DIM)
    local_ids = first_block + jnp.arange(blocks_here, dtype=jnp.int32)
    token_live = (jnp.arange(BLK_TOKENS, dtype=jnp.int32)[None, :] < block_fill[:, None]).reshape(
        tokens_here
    )
    count = rows_query.shape[0]
    block_rows = 32

    def one_block(items):
        query, lists, length = items
        listed = jnp.arange(lists.shape[1], dtype=jnp.int32)[None, :] < length[:, None]
        hits = jnp.any((lists[:, :, None] == local_ids[None, None, :]) & listed[:, :, None], axis=1)
        spread = jnp.broadcast_to(hits[:, :, None], (block_rows, blocks_here, BLK_TOKENS)).reshape(
            block_rows, tokens_here
        )
        live = (spread & token_live[None, :])[:, None, None, :]
        grouped = query.reshape(block_rows, KV_HEADS, group_size, HEAD_DIM)
        scores = (
            jnp.einsum("bhgd,thd->bhgt", grouped, keys, preferred_element_type=jnp.float32) * scale
        )
        peak = jnp.max(jnp.where(live, scores, -1e30), axis=-1)
        weights = jnp.where(live, jnp.exp(scores - peak[..., None]), 0.0)
        total = jnp.sum(weights, axis=-1)
        accum = jnp.einsum(
            "bhgt,thd->bhgd",
            weights.astype(jnp.bfloat16),
            values,
            preferred_element_type=jnp.float32,
        )
        return (
            peak.reshape(block_rows, HEADS),
            total.reshape(block_rows, HEADS),
            accum.reshape(block_rows, HEADS, HEAD_DIM),
        )

    steps_count = count // block_rows
    peaks, totals, accums = lax.map(
        one_block,
        (
            rows_query.reshape(steps_count, block_rows, -1),
            rows_lists.reshape(steps_count, block_rows, -1),
            rows_length.reshape(steps_count, block_rows),
        ),
    )
    return (
        peaks.reshape(count, HEADS),
        totals.reshape(count, HEADS),
        accums.reshape(count, HEADS, HEAD_DIM),
    )


def finish(peak, total, accum, rows_query, rows_entry):
    width = KV_HEADS * HEAD_DIM
    group_size = HEADS // KV_HEADS
    scale = 1.0 / math.sqrt(HEAD_DIM)
    count = rows_query.shape[0]
    grouped = rows_query.astype(jnp.float32).reshape(count, KV_HEADS, group_size, HEAD_DIM)
    entry = rows_entry.astype(jnp.float32)
    own_key = entry[:, :width].reshape(count, KV_HEADS, HEAD_DIM)
    own_value = entry[:, width:].reshape(count, KV_HEADS, 1, HEAD_DIM)
    own = (jnp.einsum("bhgd,bhd->bhg", grouped, own_key) * scale).reshape(count, HEADS)
    new_peak = jnp.maximum(peak, own)
    old_weight = jnp.exp(peak - new_peak)
    own_weight = jnp.exp(own - new_peak)
    total = old_weight * total + own_weight
    widened = jnp.broadcast_to(own_value, (count, KV_HEADS, group_size, HEAD_DIM)).reshape(
        count, HEADS, HEAD_DIM
    )
    accum = old_weight[..., None] * accum + own_weight[..., None] * widened
    return (accum / total[..., None]).reshape(count, HEADS * HEAD_DIM).astype(jnp.bfloat16)


def per_device(queries, new_entry, block_lists, list_lengths, block_fill, cache_pool):
    all_query, all_lists, all_length = (
        lax.all_gather(queries, "group", axis=0, tiled=True),
        lax.all_gather(block_lists, "group", axis=0, tiled=True),
        lax.all_gather(list_lengths, "group", axis=0, tiled=True),
    )
    groups = lax.axis_size("group")
    own_rows = queries.shape[0]
    first_block = lax.axis_index(("node", "group")) * cache_pool.shape[0]
    peaks, totals, accums = local_partials(
        all_query, all_lists, all_length, cache_pool, block_fill, first_block
    )

    def by_owner(array):
        return array.reshape((groups, own_rows) + array.shape[1:])

    combined = fold_sources(
        (
            lax.all_to_all(by_owner(peaks), "group", split_axis=0, concat_axis=0, tiled=True),
            lax.all_to_all(by_owner(totals), "group", split_axis=0, concat_axis=0, tiled=True),
            lax.all_to_all(by_owner(accums), "group", split_axis=0, concat_axis=0, tiled=True),
        )
    )
    combined = combined_all(combined, "node", merge_pair)
    peak, total, accum = combined
    return finish(peak, total, accum, queries, new_entry)


def solution(mesh):
    return jax.shard_map(
        per_device,
        mesh=mesh,
        in_specs=(
            P("group", None),
            P("group", None),
            P("group", None),
            P("group"),
            P(("node", "group")),
            P(("node", "group"), None, None),
        ),
        out_specs=P("group", None),
        check_vma=False,
    )
```

profile of v0, /device:TPU:1, one launch (start us, length us, event | category | flops | bytes accessed | tf_op | source)
XLA Modules:
  0.0 750.8 jit_solution(5133855723829638361)
XLA Ops:
  10.2 14.5 %all-reduce = s32[512]{0:T(512)S(1)} all-reduce(s32[512]{0:T(512)S(1)} %dynamic-update-slice), channel_id=1, replica_groups=mesh['node'=8,'group'=16] {'group'}, use_global_device_ids=true, to_apply=%add | all-reduce | flops 512 | bytes 4096
  24.8 3.4 fusion.39
  33.2 19.5 %all_gather.27 = s32[512,64]{1,0:T(8,128)} all-gather(s32[32,64]{1,0:T(8,128)S(1)} %copy-done.4), channel_id=1, replica_groups=mesh['node'=8,'group'=16] {'group'}, dimensions={0}, use_global_device_ids=true | all-gather | bytes 139264 | tf_op jit(solution)/shard_map/all_gather | solution.py:123
  52.7 32.0 %all-gather.6.cloned.1.call-done = bf16[512,8192]{1,0:T(8,128)(2,1)} async-done(((bf16[32,8192]{1,0:T(8,128)(2,1)}), bf16[512,8192]{1,0:T(8,128)(2,1)}) %all-gather.6.cloned.1.call-update) | async-done | bytes 8388624 | tf_op jit(solution)/shard_map/all_gather | solution.py:122
  84.6 248.6 %while.30 = (s32[]{:T(128)}, f32[16,32,64]{2,1,0:T(8,128)}, f32[16,32,64]{2,1,0:T(8,128)}, f32[16,32,64,128]{3,2,1,0:T(8,128)}, s32[16,32,64]{2,1,0:T(8,128)}, /...) while((s32[]{:T(128)}, f32[16,32,64]{2,1,0:T(8,128)}, ...), condition=%wide.region_4.5_spmd.clone, body=%wide.region_0.4_spmd.clone.sunk | while | flops 822924608 | bytes 59578508 | solution.py:84
  95.3 3.8 fusion.58
  110.8 3.8 fusion.58
  126.4 3.8 fusion.58
  141.9 3.8 fusion.58
  157.4 3.8 fusion.58
  172.9 3.8 fusion.58
  188.5 3.8 fusion.58
  204.0 3.8 fusion.58
  219.6 3.8 fusion.58
  235.2 3.8 fusion.58
  250.7 3.8 fusion.58
  266.2 3.8 fusion.58
  281.7 3.8 fusion.58
  297.3 3.8 fusion.58
  312.8 3.8 fusion.58
  328.4 3.8 fusion.58
  335.1 4.6 all-to-all-start
  340.8 5.7 all-to-all-done
  346.6 10.0 %all_to_all.15 = f32[16,1,2048]{2,1,0:T(1,128)S(1)} all-to-all(f32[16,1,2048]{2,1,0:T(1,128)S(1)} %reshape.142), channel_id=1, replica_groups=mesh['node'=8,'group'=16] {'group'}, dimensions={0} | all-to-all | bytes 262144 | tf_op jit(solution)/shard_map/all_to_all | solution.py:139
  356.6 5.2 all-to-all-start.2
  364.5 283.4 %all-to-all-done.2 = f32[16,32,64,128]{3,2,1,0:T(8,128)} async-done(((f32[16,32,64,128]{3,2,1,0:T(8,128)}), f32[16,32,64,128]{3,2,1,0:T(8,128)}, u32[]{:S(2)}, u32[]{:S(2)}) %all-to-all-start.2) | async-done | bytes 16777248 | tf_op jit(solution)/shard_map/all_to_all | solution.py:140
  647.9 8.8 %multiply_reduce_fusion = f32[32,64,128]{2,1,0:T(8,128)} fusion(f32[16,32,64,128]{3,2,1,0:T(8,128)} %all-to-all-done.2, f32[16,32,64]{2,1,0:T(8,128)S(1)} %get-tuple-element.271), kind=kLoop, calls=%fused_computation.41 | loop fusion | flops 8126464 | bytes 17956864 | tf_op jit(solution)/shard_map/reduce_sum | solution.py:37
  657.6 19.6 %all-gather = f32[256,64]{1,0:T(8,128)S(1)} all-gather(f32[32,64]{1,0:T(8,128)S(1)} %reduce_max.18), channel_id=2, replica_groups=mesh['node'=8,'group'=16] {'node'}, dimensions={0}, use_global_device_ids=true | all-gather | bytes 73728 | tf_op jit(solution)/shard_map/all_gather | solution.py:15
  677.2 13.0 %all-gather.1 = f32[256,64]{1,0:T(8,128)S(1)} all-gather(f32[32,64]{1,0:T(8,128)S(1)} %get-tuple-element.270), channel_id=3, replica_groups=mesh['node'=8,'group'=16] {'node'}, dimensions={0}, use_global_device_ids=true | all-gather | bytes 73728 | tf_op jit(solution)/shard_map/all_gather | solution.py:15
  690.3 28.3 %all-gather.8.cloned.1.call-done = f32[256,64,128]{2,1,0:T(8,128)} async-done(((f32[32,64,128]{2,1,0:T(8,128)}), f32[256,64,128]{2,1,0:T(8,128)}) %all-gather.8.cloned.1.call-update) | async-done | bytes 8388624 | tf_op jit(solution)/shard_map/all_gather | solution.py:15
  718.6 7.6 %slice.54 = f32[224,64,128]{2,1,0:T(8,128)} slice(f32[256,64,128]{2,1,0:T(8,128)} %all-gather.8.cloned.1.call-done), slice={[32:256], [0:64], [0:128]} | slice | bytes 14680064 | tf_op jit(solution)/shard_map/slice | solution.py:17
  726.2 15.6 %while.29 = (s32[]{:T(128)}, f32[32,64]{1,0:T(8,128)S(1)}, f32[32,64]{1,0:T(8,128)S(1)}, f32[32,64,128]{2,1,0:T(8,128)S(1)}, f32[7,32,64]{2,1,0:T(8,128)S(1)}, /...) while((s32[]{:T(128)}, f32[32,64]{1,0:T(8,128)S(1)}, f32[32,64]{1,0:T(8,128)S(1)}, ...), condition=%wide.region_9.10_spmd, body=%wide.region_8.9_spmd.sunk | while | flops 798722 | bytes 3227749 | solution.py:18
  (447 shorter events, 218.9 us)
Async XLA Ops:
  6.5 78.1 %all-gather.6.cloned.1.call-start = ((), (), s32[]{:S(2)}) async-start(), calls=%async_computation.3 | async-start | bytes 8912896 | tf_op jit(solution)/shard_map/all_gather | solution.py:122
  28.2 4.9 copy-start.4
  28.2 56.4 %copy-start.5 = (s32[48]{0:T(128)S(1)}, s32[48]{0:T(128)}, u32[]{:S(2)}) copy-start(s32[48]{0:T(128)} %param.14) | copy-start | bytes 580
  88.0 7.3 copy-start.2
  103.5 7.3 copy-start.2
  119.1 7.3 copy-start.2
  120.5 2.7 copy-start
  134.6 7.3 copy-start.2
  136.1 2.7 copy-start
  150.1 7.3 copy-start.2
  165.7 7.3 copy-start.2
  167.1 2.7 copy-start
  181.2 7.3 copy-start.2
  182.7 2.7 copy-start
  196.8 7.3 copy-start.2
  198.2 2.7 copy-start
  212.3 7.3 copy-start.2
  213.8 2.7 copy-start
  227.9 7.3 copy-start.2
  243.4 7.3 copy-start.2
  258.9 7.3 copy-start.2
  260.4 2.7 copy-start
  274.5 7.3 copy-start.2
  290.0 7.3 copy-start.2
  305.5 7.3 copy-start.2
  321.1 7.3 copy-start.2
  335.1 11.5 %all-to-all-start = ((f32[16,1,2048]{2,1,0:T(1,128)}), f32[16,1,2048]{2,1,0:T(1,128)S(1)}, u32[]{:S(2)}, u32[]{:S(2)}) async-start(f32[16,1,2048]{2,1,0:T(1,128)} %reshape.140), calls=%async_computation | async-start | bytes 262144 | tf_op jit(solution)/shard_map/all_to_all | solution.py:138
  356.6 291.4 %all-to-all-start.2 = ((f32[16,32,64,128]{3,2,1,0:T(8,128)}), f32[16,32,64,128]{3,2,1,0:T(8,128)}, u32[]{:S(2)}, u32[]{:S(2)}) async-start(f32[16,32,64,128]{3,2,1,0:T(8,128)} %get-tuple-element.105), calls=%async_computation.2 | async-start | bytes 33554432 | tf_op jit(solution)/shard_map/all_to_all | solution.py:140
  361.7 356.9 %all-gather.8.cloned.1.call-start = ((), (), s32[]{:S(2)}) async-start(), calls=%async_computation.4 | async-start | bytes 9437184 | tf_op jit(solution)/shard_map/all_gather | solution.py:15
  647.9 8.8 %copy-start.1 = (bf16[32,8192]{1,0:T(8,128)(2,1)S(1)}, bf16[32,8192]{1,0:T(8,128)(2,1)}, u32[]{:S(2)}) copy-start(bf16[32,8192]{1,0:T(8,128)(2,1)} %param.10) | copy-start | bytes 1572868
  647.9 8.9 %copy-start.3 = (bf16[32,2048]{1,0:T(8,128)(2,1)S(1)}, bf16[32,2048]{1,0:T(8,128)(2,1)}, u32[]{:S(2)}) copy-start(bf16[32,2048]{1,0:T(8,128)(2,1)} %param.11) | copy-start | bytes 393220
  718.6 7.6 %slice-start = ((f32[256,64,128]{2,1,0:T(8,128)}), f32[32,64,128]{2,1,0:T(8,128)S(1)}, s32[]{:S(2)}) async-start(f32[256,64,128]{2,1,0:T(8,128)} %all-gather.8.cloned.1.call-done), calls=%async_computation.5 | async-start | bytes 2097152 | tf_op jit(solution)/shard_map/slice | solution.py:16
  (9 other events, 24.4 us)
Sparse Core Ops, SparseCore 0:
  9.5 75.0 all-gather.5
  656.8 61.6 all-gather.7
where the time goes:
time: 753 us; the launch traced here: 751 us
  waiting for transfers between devices  350 us (46%)
  local copies, waits for them, and re-layouts  136 us (18%)
  matrix products  84.3 us (11%)
  other arithmetic  77.7 us (10%)
  blocking collectives  76.7 us (10%)
  between operations  14.3 us (2%)
  starting transfers between devices  9.84 us (1%)
    all_to_all x1, waiting for transfers between devices, per_device(): lax.all_to_all(by_owner(accums), 'group', split_axis=0, concat_axis=0, ti...  283 us
    while x96, local copies, waits for them, and re-layouts  62.5 us
    dot_general x16, matrix products, one_block(): jnp.einsum('bhgt,thd->bhgd', weights.astype(jnp.bfloat16), values, prefer...  60.5 us
    reduce_sum x16, other arithmetic, one_block(): total = jnp.sum(weights, axis=-1)  34.1 us
    all_gather x2, blocking collectives, combined_all(): pieces = jax.tree.map(lambda part: lax.all_gather(part, axis), value)  32.6 us
    all_gather x1, waiting for transfers between devices, per_device(): lax.all_gather(queries, 'group', axis=0, tiled=True)  32 us
    dynamic_update_slice x64, local copies, waits for them, and re-layouts, local_partials(): lax.map(one_block, (rows_query.reshape(steps_count, block_rows, -1), rows...  30.5 us
    all_gather x1, waiting for transfers between devices, combined_all(): pieces = jax.tree.map(lambda part: lax.all_gather(part, axis), value)  28.3 us
  transfers between devices with their start and end apart: 4, of which 4 were waited for; matrix products, arithmetic and copies ran while one was open for 2% of the time, Pallas kernels for 0%

commit v1 on v0

v1 whole, which is shorter than its diff:
```python
import functools
import math

import jax
import jax.numpy as jnp
from jax import lax
from jax.experimental import pallas as pl
from jax.experimental.pallas import tpu as pltpu
from jax.sharding import PartitionSpec as P

HEADS = 64
KV_HEADS = 8
HEAD_DIM = 128
BLK_TOKENS = 16
ROOT_BLOCKS = 40
LIST = 64
WIDTH = KV_HEADS * HEAD_DIM
GROUP = HEADS // KV_HEADS
SCALE = 1.0 / math.sqrt(HEAD_DIM)

HOLDERS = 8
OWN_BLOCKS = 48
BLOCKS = HOLDERS * OWN_BLOCKS
PIECE_ROWS = OWN_BLOCKS * BLK_TOKENS + OWN_BLOCKS
TILE = 64
CHUNK = 16
ROWS = TILE * GROUP
TOKENS = CHUNK * BLK_TOKENS
OUT_ROWS = 32 * GROUP + 16
LOW = -1e9
DEAD = -1e30


def attend_kernel(codes, counts, kv, query, lists, out, fills, keys, values, scores):
    for source in range(HOLDERS):
        base = source * PIECE_ROWS + OWN_BLOCKS * BLK_TOKENS
        fills[pl.ds(source * OWN_BLOCKS, OWN_BLOCKS), :] = kv[
            pl.ds(base, OWN_BLOCKS), 0:HEAD_DIM
        ].astype(jnp.float32)
    values[:, HEAD_DIM:] = jnp.ones((TOKENS, HEAD_DIM), jnp.bfloat16)
    row_rollout = lax.broadcasted_iota(jnp.int32, (ROWS, HEAD_DIM), 0) // GROUP
    lane = lax.broadcasted_iota(jnp.int32, (ROWS, HEAD_DIM), 1)
    member_lanes = jnp.where(row_rollout == lane, 1.0, 0.0).astype(jnp.bfloat16)
    token = lax.broadcasted_iota(jnp.int32, (BLK_TOKENS, HEAD_DIM), 0).astype(jnp.float32)
    pick = lax.broadcasted_iota(jnp.int32, (8, HEAD_DIM), 0)
    pick_lane = lax.broadcasted_iota(jnp.int32, (8, HEAD_DIM), 1)
    picked = jnp.where(pick == pick_lane, 1.0, 0.0).astype(jnp.bfloat16)

    def start_row(block):
        source = (block * 1366) >> 16
        return pl.multiple_of(block * BLK_TOKENS + source * OWN_BLOCKS, BLK_TOKENS)

    def one_tile(tile, _):
        chunks = (counts[tile] + CHUNK - 1) // CHUNK
        rows = query[pl.ds(pl.multiple_of(tile * ROWS, ROWS), ROWS), :]
        left = jnp.concatenate([rows, member_lanes], axis=1)
        listed = lists[tile]

        def first_pass(chunk, highest):
            for slot in range(CHUNK):
                code = codes[tile * BLOCKS + chunk * CHUNK + slot]
                block = jnp.maximum(code, 0)
                row = start_row(block)
                place = pl.ds(slot * BLK_TOKENS, BLK_TOKENS)
                keys[place, 0:HEAD_DIM] = kv[pl.ds(row, BLK_TOKENS), 0:HEAD_DIM]
                member = jnp.max(
                    jnp.where(listed == code, 1.0, 0.0), axis=0, keepdims=True
                )
                live = (token < fills[pl.ds(block, 1), :]) & (member > 0.5)
                keys[place, HEAD_DIM:] = jnp.where(live, 0.0, DEAD).astype(jnp.bfloat16)
            found = lax.dot_general(
                left, keys[...], (((1,), (1,)), ((), ())), preferred_element_type=jnp.float32
            )
            scores[chunk] = found
            return jnp.maximum(highest, jnp.maximum(found[:, :HEAD_DIM], found[:, HEAD_DIM:]))

        highest = lax.fori_loop(
            0, chunks, first_pass, jnp.full((ROWS, HEAD_DIM), DEAD, jnp.float32)
        )
        peak = jnp.maximum(jnp.max(highest, axis=1, keepdims=True) * SCALE, LOW)
        peak = peak.astype(jnp.bfloat16).astype(jnp.float32)

        def second_pass(chunk, accum):
            for slot in range(CHUNK):
                code = codes[tile * BLOCKS + chunk * CHUNK + slot]
                row = start_row(jnp.maximum(code, 0))
                values[pl.ds(slot * BLK_TOKENS, BLK_TOKENS), 0:HEAD_DIM] = kv[
                    pl.ds(row, BLK_TOKENS), HEAD_DIM:
                ]
            weights = jnp.exp(scores[chunk] * SCALE - peak).astype(jnp.bfloat16)
            return accum + jnp.dot(weights, values[...], preferred_element_type=jnp.float32)

        accum = lax.fori_loop(
            0, chunks, second_pass, jnp.zeros((ROWS, 2 * HEAD_DIM), jnp.float32)
        )
        total = accum[:, HEAD_DIM:]
        coarse = total.astype(jnp.bfloat16).astype(jnp.float32)
        stats = jnp.where(lane == 0, peak, jnp.where(lane == 1, coarse, total - coarse))
        flat = lax.dot_general(
            picked,
            stats.astype(jnp.bfloat16),
            (((1,), (1,)), ((), ())),
            preferred_element_type=jnp.float32,
        )
        for part in range(TILE // 32):
            count = 32 * GROUP
            out[tile * (TILE // 32) + part, 0:count, :] = accum[
                part * count : (part + 1) * count, :HEAD_DIM
            ].astype(jnp.bfloat16)
            both = jnp.concatenate(
                [
                    flat[:, part * count : part * count + HEAD_DIM],
                    flat[:, part * count + HEAD_DIM : (part + 1) * count],
                ],
                axis=0,
            )
            out[tile * (TILE // 32) + part, count:, :] = both.astype(jnp.bfloat16)
        return 0

    lax.fori_loop(0, counts.shape[0], one_tile, 0)


def attend(codes, counts, kv, query, lists):
    vmem = pl.BlockSpec(memory_space=pltpu.VMEM)
    smem = pl.BlockSpec(memory_space=pltpu.SMEM)
    sources = query.shape[0] // (32 * GROUP)
    return pl.pallas_call(
        attend_kernel,
        out_shape=jax.ShapeDtypeStruct((sources, OUT_ROWS, HEAD_DIM), jnp.bfloat16),
        in_specs=[smem, smem, vmem, vmem, vmem],
        out_specs=vmem,
        scratch_shapes=[
            pltpu.VMEM((BLOCKS, HEAD_DIM), jnp.float32),
            pltpu.VMEM((TOKENS, 2 * HEAD_DIM), jnp.bfloat16),
            pltpu.VMEM((TOKENS, 2 * HEAD_DIM), jnp.bfloat16),
            pltpu.VMEM((BLOCKS // CHUNK, ROWS, TOKENS), jnp.float32),
        ],
        compiler_params=pltpu.CompilerParams(vmem_limit_bytes=50 * 1024 * 1024),
        cost_estimate=pl.CostEstimate(
            flops=4 * 4096 * 512 * 256, bytes_accessed=6 << 20, transcendentals=4096 * 512
        ),
        name="attend",
    )(codes, counts, kv, query, lists)


def finish_kernel(parts, query, entry, out, peaks, totals):
    sources = parts.shape[0]
    count = parts.shape[1] - 16
    which = lax.broadcasted_iota(jnp.int32, (8, 2 * HEAD_DIM), 0)
    lane = lax.broadcasted_iota(jnp.int32, (8, 2 * HEAD_DIM), 1)
    spread = jnp.where(
        lane < HEAD_DIM, jnp.where(which == 0, 1.0, 0.0), jnp.where((which == 1) | (which == 2), 1.0, 0.0)
    ).astype(jnp.bfloat16)
    rollouts = count // GROUP
    own_key = jnp.broadcast_to(
        entry[:, 0:HEAD_DIM].astype(jnp.float32)[:, None, :], (rollouts, GROUP, HEAD_DIM)
    ).reshape(count, HEAD_DIM)
    own_value = jnp.broadcast_to(
        entry[:, HEAD_DIM:].astype(jnp.float32)[:, None, :], (rollouts, GROUP, HEAD_DIM)
    ).reshape(count, HEAD_DIM)
    own = jnp.sum(query[...].astype(jnp.float32) * own_key, axis=1, keepdims=True) * SCALE
    highest = jnp.broadcast_to(own, (count, HEAD_DIM))
    for source in range(sources):
        flat = parts[source, count:, :].astype(jnp.float32)
        for half in range(count // HEAD_DIM):
            wide = lax.dot_general(
                flat[half * 8 : half * 8 + 8, :].astype(jnp.bfloat16),
                spread,
                (((0,), (0,)), ((), ())),
                preferred_element_type=jnp.float32,
            )
            place = pl.ds(half * HEAD_DIM, HEAD_DIM)
            peaks[source, place, :] = wide[:, :HEAD_DIM]
            totals[source, place, :] = wide[:, HEAD_DIM:]
        highest = jnp.maximum(highest, peaks[source])
    weight = jnp.exp(own - highest)
    total = weight
    accum = weight * own_value
    for source in range(sources):
        weight = jnp.exp(peaks[source] - highest)
        total = total + weight * totals[source]
        accum = accum + weight * parts[source, 0:count, :].astype(jnp.float32)
    out[...] = (accum / total).astype(jnp.bfloat16)


def finish(parts, query, entry):
    count = query.shape[0]
    vmem = pl.BlockSpec(memory_space=pltpu.VMEM)
    return pl.pallas_call(
        finish_kernel,
        out_shape=jax.ShapeDtypeStruct((count, HEAD_DIM), jnp.bfloat16),
        in_specs=[vmem, vmem, vmem],
        out_specs=vmem,
        scratch_shapes=[
            pltpu.VMEM((parts.shape[0], count, HEAD_DIM), jnp.float32),
            pltpu.VMEM((parts.shape[0], count, HEAD_DIM), jnp.float32),
        ],
        compiler_params=pltpu.CompilerParams(vmem_limit_bytes=50 * 1024 * 1024),
        name="finish",
    )(parts, query, entry)


def local_number(ids, column):
    device = ids // OWN_BLOCKS
    here = (device % 16) == column
    return jnp.where(here, (device // 16) * OWN_BLOCKS + ids % OWN_BLOCKS, -1)


def visits(root, lists):
    tiles = lists.shape[0]
    numbers = jnp.arange(BLOCKS, dtype=jnp.int32)
    hit = jnp.any(lists[:, :, None] == numbers, axis=1)
    hit = hit | jnp.any(root[:, None] == numbers, axis=0)[None, :]
    counts = jnp.sum(hit, axis=1, dtype=jnp.int32)
    before = (numbers[:, None] < numbers[None, :]).astype(jnp.bfloat16)
    place = jnp.dot(hit.astype(jnp.bfloat16), before, preferred_element_type=jnp.float32)
    place = jnp.where(hit, place.astype(jnp.int32), -1)
    codes = jnp.sum(
        jnp.where(place[:, None, :] == numbers[None, :, None], numbers + 2, 0), axis=2
    )
    return (codes - 2).astype(jnp.int32).reshape(tiles * BLOCKS), counts


def per_device(queries, new_entry, block_lists, list_lengths, block_fill, cache_pool):
    node = lax.axis_index("node")
    column = lax.axis_index("group")
    groups = lax.axis_size("group")
    own_rows = queries.shape[0]

    by_head = cache_pool.reshape(OWN_BLOCKS * BLK_TOKENS, 2, KV_HEADS, HEAD_DIM)
    by_head = jnp.transpose(by_head, (2, 0, 1, 3)).reshape(
        KV_HEADS, OWN_BLOCKS * BLK_TOKENS, 2 * HEAD_DIM
    )
    fill_rows = jnp.broadcast_to(
        block_fill.astype(jnp.bfloat16)[None, :, None], (KV_HEADS, OWN_BLOCKS, 2 * HEAD_DIM)
    )
    sent = jnp.concatenate([by_head, fill_rows], axis=1)
    kv = lax.all_to_all(sent, "node", split_axis=0, concat_axis=0, tiled=True)
    kv = kv.reshape(HOLDERS * PIECE_ROWS, 2 * HEAD_DIM)

    head_query = lax.dynamic_slice_in_dim(queries, node * WIDTH, WIDTH, axis=1)
    entries = jnp.arange(LIST, dtype=jnp.int32)[None, :]
    tail = jnp.where(entries < list_lengths[:, None], block_lists, 8191)[:, ROOT_BLOCKS:]
    coded = jnp.concatenate([tail // 128, tail % 128], axis=1).astype(jnp.bfloat16)
    coded = jnp.pad(coded, ((0, 0), (0, HEAD_DIM - coded.shape[1])))
    told = jnp.concatenate([head_query, coded], axis=1)
    told = lax.all_to_all(
        jnp.broadcast_to(told[None], (groups,) + told.shape),
        "group",
        split_axis=0,
        concat_axis=0,
        tiled=True,
    )
    all_query = told[:, :, :WIDTH].reshape(groups * own_rows * GROUP, HEAD_DIM)
    coded = told[:, :, WIDTH:].astype(jnp.int32).reshape(groups * own_rows, HEAD_DIM)
    count = LIST - ROOT_BLOCKS
    ids = coded[:, :count] * 128 + coded[:, count : 2 * count]
    tail = jnp.where(ids < 8191, local_number(ids, column), -1)
    root = local_number(block_lists[0, :ROOT_BLOCKS], column)
    tiles = groups * own_rows // TILE
    codes, counts = visits(root, tail.reshape(tiles, TILE * count))
    listed = jnp.concatenate(
        [
            jnp.broadcast_to(root[None, :, None], (tiles, ROOT_BLOCKS, TILE)),
            jnp.transpose(tail.reshape(tiles, TILE, count), (0, 2, 1)),
        ],
        axis=1,
    )
    listed = jnp.pad(listed, ((0, 0), (0, 0), (0, HEAD_DIM - TILE)), constant_values=-1)

    partial = attend(codes, counts, kv, all_query, listed)
    parts = lax.all_to_all(partial, "group", split_axis=0, concat_axis=0, tiled=True)
    key = lax.dynamic_slice_in_dim(new_entry, node * HEAD_DIM, HEAD_DIM, axis=1)
    value = lax.dynamic_slice_in_dim(new_entry, WIDTH + node * HEAD_DIM, HEAD_DIM, axis=1)
    done = finish(
        parts,
        head_query.reshape(own_rows * GROUP, HEAD_DIM),
        jnp.concatenate([key, value], axis=1),
    )
    gathered = lax.all_gather(done.reshape(own_rows, WIDTH), "node")
    return jnp.transpose(gathered, (1, 0, 2)).reshape(own_rows, HEADS * HEAD_DIM)


def solution(mesh):
    return jax.shard_map(
        per_device,
        mesh=mesh,
        in_specs=(
            P("group", None),
            P("group", None),
            P("group", None),
            P("group"),
            P(("node", "group")),
            P(("node", "group"), None, None),
        ),
        out_specs=P("group", None),
        check_vma=False,
    )
```

time: 753 us -> 134 us (0.18)
  waiting for transfers between devices: 350 us -> 48.4 us
  local copies, waits for them, and re-layouts: 136 us -> 17.8 us
  matrix products: 84.3 us -> 0.12 us
  other arithmetic: 77.7 us -> 10.5 us
  blocking collectives: 76.7 us -> 16.3 us
  Pallas kernels: 0 us -> 19.4 us
  between operations: 14.3 us -> 0.16 us
  starting transfers between devices: 9.84 us -> 21.5 us
    all_to_all x2 -> x3, waiting for transfers between devices: 289 us -> 48.4 us  [the longest x1 33.2 us: per_device(): kv = lax.all_to_all(sent, 'node', split_axis=0, concat_axis=0, tiled=True)]
    dot_general x33 -> x1, matrix products: 84.3 us -> 0.12 us  [visits(): jnp.dot(hit.astype(jnp.bfloat16), before, preferred_element_type=jnp.floa...]
    while x96 -> x0, local copies, waits for them, and re-layouts: 62.5 us -> none
    all_gather x2 -> x0, waiting for transfers between devices: 60.3 us -> none  [the longest x1 32 us: per_device(): lax.all_gather(queries, 'group', axis=0, tiled=True)]
    reduce_sum x18 -> x2, other arithmetic: 43 us -> 0.72 us  [the longest x1 0.6 us: visits(): jnp.sum(jnp.where(place[:, None, :] == numbers[None, :, None], numbers +...]
    all_gather x3 -> x1, blocking collectives: 52.2 us -> 16.3 us  [per_device(): gathered = lax.all_gather(done.reshape(own_rows, WIDTH), 'node')]
    dynamic_update_slice x64 -> x0, local copies, waits for them, and re-layouts: 30.5 us -> none  [local_partials(): lax.map(one_block, (rows_query.reshape(steps_count, block_rows, -1), rows...]
    pallas_call x0 -> x2, Pallas kernels: none -> 19.4 us  [the longest x1 18.1 us: attend(): pl.pallas_call(attend_kernel, out_shape=jax.ShapeDtypeStruct((sources, OU...]
  transfers between devices with their start and end apart: 4 -> 3, of which waited for: 4 -> 2; matrix products, arithmetic and copies ran while one was open for 2% -> 18% of each run, Pallas kernels for 0% -> 0%
where the time goes in v1:
time: 134 us
  waiting for transfers between devices  48.4 us (36%)
  starting transfers between devices  21.5 us (16%)
  Pallas kernels  19.4 us (14%)
  local copies, waits for them, and re-layouts  17.8 us (13%)
  blocking collectives  16.3 us (12%)
  other arithmetic  10.5 us (8%)
    all_to_all x1, waiting for transfers between devices, per_device(): kv = lax.all_to_all(sent, 'node', split_axis=0, concat_axis=0, tiled=True)  33.2 us
    pallas_call x1, Pallas kernels, attend(): pl.pallas_call(attend_kernel, out_shape=jax.ShapeDtypeStruct((sources, OU...  18.1 us
    all_gather x1, blocking collectives, per_device(): gathered = lax.all_gather(done.reshape(own_rows, WIDTH), 'node')  16.3 us
    all_to_all x1, waiting for transfers between devices, per_device(): lax.all_to_all(partial, 'group', split_axis=0, concat_axis=0, tiled=True)  15.3 us
    all_to_all x1, starting transfers between devices, per_device(): lax.all_to_all(jnp.broadcast_to(told[None], (groups,) + told.shape), 'gro...  8.43 us
    all_to_all x1, starting transfers between devices, per_device(): kv = lax.all_to_all(sent, 'node', split_axis=0, concat_axis=0, tiled=True)  7.53 us
    reshape x1, local copies, waits for them, and re-layouts, per_device(): jnp.transpose(by_head, (2, 0, 1, 3))  6.01 us
    all_to_all x1, starting transfers between devices, per_device(): lax.all_to_all(partial, 'group', split_axis=0, concat_axis=0, tiled=True)  5.5 us
  transfers between devices with their start and end apart: 3, of which 2 were waited for; matrix products, arithmetic and copies ran while one was open for 18% of the time, Pallas kernels for 0%

profile of v1, /device:TPU:1, one launch (start us, length us, event | category | flops | bytes accessed | tf_op | source)
XLA Modules:
  0.0 134.1 jit_solution(7487242036727534439)
XLA Ops:
  0.0 0.0 copy-start
  0.0 1.0 copy-done
  1.0 0.8 fusion.11
  1.9 0.1 fusion.17
  2.0 1.1 broadcast_in_dim.26
  3.1 8.4 %all-to-all-start = ((bf16[16,32,1152]{2,1,0:T(8,128)(2,1)}), bf16[16,32,1152]{2,1,0:T(8,128)(2,1)S(1)}, u32[]{:S(2)}, u32[]{:S(2)}) async-start(bf16[16,32,1152]{2,1,0:T(8,128)(2,1)} %broadcast_in_dim.26), calls=%async_computation | async-start | bytes 2359296 | tf_op jit(solution)/shard_map/all_to_all | solution.py:247
  11.5 2.9 %copy.32 = bf16[96,8,16,128]{3,2,1,0:T(8,128)(2,1)S(1)} copy(bf16[96,8,16,128]{3,1,2,0:T(8,128)(2,1)} %bitcast.31) | data formatting | bytes 6291456
  14.4 4.1 %copy.25 = bf16[8,768,2,128]{3,2,1,0:T(2,128)(2,1)} copy(bf16[8,768,2,128]{3,0,2,1:T(8,128)(2,1)S(1)} %bitcast.30) | data formatting | bytes 6291456 | tf_op jit(solution)/shard_map/transpose | solution.py:231
  18.5 6.0 %reshape.151 = bf16[8,768,256]{2,1,0:T(8,128)(2,1)} reshape(bf16[8,768,2,128]{3,2,1,0:T(2,128)(2,1)} %copy.25) | data formatting | bytes 6291456 | tf_op jit(solution)/shard_map/reshape | solution.py:231
  24.5 4.2 %pad_maximum_fusion = bf16[8,816,256]{2,1,0:T(8,128)(2,1)} fusion(bf16[8,768,256]{2,1,0:T(8,128)(2,1)} %reshape.151, bf16[816]{0:T(1024)(128)(2,1)S(1)} %pad.15.clone), kind=kLoop, calls=%fused_computation.4 | loop fusion | flops 6684672 | bytes 6489696 | tf_op jit(solution)/shard_map/concatenate | solution.py:237
  28.7 0.0 all-to-all-done
  28.7 7.5 %all-to-all-start.1 = ((bf16[8,816,256]{2,1,0:T(8,128)(2,1)}), bf16[8,816,256]{2,1,0:T(8,128)(2,1)}, u32[]{:S(2)}, u32[]{:S(2)}) async-start(bf16[8,816,256]{2,1,0:T(8,128)(2,1)} %pad_maximum_fusion), calls=%async_computation.1 | async-start | bytes 6684672 | tf_op jit(solution)/shard_map/all_to_all | solution.py:238
  36.2 0.7 compare_select_fusion
  37.0 0.1 fusion.10
  37.1 0.6 fusion.6
  37.8 0.2 eq.71
  37.9 3.2 %fusion = pred[8,384]{1,0:T(8,128)(4,1)S(1)} fusion(s32[8,1536]{1,0:T(8,128)S(1)} %eq.71), kind=kLoop, calls=%fused_computation.1 | loop fusion | flops 9434112 | bytes 52224 | tf_op jit(solution)/shard_map/reduce_or | solution.py:212
  41.1 0.1 fusion.1
  41.2 0.6 select_reduce_fusion
  41.8 0.1 copy.27
  42.0 0.1 slice.28
  42.1 0.5 reshape.153.query
  42.6 0.1 pad_add_fusion
  42.7 0.1 convert_reduce_fusion.counts
  42.9 33.2 %all-to-all-done.1 = bf16[8,816,256]{2,1,0:T(8,128)(2,1)} async-done(((bf16[8,816,256]{2,1,0:T(8,128)(2,1)}), bf16[8,816,256]{2,1,0:T(8,128)(2,1)}, u32[]{:S(2)}, u32[]{:S(2)}) %all-to-all-start.1) | async-done | bytes 3342368 | tf_op jit(solution)/shard_map/all_to_all | solution.py:238
  76.0 18.1 %attend.1 = bf16[16,272,128]{2,1,0:T(8,128)(2,1)} custom-call(s32[3072]{0:T(1024)S(1)} %sub.38.codes, s32[8]{0:T(128)S(1)} %convert_reduce_fusion.counts, bf16[6528,256]{1,0:T(8,128)(2,1)} %bitcast.6.kv, bf16[4096,128]{1,0:T(8,128)(2,1)S(1)} %reshape.153.query, s32[8,64,128]{2,1,0:T(8,128)S(1)} %pad.9.lists), custom_call_target="tpu_custom_call" | custom-call | flops 2147483648 | bytes 6291456 | tf_op jit(solution)/shard_map/attend/pallas_call | solution.py:127
  94.1 5.5 %all-to-all-start.2 = ((bf16[16,272,128]{2,1,0:T(8,128)(2,1)}), bf16[16,272,128]{2,1,0:T(8,128)(2,1)S(1)}, u32[]{:S(2)}, u32[]{:S(2)}) async-start(bf16[16,272,128]{2,1,0:T(8,128)(2,1)} %attend.1), calls=%async_computation.2 | async-start | bytes 2228224 | tf_op jit(solution)/shard_map/all_to_all | solution.py:272
  99.7 0.7 constant_dynamic-slice_fusion.1
  100.4 15.3 %all-to-all-done.2.parts = bf16[16,272,128]{2,1,0:T(8,128)(2,1)S(1)} async-done(((bf16[16,272,128]{2,1,0:T(8,128)(2,1)}), bf16[16,272,128]{2,1,0:T(8,128)(2,1)S(1)}, u32[]{:S(2)}, u32[]{:S(2)}) %all-to-all-start.2) | async-done | bytes 1114144 | tf_op jit(solution)/shard_map/all_to_all | solution.py:272
  115.7 1.3 finish.1
  117.1 16.3 %all_gather.3 = bf16[8,32,1024]{2,1,0:T(8,128)(2,1)S(1)} all-gather(bf16[1,32,1024]{2,1,0:T(8,128)(2,1)S(1)} %all_gather_reshape.3), channel_id=1, replica_groups=mesh['node'=8,'group'=16] {'node'}, dimensions={0}, use_global_device_ids=true | all-gather | bytes 589824 | tf_op jit(solution)/shard_map/all_gather | solution.py:280
  133.3 0.8 copy.31
  (16 shorter events, 0.2 us)
Async XLA Ops:
  0.0 1.0 copy-start
  3.1 25.6 %all-to-all-start = ((bf16[16,32,1152]{2,1,0:T(8,128)(2,1)}), bf16[16,32,1152]{2,1,0:T(8,128)(2,1)S(1)}, u32[]{:S(2)}, u32[]{:S(2)}) async-start(bf16[16,32,1152]{2,1,0:T(8,128)(2,1)} %broadcast_in_dim.26), calls=%async_computation | async-start | bytes 2359296 | tf_op jit(solution)/shard_map/all_to_all | solution.py:247
  18.5 6.0 %copy-start.1 = (s32[48]{0:T(128)S(1)}, s32[48]{0:T(128)}, u32[]{:S(2)}) copy-start(s32[48]{0:T(128)} %param.10) | copy-start | bytes 580
  28.7 47.3 %all-to-all-start.1 = ((bf16[8,816,256]{2,1,0:T(8,128)(2,1)}), bf16[8,816,256]{2,1,0:T(8,128)(2,1)}, u32[]{:S(2)}, u32[]{:S(2)}) async-start(bf16[8,816,256]{2,1,0:T(8,128)(2,1)} %pad_maximum_fusion), calls=%async_computation.1 | async-start | bytes 6684672 | tf_op jit(solution)/shard_map/all_to_all | solution.py:238
  94.1 21.6 %all-to-all-start.2 = ((bf16[16,272,128]{2,1,0:T(8,128)(2,1)}), bf16[16,272,128]{2,1,0:T(8,128)(2,1)S(1)}, u32[]{:S(2)}, u32[]{:S(2)}) async-start(bf16[16,272,128]{2,1,0:T(8,128)(2,1)} %attend.1), calls=%async_computation.2 | async-start | bytes 2228224 | tf_op jit(solution)/shard_map/all_to_all | solution.py:272

commit v2 on v1

v2 whole, which is shorter than its diff:
```python
import functools
import math

import jax
import jax.numpy as jnp
from jax import lax
from jax.experimental import pallas as pl
from jax.experimental.pallas import tpu as pltpu
from jax.sharding import PartitionSpec as P

HEADS = 64
KV_HEADS = 8
HEAD_DIM = 128
BLK_TOKENS = 16
ROOT_BLOCKS = 40
LIST = 64
WIDTH = KV_HEADS * HEAD_DIM
GROUP = HEADS // KV_HEADS
SCALE = 1.0 / math.sqrt(HEAD_DIM)

HOLDERS = 8
OWN_BLOCKS = 48
BLOCKS = HOLDERS * OWN_BLOCKS
FILL_ROWS = 16
PIECE_ROWS = OWN_BLOCKS * BLK_TOKENS + FILL_ROWS
TILE = 64
CHUNK = 32
ROWS = TILE * GROUP
PACK_PARTS = 4
TOGETHER = 2
TOKENS = CHUNK * BLK_TOKENS
OUT_ROWS = 32 * GROUP + 16
LOW = -1e9
DEAD = -1e30


def pack_kernel(fill, pool, out, staged, fill_rows, arrived, left):
    tokens = OWN_BLOCKS * BLK_TOKENS
    span = tokens // PACK_PARTS

    def fetch(part):
        place = pl.ds(part * span, span)
        return pltpu.make_async_copy(pool.at[place, :], staged.at[place, :], arrived.at[part])

    def send(part, head, half):
        place = pl.ds(part * span, span)
        return pltpu.make_async_copy(
            staged.at[place, pl.ds((half * KV_HEADS + head) * HEAD_DIM, HEAD_DIM)],
            out.at[head, place, pl.ds(half * HEAD_DIM, HEAD_DIM)],
            left.at[(part * KV_HEADS + head) * 2 + half],
        )

    def send_fill(head):
        return pltpu.make_async_copy(
            fill_rows,
            out.at[head, pl.ds(tokens, FILL_ROWS), :],
            left.at[PACK_PARTS * KV_HEADS * 2 + head],
        )

    for part in range(PACK_PARTS):
        fetch(part).start()
    row = lax.broadcasted_iota(jnp.int32, (FILL_ROWS, 2 * HEAD_DIM), 0)
    part_of = lax.broadcasted_iota(jnp.int32, (FILL_ROWS, 2 * HEAD_DIM), 1) // 64
    number = part_of * FILL_ROWS + row
    filled = jnp.zeros((FILL_ROWS, 2 * HEAD_DIM), jnp.int32)
    for block in range(OWN_BLOCKS):
        filled = jnp.where(number == block, fill[block], filled)
    fill_rows[...] = filled.astype(jnp.float32).astype(jnp.bfloat16)
    for head in range(KV_HEADS):
        send_fill(head).start()
    for part in range(PACK_PARTS):
        fetch(part).wait()
        for head in range(KV_HEADS):
            for half in range(2):
                send(part, head, half).start()
    for head in range(KV_HEADS):
        send_fill(head).wait()
        for part in range(PACK_PARTS):
            for half in range(2):
                send(part, head, half).wait()


def pack(block_fill, cache_pool):
    tokens = OWN_BLOCKS * BLK_TOKENS
    return pl.pallas_call(
        pack_kernel,
        out_shape=jax.ShapeDtypeStruct((KV_HEADS, PIECE_ROWS, 2 * HEAD_DIM), jnp.bfloat16),
        in_specs=[
            pl.BlockSpec(memory_space=pltpu.SMEM),
            pl.BlockSpec(memory_space=pltpu.HBM),
        ],
        out_specs=pl.BlockSpec(memory_space=pltpu.HBM),
        scratch_shapes=[
            pltpu.VMEM((tokens, 2 * WIDTH), jnp.bfloat16),
            pltpu.VMEM((FILL_ROWS, 2 * HEAD_DIM), jnp.bfloat16),
            pltpu.SemaphoreType.DMA((PACK_PARTS,)),
            pltpu.SemaphoreType.DMA((PACK_PARTS * KV_HEADS * 2 + KV_HEADS,)),
        ],
        compiler_params=pltpu.CompilerParams(vmem_limit_bytes=60 * 1024 * 1024),
        name="pack",
    )(block_fill, cache_pool.reshape(tokens, 2 * WIDTH))


def attend_kernel(codes, counts, kv, query, barred, out, fills, keys, values, peaks, sums):
    for source in range(HOLDERS):
        base = source * PIECE_ROWS + OWN_BLOCKS * BLK_TOKENS
        packed = kv[pl.ds(base, FILL_ROWS), :].astype(jnp.float32)
        for third in range(OWN_BLOCKS // FILL_ROWS):
            start = third // 2 * HEAD_DIM
            lanes = packed[:, start : start + HEAD_DIM]
            if third % 2:
                lanes = jnp.concatenate([lanes[:, 64:], lanes[:, :64]], axis=1)
            place = pl.ds(source * OWN_BLOCKS + third * FILL_ROWS, FILL_ROWS)
            fills[place, :] = lanes
    values[:, :, HEAD_DIM:] = jnp.ones((TOGETHER, TOKENS, HEAD_DIM), jnp.bfloat16)
    row_rollout = lax.broadcasted_iota(jnp.int32, (ROWS, HEAD_DIM), 0) // GROUP
    lane = lax.broadcasted_iota(jnp.int32, (ROWS, HEAD_DIM), 1)
    member_lanes = jnp.where(row_rollout == lane, 1.0, 0.0).astype(jnp.bfloat16)
    token = lax.broadcasted_iota(jnp.int32, (BLK_TOKENS, HEAD_DIM), 0).astype(jnp.float32)
    pick = lax.broadcasted_iota(jnp.int32, (8, HEAD_DIM), 0)
    pick_lane = lax.broadcasted_iota(jnp.int32, (8, HEAD_DIM), 1)
    picked = jnp.where(pick == pick_lane, 1.0, 0.0).astype(jnp.bfloat16)

    def chunk_scores(tile, chunk, lane_of):
        rows = query[pl.ds(pl.multiple_of(tile * ROWS, ROWS), ROWS), :]
        left = jnp.concatenate([rows, member_lanes], axis=1)
        for slot in range(CHUNK):
            number = chunk * CHUNK + slot
            code = codes[tile * BLOCKS + number]
            source = (code * 1366) >> 16
            row = pl.multiple_of((code + source) * BLK_TOKENS, BLK_TOKENS)
            place = pl.ds(slot * BLK_TOKENS, BLK_TOKENS)
            keys[lane_of, place, 0:HEAD_DIM] = kv[pl.ds(row, BLK_TOKENS), 0:HEAD_DIM]
            values[lane_of, place, 0:HEAD_DIM] = kv[pl.ds(row, BLK_TOKENS), HEAD_DIM:]
            fill = jnp.where(number < counts[tile], fills[pl.ds(code, 1), :], 0.0)
            keys[lane_of, place, HEAD_DIM:] = jnp.where(
                token < fill, barred[pl.ds(tile * BLOCKS + code, 1), :], DEAD
            ).astype(jnp.bfloat16)
        return lax.dot_general(
            left, keys[lane_of], (((1,), (1,)), ((), ())), preferred_element_type=jnp.float32
        )

    def highest(found, low):
        peak = jnp.maximum(jnp.max(found, axis=1, keepdims=True) * SCALE, low)
        return peak.astype(jnp.bfloat16).astype(jnp.float32)

    def summed(found, peak, lane_of):
        weights = jnp.exp(found * SCALE - peak).astype(jnp.bfloat16)
        return jnp.dot(weights, values[lane_of], preferred_element_type=jnp.float32)

    def put_out(tile, peak, sums):
        total = sums[:, HEAD_DIM:]
        coarse = total.astype(jnp.bfloat16).astype(jnp.float32)
        stats = jnp.where(lane == 0, peak, jnp.where(lane == 1, coarse, total - coarse))
        flat = lax.dot_general(
            picked,
            stats.astype(jnp.bfloat16),
            (((1,), (1,)), ((), ())),
            preferred_element_type=jnp.float32,
        )
        for part in range(TILE // 32):
            count = 32 * GROUP
            out[tile * (TILE // 32) + part, 0:count, :] = sums[
                part * count : (part + 1) * count, 0:HEAD_DIM
            ].astype(jnp.bfloat16)
            both = jnp.concatenate(
                [
                    flat[:, part * count : part * count + HEAD_DIM],
                    flat[:, part * count + HEAD_DIM : (part + 1) * count],
                ],
                axis=0,
            )
            out[tile * (TILE // 32) + part, count:, :] = both.astype(jnp.bfloat16)

    def long_tile(tile):
        chunks = (counts[tile] + CHUNK - 1) // CHUNK
        found = chunk_scores(tile, 0, 0)
        peak = highest(found, LOW)
        peaks[...] = jnp.broadcast_to(peak, (ROWS, HEAD_DIM))
        sums[...] = summed(found, peak, 0)

        def more(chunk, _):
            found = chunk_scores(tile, chunk, 0)
            old = peaks[:, 0:1]
            peak = highest(found, old)
            sums[...] = sums[...] * jnp.exp(old - peak) + summed(found, peak, 0)
            peaks[...] = jnp.broadcast_to(peak, (ROWS, HEAD_DIM))
            return 0

        lax.fori_loop(1, chunks, more, 0)
        put_out(tile, peaks[...], sums[...])

    def some_tiles(step, _):
        tiles = [step * TOGETHER + k for k in range(TOGETHER)]
        most = counts[tiles[0]]
        for tile in tiles[1:]:
            most = jnp.maximum(most, counts[tile])

        @pl.when(most <= CHUNK)
        def _():
            found = [chunk_scores(tile, 0, k) for k, tile in enumerate(tiles)]
            peak = [highest(one, LOW) for one in found]
            added = [summed(found[k], peak[k], k) for k in range(TOGETHER)]
            for k, tile in enumerate(tiles):
                put_out(tile, peak[k], added[k])

        @pl.when(most > CHUNK)
        def _():
            lax.fori_loop(0, TOGETHER, lambda k, _: long_tile(tiles[0] + k) or 0, 0)

        return 0

    lax.fori_loop(0, counts.shape[0] // TOGETHER, some_tiles, 0)


def attend(codes, counts, kv, query, barred):
    vmem = pl.BlockSpec(memory_space=pltpu.VMEM)
    smem = pl.BlockSpec(memory_space=pltpu.SMEM)
    sources = query.shape[0] // (32 * GROUP)
    return pl.pallas_call(
        attend_kernel,
        out_shape=jax.ShapeDtypeStruct((sources, OUT_ROWS, HEAD_DIM), jnp.bfloat16),
        in_specs=[smem, smem, vmem, vmem, vmem],
        out_specs=vmem,
        scratch_shapes=[
            pltpu.VMEM((BLOCKS, HEAD_DIM), jnp.float32),
            pltpu.VMEM((TOGETHER, TOKENS, 2 * HEAD_DIM), jnp.bfloat16),
            pltpu.VMEM((TOGETHER, TOKENS, 2 * HEAD_DIM), jnp.bfloat16),
            pltpu.VMEM((ROWS, HEAD_DIM), jnp.float32),
            pltpu.VMEM((ROWS, 2 * HEAD_DIM), jnp.float32),
        ],
        compiler_params=pltpu.CompilerParams(vmem_limit_bytes=50 * 1024 * 1024),
        cost_estimate=pl.CostEstimate(
            flops=4 * 4096 * 512 * 256, bytes_accessed=6 << 20, transcendentals=4096 * 512
        ),
        name="attend",
    )(codes, counts, kv, query, barred)


def finish_kernel(parts, query, entry, out, peaks, totals, ended):
    sources = parts.shape[0]
    count = parts.shape[1] - 16
    which = lax.broadcasted_iota(jnp.int32, (8, 2 * HEAD_DIM), 0)
    lane = lax.broadcasted_iota(jnp.int32, (8, 2 * HEAD_DIM), 1)
    spread = jnp.where(
        lane < HEAD_DIM, jnp.where(which == 0, 1.0, 0.0), jnp.where((which == 1) | (which == 2), 1.0, 0.0)
    ).astype(jnp.bfloat16)
    rollouts = count // GROUP
    own_key = jnp.broadcast_to(
        entry[:, 0:HEAD_DIM].astype(jnp.float32)[:, None, :], (rollouts, GROUP, HEAD_DIM)
    ).reshape(count, HEAD_DIM)
    own_value = jnp.broadcast_to(
        entry[:, HEAD_DIM:].astype(jnp.float32)[:, None, :], (rollouts, GROUP, HEAD_DIM)
    ).reshape(count, HEAD_DIM)
    own = jnp.sum(query[...].astype(jnp.float32) * own_key, axis=1, keepdims=True) * SCALE
    highest = jnp.broadcast_to(own, (count, HEAD_DIM))
    for source in range(sources):
        flat = parts[source, count:, :].astype(jnp.float32)
        for half in range(count // HEAD_DIM):
            wide = lax.dot_general(
                flat[half * 8 : half * 8 + 8, :].astype(jnp.bfloat16),
                spread,
                (((0,), (0,)), ((), ())),
                preferred_element_type=jnp.float32,
            )
            place = pl.ds(half * HEAD_DIM, HEAD_DIM)
            peaks[source, place, :] = wide[:, :HEAD_DIM]
            totals[source, place, :] = wide[:, HEAD_DIM:]
        highest = jnp.maximum(highest, peaks[source])
    weight = jnp.exp(own - highest)
    total = weight
    accum = weight * own_value
    for source in range(sources):
        weight = jnp.exp(peaks[source] - highest)
        total = total + weight * totals[source]
        accum = accum + weight * parts[source, 0:count, :].astype(jnp.float32)
    ended[...] = accum / total
    for head in range(GROUP):
        out[:, head * HEAD_DIM : (head + 1) * HEAD_DIM] = ended[
            pl.ds(head, rollouts, stride=GROUP), :
        ].astype(jnp.bfloat16)


def finish(parts, query, entry):
    count = query.shape[0]
    vmem = pl.BlockSpec(memory_space=pltpu.VMEM)
    return pl.pallas_call(
        finish_kernel,
        out_shape=jax.ShapeDtypeStruct((count // GROUP, WIDTH), jnp.bfloat16),
        in_specs=[vmem, vmem, vmem],
        out_specs=vmem,
        scratch_shapes=[
            pltpu.VMEM((parts.shape[0], count, HEAD_DIM), jnp.float32),
            pltpu.VMEM((parts.shape[0], count, HEAD_DIM), jnp.float32),
            pltpu.VMEM((count, HEAD_DIM), jnp.float32),
        ],
        compiler_params=pltpu.CompilerParams(vmem_limit_bytes=50 * 1024 * 1024),
        name="finish",
    )(parts, query, entry)


def place_kernel(node, *refs):
    pairs, out = refs[:-1], refs[-1]
    chips = len(pairs)
    for hop in range(chips):
        chip = lax.rem(node[0] // 2 - hop + chips, chips)
        for which in range(2):
            core = lax.rem(node[0] + which, 2)
            start = pl.multiple_of((chip * 2 + core) * WIDTH, WIDTH)
            out[:, pl.ds(start, WIDTH)] = pairs[hop][which]


def place_heads(node, pairs):
    vmem = pl.BlockSpec(memory_space=pltpu.VMEM)
    rollouts = pairs[0].shape[1]
    return pl.pallas_call(
        place_kernel,
        out_shape=jax.ShapeDtypeStruct((rollouts, HEADS * HEAD_DIM), jnp.bfloat16),
        in_specs=[pl.BlockSpec(memory_space=pltpu.SMEM)] + [vmem] * len(pairs),
        out_specs=vmem,
        compiler_params=pltpu.CompilerParams(vmem_limit_bytes=16 * 1024 * 1024),
        name="place_heads",
    )(node.reshape(1).astype(jnp.int32), *pairs)


def local_number(ids, column):
    device = ids // OWN_BLOCKS
    here = (device % 16) == column
    return jnp.where(here, (device // 16) * OWN_BLOCKS + ids % OWN_BLOCKS, -1)


def visits(root, lists):
    tiles, _, rollouts = lists.shape
    numbers = jnp.arange(BLOCKS, dtype=jnp.int32)
    everyone = jnp.any(root[:, None] == numbers, axis=0)
    member = jnp.any(lists[:, :, None, :] == numbers[None, None, :, None], axis=1)
    member = member | everyone[None, :, None]
    hit = jnp.any(member, axis=2)
    counts = jnp.sum(hit, axis=1, dtype=jnp.int32)
    before = (numbers[:, None] < numbers[None, :]).astype(jnp.bfloat16)
    place = jnp.dot(hit.astype(jnp.bfloat16), before, preferred_element_type=jnp.float32)
    place = jnp.where(hit, place.astype(jnp.int32), -1)
    codes = jnp.sum(jnp.where(place[:, None, :] == numbers[None, :, None], numbers, 0), axis=2)
    barred = jnp.pad(jnp.where(member, 0.0, DEAD), ((0, 0), (0, 0), (0, HEAD_DIM - rollouts)))
    return (
        codes.astype(jnp.int32).reshape(tiles * BLOCKS),
        counts,
        barred.reshape(tiles * BLOCKS, HEAD_DIM),
    )


def per_device(queries, new_entry, block_lists, list_lengths, block_fill, cache_pool):
    node = lax.axis_index("node")
    column = lax.axis_index("group")
    groups = lax.axis_size("group")
    own_rows = queries.shape[0]

    sent = pack(block_fill, cache_pool)
    kv = lax.all_to_all(sent, "node", split_axis=0, concat_axis=0, tiled=True)
    kv = kv.reshape(HOLDERS * PIECE_ROWS, 2 * HEAD_DIM)

    head_query = lax.dynamic_slice_in_dim(queries, node * WIDTH, WIDTH, axis=1)
    entries = jnp.arange(LIST, dtype=jnp.int32)[None, :]
    tail = jnp.where(entries < list_lengths[:, None], block_lists, 8191)[:, ROOT_BLOCKS:]
    coded = jnp.concatenate([tail // 128, tail % 128], axis=1).astype(jnp.bfloat16)
    coded = jnp.pad(coded, ((0, 0), (0, HEAD_DIM - coded.shape[1])))
    told = jnp.concatenate([head_query, coded], axis=1)
    sent, told = lax.optimization_barrier((sent, told))
    side = 4
    def shifted(value, hop_x, hop_z):
        pairs = [
            (x * side + z, (x + hop_x) % side * side + (z + hop_z) % side)
            for x in range(side)
            for z in range(side)
        ]
        return lax.ppermute(value, "group", pairs)

    line = jnp.stack([told] + [shifted(told, 0, hop) for hop in range(1, side)])
    told = jnp.stack([line] + [shifted(line, hop, 0) for hop in range(1, side)])
    column_x, column_z = column // side, column % side
    order = jnp.arange(side, dtype=jnp.int32)
    told = jnp.take(told, (column_x - order) % side, axis=0)
    told = jnp.take(told, (column_z - order) % side, axis=1)
    told = told.reshape((groups,) + told.shape[2:])
    all_query = told[:, :, :WIDTH].reshape(groups * own_rows * GROUP, HEAD_DIM)
    coded = told[:, :, WIDTH:].astype(jnp.int32).reshape(groups * own_rows, HEAD_DIM)
    count = LIST - ROOT_BLOCKS
    ids = coded[:, :count] * 128 + coded[:, count : 2 * count]
    tail = jnp.where(ids < 8191, local_number(ids, column), -1)
    root = local_number(block_lists[0, :ROOT_BLOCKS], column)
    tiles = groups * own_rows // TILE
    codes, counts, barred = visits(
        root, jnp.transpose(tail.reshape(tiles, TILE, count), (0, 2, 1))
    )
    partial = attend(codes, counts, kv, all_query, barred)
    parts = lax.all_to_all(partial, "group", split_axis=0, concat_axis=0, tiled=True)
    key = lax.dynamic_slice_in_dim(new_entry, node * HEAD_DIM, HEAD_DIM, axis=1)
    value = lax.dynamic_slice_in_dim(new_entry, WIDTH + node * HEAD_DIM, HEAD_DIM, axis=1)
    done = finish(
        parts,
        head_query.reshape(own_rows * GROUP, HEAD_DIM),
        jnp.concatenate([key, value], axis=1),
    )
    nodes = lax.axis_size("node")
    other = lax.ppermute(done, "node", [(i, i ^ 1) for i in range(nodes)])
    pair = jnp.stack([done, other])
    pairs = [pair] + [
        lax.ppermute(pair, "node", [(i, (i + 2 * hop) % nodes) for i in range(nodes)])
        for hop in range(1, nodes // 2)
    ]
    return place_heads(node, pairs)


def solution(mesh):
    return jax.shard_map(
        per_device,
        mesh=mesh,
        in_specs=(
            P("group", None),
            P("group", None),
            P("group", None),
            P("group"),
            P(("node", "group")),
            P(("node", "group"), None, None),
        ),
        out_specs=P("group", None),
        check_vma=False,
    )
```

time: 134 us -> 98.1 us (0.73)
  blocking collectives: 16.3 us -> 0 us
  local copies, waits for them, and re-layouts: 17.8 us -> 6.35 us
  starting transfers between devices: 21.5 us -> 28.7 us
  waiting for transfers between devices: 48.4 us -> 41.8 us
  other arithmetic: 10.5 us -> 5.64 us
  Pallas kernels: 19.4 us -> 14.8 us
    all_to_all x1, waiting for transfers between devices: 33.2 us -> 0.01 us  [per_device(): kv = lax.all_to_all(sent, 'node', split_axis=0, concat_axis=0, tiled=True)]
    ppermute x0 -> x10, waiting for transfers between devices: none -> 26.5 us  [the longest x6 17.3 us: shifted(): return lax.ppermute(value, 'group', pairs)]
    all_gather x1 -> x0, blocking collectives: 16.3 us -> none  [per_device(): gathered = lax.all_gather(done.reshape(own_rows, WIDTH), 'node')]
    ppermute x0 -> x10, starting transfers between devices: none -> 15.5 us  [the longest x6 10 us: shifted(): return lax.ppermute(value, 'group', pairs)]
    pallas_call x1, Pallas kernels: 18.1 us -> 8.28 us  [attend(): pl.pallas_call(attend_kernel, out_shape=jax.ShapeDtypeStruct((sources, OU...]
    all_to_all x1 -> x0, starting transfers between devices: 8.43 us -> none  [per_device(): lax.all_to_all(jnp.broadcast_to(told[None], (groups,) + told.shape), 'gro...]
    reshape x2 -> x1, local copies, waits for them, and re-layouts: 6.84 us -> 0.01 us  [visits(): codes.astype(jnp.int32).reshape(tiles * BLOCKS)]
    pallas_call x1 -> x3, Pallas kernels: 1.32 us -> 6.51 us  [the longest x1 4.33 us: pack(): pl.pallas_call(pack_kernel, out_shape=jax.ShapeDtypeStruct((KV_HEADS, PIE...]
  transfers between devices with their start and end apart: 3 -> 12, of which waited for: 2 -> 10; matrix products, arithmetic and copies ran while one was open for 18% -> 12% of each run, Pallas kernels for 0% -> 0%
where the time goes in v2:
time: 98.1 us; the launch traced here: 97.6 us
  waiting for transfers between devices  41.8 us (43%)
  starting transfers between devices  28.7 us (29%)
  Pallas kernels  14.8 us (15%)
  local copies, waits for them, and re-layouts  6.35 us (6%)
  other arithmetic  5.64 us (6%)
    ppermute x6, waiting for transfers between devices, shifted(): return lax.ppermute(value, 'group', pairs)  17.3 us
    all_to_all x1, waiting for transfers between devices, per_device(): lax.all_to_all(partial, 'group', split_axis=0, concat_axis=0, tiled=True)  15.3 us
    ppermute x6, starting transfers between devices, shifted(): return lax.ppermute(value, 'group', pairs)  10 us
    ppermute x3, waiting for transfers between devices, per_device(): lax.ppermute(pair, 'node', [(i, (i + 2 * hop) % nodes) for i in range(nod...  8.34 us
    pallas_call x1, Pallas kernels, attend(): pl.pallas_call(attend_kernel, out_shape=jax.ShapeDtypeStruct((sources, OU...  8.28 us
    all_to_all x1, starting transfers between devices, per_device(): lax.all_to_all(partial, 'group', split_axis=0, concat_axis=0, tiled=True)  7.15 us
    all_to_all x1, starting transfers between devices, per_device(): kv = lax.all_to_all(sent, 'node', split_axis=0, concat_axis=0, tiled=True)  5.98 us
    pallas_call x1, Pallas kernels, pack(): pl.pallas_call(pack_kernel, out_shape=jax.ShapeDtypeStruct((KV_HEADS, PIE...  4.33 us
  transfers between devices with their start and end apart: 12, of which 10 were waited for; matrix products, arithmetic and copies ran while one was open for 12% of the time, Pallas kernels for 0%

profile of v2, /device:TPU:1, one launch (start us, length us, event | category | flops | bytes accessed | tf_op | source)
XLA Modules:
  0.0 97.6 jit_solution(13184336722071880158)
XLA Ops:
  0.0 4.3 %pack.1 = bf16[8,784,256]{2,1,0:T(8,128)(2,1)} custom-call(s32[48]{0:T(128)} %fill.1, bf16[768,2048]{1,0:T(8,128)(2,1)} %bitcast.46), custom_call_target="tpu_custom_call" | custom-call | tf_op jit(solution)/shard_map/pack/pallas_call | solution.py:85
  4.4 6.0 %all-to-all-start = ((bf16[8,784,256]{2,1,0:T(8,128)(2,1)}), bf16[8,784,256]{2,1,0:T(8,128)(2,1)}, u32[]{:S(2)}, u32[]{:S(2)}) async-start(bf16[8,784,256]{2,1,0:T(8,128)(2,1)} %pack.1), calls=%async_computation | async-start | bytes 6422528 | tf_op jit(solution)/shard_map/all_to_all | solution.py:359
  10.6 3.8 %collective-permute-start.2 = (bf16[32,1152]{1,0:T(8,128)(2,1)S(1)}, bf16[32,1152]{1,0:T(8,128)(2,1)S(1)}, u32[]{:S(2)}, u32[]{:S(2)}) collective-permute-start(bf16[32,1152]{1,0:T(8,128)(2,1)S(1)} %pad_maximum_fusion.3), channel_id=1, source_target_pairs={{0,3},{1,0},{2,1},{3,2},{4,7},{5,4},{6,5},{7,6},{8,11},{9,8},{10,9... | collective-permute-start | bytes 221192 | tf_op jit(solution)/shard_map/ppermute | solution.py:376
  14.4 0.7 collective-permute-start
  15.3 2.3 %collective-permute-done.2 = bf16[32,1152]{1,0:T(8,128)(2,1)S(1)} collective-permute-done((bf16[32,1152]{1,0:T(8,128)(2,1)S(1)}, bf16[32,1152]{1,0:T(8,128)(2,1)S(1)}, u32[]{:S(2)}, u32[]{:S(2)}) %collective-permute-start.2) | collective-permute-done | bytes 73760 | tf_op jit(solution)/shard_map/ppermute | solution.py:376
  17.5 2.0 %collective-permute-done.1 = bf16[32,1152]{1,0:T(8,128)(2,1)S(1)} collective-permute-done((bf16[32,1152]{1,0:T(8,128)(2,1)S(1)}, bf16[32,1152]{1,0:T(8,128)(2,1)S(1)}, u32[]{:S(2)}, u32[]{:S(2)}) %collective-permute-start.1) | collective-permute-done | bytes 73760 | tf_op jit(solution)/shard_map/ppermute | solution.py:376
  19.6 1.7 %collective-permute-done = bf16[32,1152]{1,0:T(8,128)(2,1)S(1)} collective-permute-done((bf16[32,1152]{1,0:T(8,128)(2,1)S(1)}, bf16[32,1152]{1,0:T(8,128)(2,1)S(1)}, u32[]{:S(2)}, u32[]{:S(2)}) %collective-permute-start) | collective-permute-done | bytes 73760 | tf_op jit(solution)/shard_map/ppermute | solution.py:376
  21.3 2.8 %collective-permute-start.4 = (bf16[4,32,1152]{2,1,0:T(8,128)(2,1)S(1)}, bf16[4,32,1152]{2,1,0:T(8,128)(2,1)S(1)}, u32[]{:S(2)}, u32[]{:S(2)}) collective-permute-start(bf16[4,32,1152]{2,1,0:T(8,128)(2,1)S(1)} %get-tuple-element.8), channel_id=1, source_target_pairs={{0,8},{1,9},{2,10},{3,11},{4,12},{5,13},{6,14},{7,15},{8,0},{9,1},... | collective-permute-start | bytes 884744 | tf_op jit(solution)/shard_map/ppermute | solution.py:376
  24.4 2.4 %collective-permute-start.5 = (bf16[4,32,1152]{2,1,0:T(8,128)(2,1)S(1)}, bf16[4,32,1152]{2,1,0:T(8,128)(2,1)S(1)}, u32[]{:S(2)}, u32[]{:S(2)}) collective-permute-start(bf16[4,32,1152]{2,1,0:T(8,128)(2,1)S(1)} %get-tuple-element.8), channel_id=1, source_target_pairs={{0,12},{1,13},{2,14},{3,15},{4,0},{5,1},{6,2},{7,3},{8,4},{9,5},{1... | collective-permute-start | bytes 884744 | tf_op jit(solution)/shard_map/ppermute | solution.py:376
  26.9 3.9 %collective-permute-done.4 = bf16[4,32,1152]{2,1,0:T(8,128)(2,1)S(1)} collective-permute-done((bf16[4,32,1152]{2,1,0:T(8,128)(2,1)S(1)}, bf16[4,32,1152]{2,1,0:T(8,128)(2,1)S(1)}, u32[]{:S(2)}, u32[]{:S(2)}) %collective-permute-start.4) | collective-permute-done | bytes 294944 | tf_op jit(solution)/shard_map/ppermute | solution.py:376
  30.8 7.4 %collective-permute-done.3 = bf16[4,32,1152]{2,1,0:T(8,128)(2,1)S(1)} collective-permute-done((bf16[4,32,1152]{2,1,0:T(8,128)(2,1)S(1)}, bf16[4,32,1152]{2,1,0:T(8,128)(2,1)S(1)}, u32[]{:S(2)}, u32[]{:S(2)}) %collective-permute-start.3) | collective-permute-done | bytes 294944 | tf_op jit(solution)/shard_map/ppermute | solution.py:376
  38.4 0.7 gather_fusion
  39.3 0.7 gather_fusion.1
  40.6 0.5 reshape.211.query
  41.1 0.6 fusion.6
  41.9 3.1 %fusion = pred[8,384,64]{1,2,0:T(8,128)(4,1)S(1)} fusion(s32[8,24,64]{2,1,0:T(8,128)S(1)} %bitcast.48), kind=kLoop, calls=%fused_computation.3 | loop fusion | flops 9240576 | bytes 245760 | tf_op jit(solution)/shard_map/reduce_or | solution.py:336
  45.2 0.6 select_reduce_fusion
  45.9 1.6 %copy.14 = f32[8,384,64]{2,1,0:T(8,128)} copy(f32[8,384,64]{1,2,0:T(8,128)S(1)} %or_select_fusion) | data formatting | bytes 1572864
  47.5 1.5 %pad.9.clone = f32[8,384,128]{2,1,0:T(8,128)S(1)} pad(f32[8,384,64]{2,1,0:T(8,128)} %copy.14, f32[]{:T(128)} %constant.182.clone.1), padding=0_0x0_0x0_64 | pad | bytes 2359300 | tf_op jit(solution)/shard_map/jit(_pad)/pad | solution.py:344
  49.2 8.3 %attend.1 = bf16[16,272,128]{2,1,0:T(8,128)(2,1)} custom-call(s32[3072]{0:T(1024)S(1)} %reshape.209.codes, s32[8]{0:T(128)S(1)} %convert_reduce_fusion.counts, bf16[6272,256]{1,0:T(8,128)(2,1)} %bitcast.21.kv, bf16[4096,128]{1,0:T(8,128)(2,1)S(1)} %reshape.211.query, f32[3072,128]{1,0:T(8,128)S(1)} %bitcast.43), custom_call_target="tpu_custom_call" | custom-call | flops 2147483648 | bytes 6291456 | tf_op jit(solution)/shard_map/attend/pallas_call | solution.py:220
  57.4 7.2 %all-to-all-start.1 = ((bf16[16,272,128]{2,1,0:T(8,128)(2,1)}), bf16[16,272,128]{2,1,0:T(8,128)(2,1)S(1)}, u32[]{:S(2)}, u32[]{:S(2)}) async-start(bf16[16,272,128]{2,1,0:T(8,128)(2,1)} %attend.1), calls=%async_computation.1 | async-start | bytes 2228224 | tf_op jit(solution)/shard_map/all_to_all | solution.py:396
  64.7 0.7 constant_dynamic-slice_fusion
  65.4 15.3 %all-to-all-done.1.parts = bf16[16,272,128]{2,1,0:T(8,128)(2,1)S(1)} async-done(((bf16[16,272,128]{2,1,0:T(8,128)(2,1)}), bf16[16,272,128]{2,1,0:T(8,128)(2,1)S(1)}, u32[]{:S(2)}, u32[]{:S(2)}) %all-to-all-start.1) | async-done | bytes 1114144 | tf_op jit(solution)/shard_map/all_to_all | solution.py:396
  80.7 1.3 %finish.1 = bf16[32,1024]{1,0:T(8,128)(2,1)S(1)} custom-call(bf16[16,272,128]{2,1,0:T(8,128)(2,1)S(1)} %all-to-all-done.1.parts, bf16[256,128]{1,0:T(8,128)(2,1)S(1)} %reshape.213.query, bf16[32,256]{1,0:T(8,128)(2,1)S(1)} %pad_maximum_fusion.4.entry), custom_call_target="tpu_custom_call" | custom-call | tf_op jit(solution)/shard_map/finish/pallas_call | solution.py:287
  82.0 3.4 %collective-permute-start.6 = (bf16[32,1024]{1,0:T(8,128)(2,1)S(1)}, bf16[32,1024]{1,0:T(8,128)(2,1)S(1)}, u32[]{:S(2)}, u32[]{:S(2)}) collective-permute-start(bf16[32,1024]{1,0:T(8,128)(2,1)S(1)} %finish.1), channel_id=1, source_target_pairs={{0,16},{16,0},{32,48},{48,32},{64,80},{80,64},{96,112},{112,96},{1... | collective-permute-start | bytes 196616 | tf_op jit(solution)/shard_map/ppermute | solution.py:405
  85.4 0.9 collective-permute-done.6
  86.3 0.9 collective-permute-start.9
  87.3 1.2 %collective-permute-start.8 = (bf16[2,32,1024]{2,1,0:T(8,128)(2,1)S(1)}, bf16[2,32,1024]{2,1,0:T(8,128)(2,1)S(1)}, u32[]{:S(2)}, u32[]{:S(2)}) collective-permute-start(bf16[2,32,1024]{2,1,0:T(8,128)(2,1)S(1)} %pad_maximum_fusion.2.refs_0_), channel_id=1, source_target_pairs={{0,64},{16,80},{32,96},{48,112},{64,0},{80,16},{96,32},{112,48},{1... | collective-permute-start | bytes 393224 | tf_op jit(solution)/shard_map/ppermute | solution.py:408
  88.5 2.6 %collective-permute-done.9.refs_3_ = bf16[2,32,1024]{2,1,0:T(8,128)(2,1)S(1)} collective-permute-done((bf16[2,32,1024]{2,1,0:T(8,128)(2,1)S(1)}, bf16[2,32,1024]{2,1,0:T(8,128)(2,1)S(1)}, u32[]{:S(2)}, u32[]{:S(2)}) %collective-permute-start.9) | collective-permute-done | bytes 131104 | tf_op jit(solution)/shard_map/ppermute | solution.py:408
  91.1 2.1 %collective-permute-done.8.refs_2_ = bf16[2,32,1024]{2,1,0:T(8,128)(2,1)S(1)} collective-permute-done((bf16[2,32,1024]{2,1,0:T(8,128)(2,1)S(1)}, bf16[2,32,1024]{2,1,0:T(8,128)(2,1)S(1)}, u32[]{:S(2)}, u32[]{:S(2)}) %collective-permute-start.8) | collective-permute-done | bytes 131104 | tf_op jit(solution)/shard_map/ppermute | solution.py:408
  93.2 3.6 %collective-permute-done.7.refs_1_ = bf16[2,32,1024]{2,1,0:T(8,128)(2,1)S(1)} collective-permute-done((bf16[2,32,1024]{2,1,0:T(8,128)(2,1)S(1)}, bf16[2,32,1024]{2,1,0:T(8,128)(2,1)S(1)}, u32[]{:S(2)}, u32[]{:S(2)}) %collective-permute-start.7) | collective-permute-done | bytes 131104 | tf_op jit(solution)/shard_map/ppermute | solution.py:408
  96.8 0.8 place_heads.1
  (41 shorter events, 2.4 us)
Async XLA Ops:
  0.0 10.5 %copy-start = (bf16[32,8192]{1,0:T(8,128)(2,1)S(1)}, bf16[32,8192]{1,0:T(8,128)(2,1)}, u32[]{:S(2)}) copy-start(bf16[32,8192]{1,0:T(8,128)(2,1)} %param.6) | copy-start | bytes 1572868
  4.3 6.0 %copy-start.1 = (s32[32,64]{1,0:T(8,128)S(1)}, s32[32,64]{1,0:T(8,128)}, u32[]{:S(2)}) copy-start(s32[32,64]{1,0:T(8,128)} %param.8) | copy-start | bytes 24580
  4.4 6.0 %copy-start.2 = (s32[32]{0:T(128)S(1)}, s32[32]{0:T(128)}, u32[]{:S(2)}) copy-start(s32[32]{0:T(128)} %param.9) | copy-start | bytes 388
  4.4 44.8 %all-to-all-start = ((bf16[8,784,256]{2,1,0:T(8,128)(2,1)}), bf16[8,784,256]{2,1,0:T(8,128)(2,1)}, u32[]{:S(2)}, u32[]{:S(2)}) async-start(bf16[8,784,256]{2,1,0:T(8,128)(2,1)} %pack.1), calls=%async_computation | async-start | bytes 6422528 | tf_op jit(solution)/shard_map/all_to_all | solution.py:359
  10.6 7.0 %collective-permute-start.2 = (bf16[32,1152]{1,0:T(8,128)(2,1)S(1)}, bf16[32,1152]{1,0:T(8,128)(2,1)S(1)}, u32[]{:S(2)}, u32[]{:S(2)}) collective-permute-start(bf16[32,1152]{1,0:T(8,128)(2,1)S(1)} %pad_maximum_fusion.3), channel_id=1, source_target_pairs={{0,3},{1,0},{2,1},{3,2},{4,7},{5,4},{6,5},{7,6},{8,11},{9,8},{10,9... | collective-permute-start | bytes 221192 | tf_op jit(solution)/shard_map/ppermute | solution.py:376
  14.4 5.2 %collective-permute-start.1 = (bf16[32,1152]{1,0:T(8,128)(2,1)S(1)}, bf16[32,1152]{1,0:T(8,128)(2,1)S(1)}, u32[]{:S(2)}, u32[]{:S(2)}) collective-permute-start(bf16[32,1152]{1,0:T(8,128)(2,1)S(1)} %pad_maximum_fusion.3), channel_id=1, source_target_pairs={{0,2},{1,3},{2,0},{3,1},{4,6},{5,7},{6,4},{7,5},{8,10},{9,11},{10,... | collective-permute-start | bytes 221192 | tf_op jit(solution)/shard_map/ppermute | solution.py:376
  14.4 6.8 %collective-permute-start = (bf16[32,1152]{1,0:T(8,128)(2,1)S(1)}, bf16[32,1152]{1,0:T(8,128)(2,1)S(1)}, u32[]{:S(2)}, u32[]{:S(2)}) collective-permute-start(bf16[32,1152]{1,0:T(8,128)(2,1)S(1)} %pad_maximum_fusion.3), channel_id=1, source_target_pairs={{0,1},{1,2},{2,3},{3,0},{4,5},{5,6},{6,7},{7,4},{8,9},{9,10},{10,1... | collective-permute-start | bytes 221192 | tf_op jit(solution)/shard_map/ppermute | solution.py:376
  21.3 9.5 %collective-permute-start.4 = (bf16[4,32,1152]{2,1,0:T(8,128)(2,1)S(1)}, bf16[4,32,1152]{2,1,0:T(8,128)(2,1)S(1)}, u32[]{:S(2)}, u32[]{:S(2)}) collective-permute-start(bf16[4,32,1152]{2,1,0:T(8,128)(2,1)S(1)} %get-tuple-element.8), channel_id=1, source_target_pairs={{0,8},{1,9},{2,10},{3,11},{4,12},{5,13},{6,14},{7,15},{8,0},{9,1},... | collective-permute-start | bytes 884744 | tf_op jit(solution)/shard_map/ppermute | solution.py:376
  24.1 14.1 %collective-permute-start.3 = (bf16[4,32,1152]{2,1,0:T(8,128)(2,1)S(1)}, bf16[4,32,1152]{2,1,0:T(8,128)(2,1)S(1)}, u32[]{:S(2)}, u32[]{:S(2)}) collective-permute-start(bf16[4,32,1152]{2,1,0:T(8,128)(2,1)S(1)} %get-tuple-element.8), channel_id=1, source_target_pairs={{0,4},{1,5},{2,6},{3,7},{4,8},{5,9},{6,10},{7,11},{8,12},{9,13},{1... | collective-permute-start | bytes 884744 | tf_op jit(solution)/shard_map/ppermute | solution.py:376
  24.4 13.8 %collective-permute-start.5 = (bf16[4,32,1152]{2,1,0:T(8,128)(2,1)S(1)}, bf16[4,32,1152]{2,1,0:T(8,128)(2,1)S(1)}, u32[]{:S(2)}, u32[]{:S(2)}) collective-permute-start(bf16[4,32,1152]{2,1,0:T(8,128)(2,1)S(1)} %get-tuple-element.8), channel_id=1, source_target_pairs={{0,12},{1,13},{2,14},{3,15},{4,0},{5,1},{6,2},{7,3},{8,4},{9,5},{1... | collective-permute-start | bytes 884744 | tf_op jit(solution)/shard_map/ppermute | solution.py:376
  57.4 23.2 %all-to-all-start.1 = ((bf16[16,272,128]{2,1,0:T(8,128)(2,1)}), bf16[16,272,128]{2,1,0:T(8,128)(2,1)S(1)}, u32[]{:S(2)}, u32[]{:S(2)}) async-start(bf16[16,272,128]{2,1,0:T(8,128)(2,1)} %attend.1), calls=%async_computation.1 | async-start | bytes 2228224 | tf_op jit(solution)/shard_map/all_to_all | solution.py:396
  82.0 4.3 %collective-permute-start.6 = (bf16[32,1024]{1,0:T(8,128)(2,1)S(1)}, bf16[32,1024]{1,0:T(8,128)(2,1)S(1)}, u32[]{:S(2)}, u32[]{:S(2)}) collective-permute-start(bf16[32,1024]{1,0:T(8,128)(2,1)S(1)} %finish.1), channel_id=1, source_target_pairs={{0,16},{16,0},{32,48},{48,32},{64,80},{80,64},{96,112},{112,96},{1... | collective-permute-start | bytes 196616 | tf_op jit(solution)/shard_map/ppermute | solution.py:405
  86.3 4.8 %collective-permute-start.9 = (bf16[2,32,1024]{2,1,0:T(8,128)(2,1)S(1)}, bf16[2,32,1024]{2,1,0:T(8,128)(2,1)S(1)}, u32[]{:S(2)}, u32[]{:S(2)}) collective-permute-start(bf16[2,32,1024]{2,1,0:T(8,128)(2,1)S(1)} %pad_maximum_fusion.2.refs_0_), channel_id=1, source_target_pairs={{0,96},{16,112},{32,0},{48,16},{64,32},{80,48},{96,64},{112,80},{1... | collective-permute-start | bytes 393224 | tf_op jit(solution)/shard_map/ppermute | solution.py:408
  87.3 5.9 %collective-permute-start.8 = (bf16[2,32,1024]{2,1,0:T(8,128)(2,1)S(1)}, bf16[2,32,1024]{2,1,0:T(8,128)(2,1)S(1)}, u32[]{:S(2)}, u32[]{:S(2)}) collective-permute-start(bf16[2,32,1024]{2,1,0:T(8,128)(2,1)S(1)} %pad_maximum_fusion.2.refs_0_), channel_id=1, source_target_pairs={{0,64},{16,80},{32,96},{48,112},{64,0},{80,16},{96,32},{112,48},{1... | collective-permute-start | bytes 393224 | tf_op jit(solution)/shard_map/ppermute | solution.py:408
  88.5 8.3 %collective-permute-start.7 = (bf16[2,32,1024]{2,1,0:T(8,128)(2,1)S(1)}, bf16[2,32,1024]{2,1,0:T(8,128)(2,1)S(1)}, u32[]{:S(2)}, u32[]{:S(2)}) collective-permute-start(bf16[2,32,1024]{2,1,0:T(8,128)(2,1)S(1)} %pad_maximum_fusion.2.refs_0_), channel_id=1, source_target_pairs={{0,32},{16,48},{32,64},{48,80},{64,96},{80,112},{96,0},{112,16},{1... | collective-permute-start | bytes 393224 | tf_op jit(solution)/shard_map/ppermute | solution.py:408

commit v3 on v2

v3 whole, which is shorter than its diff:
```python
import functools
import math

import jax
import jax.numpy as jnp
from jax import lax
from jax.experimental import pallas as pl
from jax.experimental.pallas import tpu as pltpu
from jax.sharding import PartitionSpec as P

HEADS = 64
KV_HEADS = 8
HEAD_DIM = 128
BLK_TOKENS = 16
ROOT_BLOCKS = 40
LIST = 64
WIDTH = KV_HEADS * HEAD_DIM
GROUP = HEADS // KV_HEADS
SCALE = 1.0 / math.sqrt(HEAD_DIM)
SCALE2 = SCALE * math.log2(math.e)

HOLDERS = 8
OWN_BLOCKS = 48
BLOCKS = HOLDERS * OWN_BLOCKS
PIECE_ROWS = OWN_BLOCKS * BLK_TOKENS
MARK = 2.0**120
TILE = 64
CHUNK = 40
SIZES = (24, 32, 40)
ROWS = TILE * GROUP
PACK_PARTS = 4
TOGETHER = 4
TOKENS = CHUNK * BLK_TOKENS
OUT_ROWS = 32 * GROUP + 16
LOW = -1e9
DEAD = -1e30


def pack_kernel(fill, pool, out, staged, ready, arrived, left):
    span = PIECE_ROWS // PACK_PARTS

    def fetch(part):
        place = pl.ds(part * span, span)
        return pltpu.make_async_copy(pool.at[place, :], staged.at[part], arrived.at[part])

    def send(part, head):
        return pltpu.make_async_copy(
            ready.at[part, head],
            out.at[head, pl.ds(part * span, span), :],
            left.at[part * KV_HEADS + head],
        )

    for part in range(PACK_PARTS):
        fetch(part).start()
    token = lax.broadcasted_iota(jnp.int32, (BLK_TOKENS, HEAD_DIM), 0)
    blocks = span // BLK_TOKENS
    for part in range(PACK_PARTS):
        fetch(part).wait()
        live = [token < fill[part * blocks + block] for block in range(blocks)]
        for head in range(KV_HEADS):
            lanes = slice(head * HEAD_DIM, (head + 1) * HEAD_DIM)
            for block in range(blocks):
                place = slice(block * BLK_TOKENS, (block + 1) * BLK_TOKENS)
                key = staged[part, place, lanes].astype(jnp.float32)
                ready[part, head, place, 0:HEAD_DIM] = jnp.where(live[block], key, MARK).astype(
                    jnp.bfloat16
                )
            lanes = slice(WIDTH + head * HEAD_DIM, WIDTH + (head + 1) * HEAD_DIM)
            ready[part, head, :, HEAD_DIM:] = staged[part, :, lanes]
            send(part, head).start()
    for part in range(PACK_PARTS):
        for head in range(KV_HEADS):
            send(part, head).wait()


def pack(block_fill, cache_pool):
    span = PIECE_ROWS // PACK_PARTS
    hbm = pl.BlockSpec(memory_space=pltpu.HBM)
    return pl.pallas_call(
        pack_kernel,
        out_shape=jax.ShapeDtypeStruct((KV_HEADS, PIECE_ROWS, 2 * HEAD_DIM), jnp.bfloat16),
        in_specs=[pl.BlockSpec(memory_space=pltpu.SMEM), hbm],
        out_specs=hbm,
        scratch_shapes=[
            pltpu.VMEM((PACK_PARTS, span, 2 * WIDTH), jnp.bfloat16),
            pltpu.VMEM((PACK_PARTS, KV_HEADS, span, 2 * HEAD_DIM), jnp.bfloat16),
            pltpu.SemaphoreType.DMA((PACK_PARTS,)),
            pltpu.SemaphoreType.DMA((PACK_PARTS * KV_HEADS,)),
        ],
        compiler_params=pltpu.CompilerParams(vmem_limit_bytes=60 * 1024 * 1024),
        name="pack",
    )(block_fill, cache_pool.reshape(PIECE_ROWS, 2 * WIDTH))


def attend_kernel(codes, counts, group, kv, query, barred, out, keys, values, peaks, sums):
    values[:, :, HEAD_DIM:] = jnp.ones((TOGETHER, TOKENS, HEAD_DIM), jnp.bfloat16)
    row_rollout = lax.broadcasted_iota(jnp.int32, (ROWS, HEAD_DIM), 0) // GROUP
    lane = lax.broadcasted_iota(jnp.int32, (ROWS, HEAD_DIM), 1)
    member_lanes = jnp.where(row_rollout == lane, 1.0, 0.0).astype(jnp.bfloat16)
    pick = lax.broadcasted_iota(jnp.int32, (8, HEAD_DIM), 0)
    pick_lane = lax.broadcasted_iota(jnp.int32, (8, HEAD_DIM), 1)
    picked = jnp.where(pick == pick_lane, 1.0, 0.0).astype(jnp.bfloat16)

    def chunk_scores(tile, chunk, lane_of, size=CHUNK):
        rows = query[pl.ds(pl.multiple_of(tile * ROWS, ROWS), ROWS), :]
        left = jnp.concatenate([rows, member_lanes], axis=1)
        for slot in range(size):
            number = chunk * CHUNK + slot
            code = codes[tile * BLOCKS + number]
            row = pl.multiple_of(code * BLK_TOKENS, BLK_TOKENS)
            place = pl.ds(slot * BLK_TOKENS, BLK_TOKENS)
            key = kv[pl.ds(row, BLK_TOKENS), 0:HEAD_DIM].astype(jnp.float32)
            live = (key < MARK) & (number < counts[tile])
            keys[lane_of, place, 0:HEAD_DIM] = jnp.where(live, key, 0.0).astype(jnp.bfloat16)
            keys[lane_of, place, HEAD_DIM:] = jnp.where(
                live, barred[pl.ds(tile * BLOCKS + code, 1), :], DEAD
            ).astype(jnp.bfloat16)
            values[lane_of, place, 0:HEAD_DIM] = kv[pl.ds(row, BLK_TOKENS), HEAD_DIM:]
        return lax.dot_general(
            left,
            keys[lane_of, 0 : size * BLK_TOKENS],
            (((1,), (1,)), ((), ())),
            preferred_element_type=jnp.float32,
        )

    def highest(found, low):
        peak = jnp.maximum(jnp.max(found, axis=1, keepdims=True) * SCALE2, low)
        return peak.astype(jnp.bfloat16).astype(jnp.float32)

    def summed(found, peak, lane_of):
        weights = jnp.exp2(found * SCALE2 - peak).astype(jnp.bfloat16)
        return jnp.dot(
            weights, values[lane_of, 0 : found.shape[1]], preferred_element_type=jnp.float32
        )

    def put_out(tile, peak, sums):
        total = sums[:, HEAD_DIM:]
        coarse = total.astype(jnp.bfloat16).astype(jnp.float32)
        stats = jnp.where(lane == 0, peak, jnp.where(lane == 1, coarse, total - coarse))
        flat = lax.dot_general(
            picked,
            stats.astype(jnp.bfloat16),
            (((1,), (1,)), ((), ())),
            preferred_element_type=jnp.float32,
        )
        for part in range(TILE // 32):
            count = 32 * GROUP
            owner = tile * (TILE // 32) + part
            owner = (((group[0] >> 2) - (owner >> 2)) & 3) * 4 + ((group[0] - owner) & 3)
            out[owner, 0:count, :] = sums[
                part * count : (part + 1) * count, 0:HEAD_DIM
            ].astype(jnp.bfloat16)
            both = jnp.concatenate(
                [
                    flat[:, part * count : part * count + HEAD_DIM],
                    flat[:, part * count + HEAD_DIM : (part + 1) * count],
                ],
                axis=0,
            )
            out[owner, count:, :] = both.astype(jnp.bfloat16)

    def long_tile(tile):
        chunks = (counts[tile] + CHUNK - 1) // CHUNK
        found = chunk_scores(tile, 0, 0)
        peak = highest(found, LOW)
        peaks[...] = jnp.broadcast_to(peak, (ROWS, HEAD_DIM))
        sums[...] = summed(found, peak, 0)

        def more(chunk, _):
            found = chunk_scores(tile, chunk, 0)
            old = peaks[:, 0:1]
            peak = highest(found, old)
            sums[...] = sums[...] * jnp.exp2(old - peak) + summed(found, peak, 0)
            peaks[...] = jnp.broadcast_to(peak, (ROWS, HEAD_DIM))
            return 0

        lax.fori_loop(1, chunks, more, 0)
        put_out(tile, peaks[...], sums[...])

    def some_tiles(step, _):
        tiles = [step * TOGETHER + k for k in range(TOGETHER)]
        most = counts[tiles[0]]
        for tile in tiles[1:]:
            most = jnp.maximum(most, counts[tile])

        for fewer, size in zip((-1,) + SIZES, SIZES):

            @pl.when((most > fewer) & (most <= size))
            def _():
                found = [chunk_scores(tile, 0, k, size) for k, tile in enumerate(tiles)]
                peak = [highest(one, LOW) for one in found]
                added = [summed(found[k], peak[k], k) for k in range(TOGETHER)]
                for k, tile in enumerate(tiles):
                    put_out(tile, peak[k], added[k])

        @pl.when(most > CHUNK)
        def _():
            lax.fori_loop(0, TOGETHER, lambda k, _: long_tile(tiles[0] + k) or 0, 0)

        return 0

    lax.fori_loop(0, counts.shape[0] // TOGETHER, some_tiles, 0)


def attend(codes, counts, group, kv, query, barred):
    vmem = pl.BlockSpec(memory_space=pltpu.VMEM)
    smem = pl.BlockSpec(memory_space=pltpu.SMEM)
    sources = query.shape[0] // (32 * GROUP)
    return pl.pallas_call(
        attend_kernel,
        out_shape=jax.ShapeDtypeStruct((sources, OUT_ROWS, HEAD_DIM), jnp.bfloat16),
        in_specs=[smem, smem, smem, vmem, vmem, vmem],
        out_specs=vmem,
        scratch_shapes=[
            pltpu.VMEM((TOGETHER, TOKENS, 2 * HEAD_DIM), jnp.bfloat16),
            pltpu.VMEM((TOGETHER, TOKENS, 2 * HEAD_DIM), jnp.bfloat16),
            pltpu.VMEM((ROWS, HEAD_DIM), jnp.float32),
            pltpu.VMEM((ROWS, 2 * HEAD_DIM), jnp.float32),
        ],
        compiler_params=pltpu.CompilerParams(vmem_limit_bytes=26 * 1024 * 1024),
        cost_estimate=pl.CostEstimate(
            flops=4 * 4096 * 512 * 256, bytes_accessed=6 << 20, transcendentals=4096 * 512
        ),
        name="attend",
    )(codes, counts, group, kv, query, barred)


def finish_kernel(parts, query, entry, out, peaks, totals, ended):
    sources = parts.shape[0]
    count = parts.shape[1] - 16
    which = lax.broadcasted_iota(jnp.int32, (8, 2 * HEAD_DIM), 0)
    lane = lax.broadcasted_iota(jnp.int32, (8, 2 * HEAD_DIM), 1)
    spread = jnp.where(
        lane < HEAD_DIM, jnp.where(which == 0, 1.0, 0.0), jnp.where((which == 1) | (which == 2), 1.0, 0.0)
    ).astype(jnp.bfloat16)
    rollouts = count // GROUP
    own_key = jnp.broadcast_to(
        entry[:, 0:HEAD_DIM].astype(jnp.float32)[:, None, :], (rollouts, GROUP, HEAD_DIM)
    ).reshape(count, HEAD_DIM)
    own_value = jnp.broadcast_to(
        entry[:, HEAD_DIM:].astype(jnp.float32)[:, None, :], (rollouts, GROUP, HEAD_DIM)
    ).reshape(count, HEAD_DIM)
    own = jnp.sum(query[...].astype(jnp.float32) * own_key, axis=1, keepdims=True) * SCALE2
    highest = jnp.broadcast_to(own, (count, HEAD_DIM))
    for source in range(sources):
        flat = parts[source, count:, :].astype(jnp.float32)
        for half in range(count // HEAD_DIM):
            wide = lax.dot_general(
                flat[half * 8 : half * 8 + 8, :].astype(jnp.bfloat16),
                spread,
                (((0,), (0,)), ((), ())),
                preferred_element_type=jnp.float32,
            )
            place = pl.ds(half * HEAD_DIM, HEAD_DIM)
            peaks[source, place, :] = wide[:, :HEAD_DIM]
            totals[source, place, :] = wide[:, HEAD_DIM:]
        highest = jnp.maximum(highest, peaks[source])
    weight = jnp.exp2(own - highest)
    total = weight
    accum = weight * own_value
    for source in range(sources):
        weight = jnp.exp2(peaks[source] - highest)
        total = total + weight * totals[source]
        accum = accum + weight * parts[source, 0:count, :].astype(jnp.float32)
    ended[...] = accum / total
    for head in range(GROUP):
        out[:, head * HEAD_DIM : (head + 1) * HEAD_DIM] = ended[
            pl.ds(head, rollouts, stride=GROUP), :
        ].astype(jnp.bfloat16)


def finish(parts, query, entry):
    count = query.shape[0]
    vmem = pl.BlockSpec(memory_space=pltpu.VMEM)
    return pl.pallas_call(
        finish_kernel,
        out_shape=jax.ShapeDtypeStruct((count // GROUP, WIDTH), jnp.bfloat16),
        in_specs=[vmem, vmem, vmem],
        out_specs=vmem,
        scratch_shapes=[
            pltpu.VMEM((parts.shape[0], count, HEAD_DIM), jnp.float32),
            pltpu.VMEM((parts.shape[0], count, HEAD_DIM), jnp.float32),
            pltpu.VMEM((count, HEAD_DIM), jnp.float32),
        ],
        compiler_params=pltpu.CompilerParams(vmem_limit_bytes=50 * 1024 * 1024),
        name="finish",
    )(parts, query, entry)


def place_kernel(node, *refs):
    heads, out = refs[:-1], refs[-1]
    chips = len(heads) // 2
    for which in range(2):
        core = lax.rem(node[0] + which, 2)
        for hop, ref in zip((0, 1, 3, 2), heads[which * chips : (which + 1) * chips]):
            chip = lax.rem(node[0] // 2 - hop + chips, chips)
            start = pl.multiple_of((chip * 2 + core) * WIDTH, WIDTH)
            out[:, pl.ds(start, WIDTH)] = ref[...]


def place_heads(node, mine, other):
    vmem = pl.BlockSpec(memory_space=pltpu.VMEM)
    rollouts = mine[0].shape[0]
    return pl.pallas_call(
        place_kernel,
        out_shape=jax.ShapeDtypeStruct((rollouts, HEADS * HEAD_DIM), jnp.bfloat16),
        in_specs=[pl.BlockSpec(memory_space=pltpu.SMEM)] + [vmem] * (2 * len(mine)),
        out_specs=vmem,
        compiler_params=pltpu.CompilerParams(vmem_limit_bytes=16 * 1024 * 1024),
        name="place_heads",
    )(node.reshape(1).astype(jnp.int32), *mine, *other)


def local_number(ids, column):
    device = ids // OWN_BLOCKS
    here = (device % 16) == column
    return jnp.where(here, (device // 16) * OWN_BLOCKS + ids % OWN_BLOCKS, -1)


def visits(root, lists):
    tiles, _, rollouts = lists.shape
    numbers = jnp.arange(BLOCKS, dtype=jnp.int32)
    everyone = jnp.any(root[:, None] == numbers, axis=0)
    member = jnp.any(lists[:, :, None, :] == numbers[None, None, :, None], axis=1)
    member = member | everyone[None, :, None]
    hit = jnp.any(member, axis=2)
    counts = jnp.sum(hit, axis=1, dtype=jnp.int32)
    before = (numbers[:, None] < numbers[None, :]).astype(jnp.bfloat16)
    place = jnp.dot(hit.astype(jnp.bfloat16), before, preferred_element_type=jnp.float32)
    place = jnp.where(hit, place.astype(jnp.int32), -1)
    codes = jnp.sum(jnp.where(place[:, None, :] == numbers[None, :, None], numbers, 0), axis=2)
    barred = jnp.pad(jnp.where(member, 0.0, DEAD), ((0, 0), (0, 0), (0, HEAD_DIM - rollouts)))
    return (
        codes.astype(jnp.int32).reshape(tiles * BLOCKS),
        counts,
        barred.reshape(tiles * BLOCKS, HEAD_DIM),
    )


def per_device(queries, new_entry, block_lists, list_lengths, block_fill, cache_pool):
    node = lax.axis_index("node")
    column = lax.axis_index("group")
    groups = lax.axis_size("group")
    own_rows = queries.shape[0]

    sent = pack(block_fill, cache_pool)
    kv = lax.all_to_all(sent, "node", split_axis=0, concat_axis=0, tiled=True)
    kv = kv.reshape(HOLDERS * PIECE_ROWS, 2 * HEAD_DIM)

    head_query = lax.dynamic_slice_in_dim(queries, node * WIDTH, WIDTH, axis=1)
    entries = jnp.arange(LIST, dtype=jnp.int32)[None, :]
    tail = jnp.where(entries < list_lengths[:, None], block_lists, 8191)[:, ROOT_BLOCKS:]
    coded = jnp.concatenate([tail // 128, tail % 128], axis=1).astype(jnp.bfloat16)
    coded = jnp.pad(coded, ((0, 0), (0, HEAD_DIM - coded.shape[1])))
    told = jnp.concatenate([head_query, coded], axis=1)
    sent, told = lax.optimization_barrier((sent, told))
    side = 4
    def shifted(value, hop_x, hop_z):
        pairs = [
            (x * side + z, (x + hop_x) % side * side + (z + hop_z) % side)
            for x in range(side)
            for z in range(side)
        ]
        return lax.ppermute(value, "group", pairs)

    line = jnp.stack([told] + [shifted(told, 0, hop) for hop in range(1, side)])
    told = jnp.stack([line] + [shifted(line, hop, 0) for hop in range(1, side)])
    told = told.reshape((groups,) + told.shape[2:])
    all_query = told[:, :, :WIDTH].reshape(groups * own_rows * GROUP, HEAD_DIM)
    coded = told[:, :, WIDTH:].astype(jnp.int32).reshape(groups * own_rows, HEAD_DIM)
    count = LIST - ROOT_BLOCKS
    ids = coded[:, :count] * 128 + coded[:, count : 2 * count]
    tail = jnp.where(ids < 8191, local_number(ids, column), -1)
    root = local_number(block_lists[0, :ROOT_BLOCKS], column)
    tiles = groups * own_rows // TILE
    codes, counts, barred = visits(
        root, jnp.transpose(tail.reshape(tiles, TILE, count), (0, 2, 1))
    )
    group = column.reshape(1).astype(jnp.int32)
    partial = attend(codes, counts, group, kv, all_query, barred)
    parts = lax.all_to_all(partial, "group", split_axis=0, concat_axis=0, tiled=True)
    key = lax.dynamic_slice_in_dim(new_entry, node * HEAD_DIM, HEAD_DIM, axis=1)
    value = lax.dynamic_slice_in_dim(new_entry, WIDTH + node * HEAD_DIM, HEAD_DIM, axis=1)
    done = finish(
        parts,
        head_query.reshape(own_rows * GROUP, HEAD_DIM),
        jnp.concatenate([key, value], axis=1),
    )
    nodes = lax.axis_size("node")

    def from_node(value, to):
        return lax.ppermute(value, "node", [(i, to(i)) for i in range(nodes)])

    def along(hop):
        return lambda i: (i + 2 * hop) % nodes

    mine = [done] + [from_node(done, along(hop)) for hop in (1, 3, 2)]
    other = [from_node(value, lambda i: i ^ 1) for value in mine]
    return place_heads(node, mine, other)


def solution(mesh):
    return jax.shard_map(
        per_device,
        mesh=mesh,
        in_specs=(
            P("group", None),
            P("group", None),
            P("group", None),
            P("group"),
            P(("node", "group")),
            P(("node", "group"), None, None),
        ),
        out_specs=P("group", None),
        check_vma=False,
    )
```

time: 98.1 us -> 94 us (0.958)
  waiting for transfers between devices: 41.8 us -> 34.5 us
  starting transfers between devices: 28.7 us -> 35.5 us
  local copies, waits for them, and re-layouts: 6.35 us -> 4.68 us
  Pallas kernels: 14.8 us -> 13.4 us
    ppermute x4 -> x7, waiting for transfers between devices: 9.24 us -> 0.91 us  [from_node(): return lax.ppermute(value, 'node', [(i, to(i)) for i in range(nodes)])]
    ppermute x4 -> x7, starting transfers between devices: 5.52 us -> 12.1 us  [from_node(): return lax.ppermute(value, 'node', [(i, to(i)) for i in range(nodes)])]
    gather x3 -> x0, local copies, waits for them, and re-layouts: 1.57 us -> none  [the longest x2 0.84 us: per_device(): told = jnp.take(told, (column_z - order) % side, axis=1)]
    pallas_call x1, Pallas kernels: 8.28 us -> 7.22 us  [attend(): pl.pallas_call(attend_kernel, out_shape=jax.ShapeDtypeStruct((sources, OU...]
  transfers between devices with their start and end apart: 12 -> 15, of which waited for: 10 -> 8; matrix products, arithmetic and copies ran while one was open for 12% -> 11% of each run, Pallas kernels for 0% -> 0%
where the time goes in v3:
time: 94 us; the launch traced here: 93.6 us
  starting transfers between devices  35.5 us (38%)
  waiting for transfers between devices  34.5 us (37%)
  Pallas kernels  13.4 us (14%)
  other arithmetic  5.17 us (6%)
  local copies, waits for them, and re-layouts  4.68 us (5%)
    ppermute x6, waiting for transfers between devices, shifted(): return lax.ppermute(value, 'group', pairs)  17.5 us
    all_to_all x1, waiting for transfers between devices, per_device(): lax.all_to_all(partial, 'group', split_axis=0, concat_axis=0, tiled=True)  15.3 us
    ppermute x7, starting transfers between devices, from_node(): return lax.ppermute(value, 'node', [(i, to(i)) for i in range(nodes)])  12.1 us
    ppermute x6, starting transfers between devices, shifted(): return lax.ppermute(value, 'group', pairs)  10 us
    all_to_all x1, starting transfers between devices, per_device(): lax.all_to_all(partial, 'group', split_axis=0, concat_axis=0, tiled=True)  7.44 us
    pallas_call x1, Pallas kernels, attend(): pl.pallas_call(attend_kernel, out_shape=jax.ShapeDtypeStruct((sources, OU...  7.22 us
    all_to_all x1, starting transfers between devices, per_device(): kv = lax.all_to_all(sent, 'node', split_axis=0, concat_axis=0, tiled=True)  5.98 us
    pallas_call x1, Pallas kernels, pack(): pl.pallas_call(pack_kernel, out_shape=jax.ShapeDtypeStruct((KV_HEADS, PIE...  4.03 us
  transfers between devices with their start and end apart: 15, of which 8 were waited for; matrix products, arithmetic and copies ran while one was open for 11% of the time, Pallas kernels for 0%

profile of v3, /device:TPU:1, one launch (start us, length us, event | category | flops | bytes accessed | tf_op | source)
XLA Modules:
  0.0 93.6 jit_solution(18295649578676590498)
XLA Ops:
  0.0 4.0 %pack.1 = bf16[8,768,256]{2,1,0:T(8,128)(2,1)} custom-call(s32[48]{0:T(128)} %fill.1, bf16[768,2048]{1,0:T(8,128)(2,1)} %bitcast.41), custom_call_target="tpu_custom_call" | custom-call | tf_op jit(solution)/shard_map/pack/pallas_call | solution.py:79
  4.1 6.0 %all-to-all-start = ((bf16[8,768,256]{2,1,0:T(8,128)(2,1)}), bf16[8,768,256]{2,1,0:T(8,128)(2,1)}, u32[]{:S(2)}, u32[]{:S(2)}) async-start(bf16[8,768,256]{2,1,0:T(8,128)(2,1)} %pack.1), calls=%async_computation | async-start | bytes 6291456 | tf_op jit(solution)/shard_map/all_to_all | solution.py:347
  10.3 3.8 %collective-permute-start.2 = (bf16[32,1152]{1,0:T(8,128)(2,1)S(1)}, bf16[32,1152]{1,0:T(8,128)(2,1)S(1)}, u32[]{:S(2)}, u32[]{:S(2)}) collective-permute-start(bf16[32,1152]{1,0:T(8,128)(2,1)S(1)} %pad_maximum_fusion.2), channel_id=1, source_target_pairs={{0,3},{1,0},{2,1},{3,2},{4,7},{5,4},{6,5},{7,6},{8,11},{9,8},{10,9... | collective-permute-start | bytes 221192 | tf_op jit(solution)/shard_map/ppermute | solution.py:364
  14.1 0.7 collective-permute-start
  14.8 2.4 %collective-permute-done.2 = bf16[32,1152]{1,0:T(8,128)(2,1)S(1)} collective-permute-done((bf16[32,1152]{1,0:T(8,128)(2,1)S(1)}, bf16[32,1152]{1,0:T(8,128)(2,1)S(1)}, u32[]{:S(2)}, u32[]{:S(2)}) %collective-permute-start.2) | collective-permute-done | bytes 73760 | tf_op jit(solution)/shard_map/ppermute | solution.py:364
  17.2 2.0 %collective-permute-done.1 = bf16[32,1152]{1,0:T(8,128)(2,1)S(1)} collective-permute-done((bf16[32,1152]{1,0:T(8,128)(2,1)S(1)}, bf16[32,1152]{1,0:T(8,128)(2,1)S(1)}, u32[]{:S(2)}, u32[]{:S(2)}) %collective-permute-start.1) | collective-permute-done | bytes 73760 | tf_op jit(solution)/shard_map/ppermute | solution.py:364
  19.3 1.7 %collective-permute-done = bf16[32,1152]{1,0:T(8,128)(2,1)S(1)} collective-permute-done((bf16[32,1152]{1,0:T(8,128)(2,1)S(1)}, bf16[32,1152]{1,0:T(8,128)(2,1)S(1)}, u32[]{:S(2)}, u32[]{:S(2)}) %collective-permute-start) | collective-permute-done | bytes 73760 | tf_op jit(solution)/shard_map/ppermute | solution.py:364
  21.0 2.8 %collective-permute-start.4 = (bf16[4,32,1152]{2,1,0:T(8,128)(2,1)S(1)}, bf16[4,32,1152]{2,1,0:T(8,128)(2,1)S(1)}, u32[]{:S(2)}, u32[]{:S(2)}) collective-permute-start(bf16[4,32,1152]{2,1,0:T(8,128)(2,1)S(1)} %get-tuple-element.8), channel_id=1, source_target_pairs={{0,8},{1,9},{2,10},{3,11},{4,12},{5,13},{6,14},{7,15},{8,0},{9,1},... | collective-permute-start | bytes 884744 | tf_op jit(solution)/shard_map/ppermute | solution.py:364
  23.8 0.3 collective-permute-start.3
  24.1 2.4 %collective-permute-start.5 = (bf16[4,32,1152]{2,1,0:T(8,128)(2,1)S(1)}, bf16[4,32,1152]{2,1,0:T(8,128)(2,1)S(1)}, u32[]{:S(2)}, u32[]{:S(2)}) collective-permute-start(bf16[4,32,1152]{2,1,0:T(8,128)(2,1)S(1)} %get-tuple-element.8), channel_id=1, source_target_pairs={{0,12},{1,13},{2,14},{3,15},{4,0},{5,1},{6,2},{7,3},{8,4},{9,5},{1... | collective-permute-start | bytes 884744 | tf_op jit(solution)/shard_map/ppermute | solution.py:364
  26.6 3.9 %collective-permute-done.4 = bf16[4,32,1152]{2,1,0:T(8,128)(2,1)S(1)} collective-permute-done((bf16[4,32,1152]{2,1,0:T(8,128)(2,1)S(1)}, bf16[4,32,1152]{2,1,0:T(8,128)(2,1)S(1)}, u32[]{:S(2)}, u32[]{:S(2)}) %collective-permute-start.4) | collective-permute-done | bytes 294944 | tf_op jit(solution)/shard_map/ppermute | solution.py:364
  30.5 7.4 %collective-permute-done.3 = bf16[4,32,1152]{2,1,0:T(8,128)(2,1)S(1)} collective-permute-done((bf16[4,32,1152]{2,1,0:T(8,128)(2,1)S(1)}, bf16[4,32,1152]{2,1,0:T(8,128)(2,1)S(1)}, u32[]{:S(2)}, u32[]{:S(2)}) %collective-permute-start.3) | collective-permute-done | bytes 294944 | tf_op jit(solution)/shard_map/ppermute | solution.py:364
  37.9 0.2 pad_maximum_fusion
  38.3 0.5 reshape.108.query
  38.8 0.6 fusion.6
  39.6 3.1 %fusion = pred[8,384,64]{1,2,0:T(8,128)(4,1)S(1)} fusion(s32[8,24,64]{2,1,0:T(8,128)S(1)} %copy.13), kind=kLoop, calls=%fused_computation.1 | loop fusion | flops 9240576 | bytes 245760 | tf_op jit(solution)/shard_map/reduce_or | solution.py:324
  42.9 0.6 select_reduce_fusion
  43.6 1.6 %copy.17 = f32[8,384,64]{2,1,0:T(8,128)} copy(f32[8,384,64]{1,2,0:T(8,128)S(1)} %or_select_fusion) | data formatting | bytes 1572864
  45.2 1.5 %pad.9.clone = f32[8,384,128]{2,1,0:T(8,128)S(1)} pad(f32[8,384,64]{2,1,0:T(8,128)} %copy.17, f32[]{:T(128)} %constant.118.clone.1), padding=0_0x0_0x0_64 | pad | bytes 2359300 | tf_op jit(solution)/shard_map/jit(_pad)/pad | solution.py:332
  46.8 0.9 all-to-all-done
  47.7 7.2 %attend.1 = bf16[16,272,128]{2,1,0:T(8,128)(2,1)} custom-call(s32[3072]{0:T(1024)S(1)} %reshape.105.codes, s32[8]{0:T(128)S(1)} %convert_reduce_fusion.counts, s32[1]{0:T(128)} %bitcast.19.group, bf16[6144,256]{1,0:T(8,128)(2,1)} %bitcast.20.kv, bf16[4096,128]{1,0:T(8,128)(2,1)S(1)} %reshape.108.query, f32[3072,128]{1,0:T(8,128)S(1)} %bitcast.38), custom_call_target="tpu_custom_call" | custom-call | flops 2147483648 | bytes 6291456 | tf_op jit(solution)/shard_map/attend/pallas_call | solution.py:209
  54.9 7.4 %all-to-all-start.1 = ((bf16[16,272,128]{2,1,0:T(8,128)(2,1)}), bf16[16,272,128]{2,1,0:T(8,128)(2,1)S(1)}, u32[]{:S(2)}, u32[]{:S(2)}) async-start(bf16[16,272,128]{2,1,0:T(8,128)(2,1)} %attend.1), calls=%async_computation.1 | async-start | bytes 2228224 | tf_op jit(solution)/shard_map/all_to_all | solution.py:381
  62.4 0.7 constant_dynamic-slice_fusion
  63.2 15.3 %all-to-all-done.1.parts = bf16[16,272,128]{2,1,0:T(8,128)(2,1)S(1)} async-done(((bf16[16,272,128]{2,1,0:T(8,128)(2,1)}), bf16[16,272,128]{2,1,0:T(8,128)(2,1)S(1)}, u32[]{:S(2)}, u32[]{:S(2)}) %all-to-all-start.1) | async-done | bytes 1114144 | tf_op jit(solution)/shard_map/all_to_all | solution.py:381
  78.4 1.3 %finish.1.refs_0_ = bf16[32,1024]{1,0:T(8,128)(2,1)S(1)} custom-call(bf16[16,272,128]{2,1,0:T(8,128)(2,1)S(1)} %all-to-all-done.1.parts, bf16[256,128]{1,0:T(8,128)(2,1)S(1)} %reshape.110.query, bf16[32,256]{1,0:T(8,128)(2,1)S(1)} %pad_maximum_fusion.3.entry), custom_call_target="tpu_custom_call" | custom-call | tf_op jit(solution)/shard_map/finish/pallas_call | solution.py:275
  79.7 0.6 collective-permute-start.8
  80.3 2.1 %collective-permute-start.7 = (bf16[32,1024]{1,0:T(8,128)(2,1)S(1)}, bf16[32,1024]{1,0:T(8,128)(2,1)S(1)}, u32[]{:S(2)}, u32[]{:S(2)}) collective-permute-start(bf16[32,1024]{1,0:T(8,128)(2,1)S(1)} %finish.1.refs_0_), channel_id=1, source_target_pairs={{0,96},{16,112},{32,0},{48,16},{64,32},{80,48},{96,64},{112,80},{1... | collective-permute-start | bytes 196616 | tf_op jit(solution)/shard_map/ppermute | solution.py:392
  82.5 3.9 %collective-permute-start.9 = (bf16[32,1024]{1,0:T(8,128)(2,1)S(1)}, bf16[32,1024]{1,0:T(8,128)(2,1)S(1)}, u32[]{:S(2)}, u32[]{:S(2)}) collective-permute-start(bf16[32,1024]{1,0:T(8,128)(2,1)S(1)} %finish.1.refs_0_), channel_id=1, source_target_pairs={{0,16},{16,0},{32,48},{48,32},{64,80},{80,64},{96,112},{112,96},{1... | collective-permute-start | bytes 196616 | tf_op jit(solution)/shard_map/ppermute | solution.py:392
  86.3 2.5 %collective-permute-start.12 = (bf16[32,1024]{1,0:T(8,128)(2,1)S(1)}, bf16[32,1024]{1,0:T(8,128)(2,1)S(1)}, u32[]{:S(2)}, u32[]{:S(2)}) collective-permute-start(bf16[32,1024]{1,0:T(8,128)(2,1)S(1)} %collective-permute-done.8.refs_3_), channel_id=1, source_target_pairs={{0,16},{16,0},{32,48},{48,32},{64,80},{80,64},{96,112},{112,96},{1... | collective-permute-start | bytes 196616 | tf_op jit(solution)/shard_map/ppermute | solution.py:392
  88.9 2.9 %collective-permute-start.10 = (bf16[32,1024]{1,0:T(8,128)(2,1)S(1)}, bf16[32,1024]{1,0:T(8,128)(2,1)S(1)}, u32[]{:S(2)}, u32[]{:S(2)}) collective-permute-start(bf16[32,1024]{1,0:T(8,128)(2,1)S(1)} %collective-permute-done.6.refs_1_), channel_id=1, source_target_pairs={{0,16},{16,0},{32,48},{48,32},{64,80},{80,64},{96,112},{112,96},{1... | collective-permute-start | bytes 196616 | tf_op jit(solution)/shard_map/ppermute | solution.py:392
  91.8 0.9 collective-permute-done.10.refs_5_
  92.7 0.8 place_heads.1
  (34 shorter events, 1.2 us)
Async XLA Ops:
  0.0 10.2 %copy-start = (bf16[32,8192]{1,0:T(8,128)(2,1)S(1)}, bf16[32,8192]{1,0:T(8,128)(2,1)}, u32[]{:S(2)}) copy-start(bf16[32,8192]{1,0:T(8,128)(2,1)} %param.6) | copy-start | bytes 1572868
  4.0 6.0 %copy-start.1 = (s32[32,64]{1,0:T(8,128)S(1)}, s32[32,64]{1,0:T(8,128)}, u32[]{:S(2)}) copy-start(s32[32,64]{1,0:T(8,128)} %param.8) | copy-start | bytes 24580
  4.1 6.0 %copy-start.2 = (s32[32]{0:T(128)S(1)}, s32[32]{0:T(128)}, u32[]{:S(2)}) copy-start(s32[32]{0:T(128)} %param.9) | copy-start | bytes 388
  4.1 43.7 %all-to-all-start = ((bf16[8,768,256]{2,1,0:T(8,128)(2,1)}), bf16[8,768,256]{2,1,0:T(8,128)(2,1)}, u32[]{:S(2)}, u32[]{:S(2)}) async-start(bf16[8,768,256]{2,1,0:T(8,128)(2,1)} %pack.1), calls=%async_computation | async-start | bytes 6291456 | tf_op jit(solution)/shard_map/all_to_all | solution.py:347
  10.3 7.0 %collective-permute-start.2 = (bf16[32,1152]{1,0:T(8,128)(2,1)S(1)}, bf16[32,1152]{1,0:T(8,128)(2,1)S(1)}, u32[]{:S(2)}, u32[]{:S(2)}) collective-permute-start(bf16[32,1152]{1,0:T(8,128)(2,1)S(1)} %pad_maximum_fusion.2), channel_id=1, source_target_pairs={{0,3},{1,0},{2,1},{3,2},{4,7},{5,4},{6,5},{7,6},{8,11},{9,8},{10,9... | collective-permute-start | bytes 221192 | tf_op jit(solution)/shard_map/ppermute | solution.py:364
  14.1 5.2 %collective-permute-start.1 = (bf16[32,1152]{1,0:T(8,128)(2,1)S(1)}, bf16[32,1152]{1,0:T(8,128)(2,1)S(1)}, u32[]{:S(2)}, u32[]{:S(2)}) collective-permute-start(bf16[32,1152]{1,0:T(8,128)(2,1)S(1)} %pad_maximum_fusion.2), channel_id=1, source_target_pairs={{0,2},{1,3},{2,0},{3,1},{4,6},{5,7},{6,4},{7,5},{8,10},{9,11},{10,... | collective-permute-start | bytes 221192 | tf_op jit(solution)/shard_map/ppermute | solution.py:364
  14.1 6.8 %collective-permute-start = (bf16[32,1152]{1,0:T(8,128)(2,1)S(1)}, bf16[32,1152]{1,0:T(8,128)(2,1)S(1)}, u32[]{:S(2)}, u32[]{:S(2)}) collective-permute-start(bf16[32,1152]{1,0:T(8,128)(2,1)S(1)} %pad_maximum_fusion.2), channel_id=1, source_target_pairs={{0,1},{1,2},{2,3},{3,0},{4,5},{5,6},{6,7},{7,4},{8,9},{9,10},{10,1... | collective-permute-start | bytes 221192 | tf_op jit(solution)/shard_map/ppermute | solution.py:364
  21.0 9.5 %collective-permute-start.4 = (bf16[4,32,1152]{2,1,0:T(8,128)(2,1)S(1)}, bf16[4,32,1152]{2,1,0:T(8,128)(2,1)S(1)}, u32[]{:S(2)}, u32[]{:S(2)}) collective-permute-start(bf16[4,32,1152]{2,1,0:T(8,128)(2,1)S(1)} %get-tuple-element.8), channel_id=1, source_target_pairs={{0,8},{1,9},{2,10},{3,11},{4,12},{5,13},{6,14},{7,15},{8,0},{9,1},... | collective-permute-start | bytes 884744 | tf_op jit(solution)/shard_map/ppermute | solution.py:364
  23.8 14.1 %collective-permute-start.3 = (bf16[4,32,1152]{2,1,0:T(8,128)(2,1)S(1)}, bf16[4,32,1152]{2,1,0:T(8,128)(2,1)S(1)}, u32[]{:S(2)}, u32[]{:S(2)}) collective-permute-start(bf16[4,32,1152]{2,1,0:T(8,128)(2,1)S(1)} %get-tuple-element.8), channel_id=1, source_target_pairs={{0,4},{1,5},{2,6},{3,7},{4,8},{5,9},{6,10},{7,11},{8,12},{9,13},{1... | collective-permute-start | bytes 884744 | tf_op jit(solution)/shard_map/ppermute | solution.py:364
  24.1 13.8 %collective-permute-start.5 = (bf16[4,32,1152]{2,1,0:T(8,128)(2,1)S(1)}, bf16[4,32,1152]{2,1,0:T(8,128)(2,1)S(1)}, u32[]{:S(2)}, u32[]{:S(2)}) collective-permute-start(bf16[4,32,1152]{2,1,0:T(8,128)(2,1)S(1)} %get-tuple-element.8), channel_id=1, source_target_pairs={{0,12},{1,13},{2,14},{3,15},{4,0},{5,1},{6,2},{7,3},{8,4},{9,5},{1... | collective-permute-start | bytes 884744 | tf_op jit(solution)/shard_map/ppermute | solution.py:364
  54.9 23.5 %all-to-all-start.1 = ((bf16[16,272,128]{2,1,0:T(8,128)(2,1)}), bf16[16,272,128]{2,1,0:T(8,128)(2,1)S(1)}, u32[]{:S(2)}, u32[]{:S(2)}) async-start(bf16[16,272,128]{2,1,0:T(8,128)(2,1)} %attend.1), calls=%async_computation.1 | async-start | bytes 2228224 | tf_op jit(solution)/shard_map/all_to_all | solution.py:381
  79.7 6.6 %collective-permute-start.8 = (bf16[32,1024]{1,0:T(8,128)(2,1)S(1)}, bf16[32,1024]{1,0:T(8,128)(2,1)S(1)}, u32[]{:S(2)}, u32[]{:S(2)}) collective-permute-start(bf16[32,1024]{1,0:T(8,128)(2,1)S(1)} %finish.1.refs_0_), channel_id=1, source_target_pairs={{0,64},{16,80},{32,96},{48,112},{64,0},{80,16},{96,32},{112,48},{1... | collective-permute-start | bytes 196616 | tf_op jit(solution)/shard_map/ppermute | solution.py:392
  80.3 8.5 %collective-permute-start.7 = (bf16[32,1024]{1,0:T(8,128)(2,1)S(1)}, bf16[32,1024]{1,0:T(8,128)(2,1)S(1)}, u32[]{:S(2)}, u32[]{:S(2)}) collective-permute-start(bf16[32,1024]{1,0:T(8,128)(2,1)S(1)} %finish.1.refs_0_), channel_id=1, source_target_pairs={{0,96},{16,112},{32,0},{48,16},{64,32},{80,48},{96,64},{112,80},{1... | collective-permute-start | bytes 196616 | tf_op jit(solution)/shard_map/ppermute | solution.py:392
  82.5 6.4 %collective-permute-start.6 = (bf16[32,1024]{1,0:T(8,128)(2,1)S(1)}, bf16[32,1024]{1,0:T(8,128)(2,1)S(1)}, u32[]{:S(2)}, u32[]{:S(2)}) collective-permute-start(bf16[32,1024]{1,0:T(8,128)(2,1)S(1)} %finish.1.refs_0_), channel_id=1, source_target_pairs={{0,32},{16,48},{32,64},{48,80},{64,96},{80,112},{96,0},{112,16},{1... | collective-permute-start | bytes 196616 | tf_op jit(solution)/shard_map/ppermute | solution.py:392
  82.5 9.3 %collective-permute-start.9 = (bf16[32,1024]{1,0:T(8,128)(2,1)S(1)}, bf16[32,1024]{1,0:T(8,128)(2,1)S(1)}, u32[]{:S(2)}, u32[]{:S(2)}) collective-permute-start(bf16[32,1024]{1,0:T(8,128)(2,1)S(1)} %finish.1.refs_0_), channel_id=1, source_target_pairs={{0,16},{16,0},{32,48},{48,32},{64,80},{80,64},{96,112},{112,96},{1... | collective-permute-start | bytes 196616 | tf_op jit(solution)/shard_map/ppermute | solution.py:392
  86.3 5.5 %collective-permute-start.12 = (bf16[32,1024]{1,0:T(8,128)(2,1)S(1)}, bf16[32,1024]{1,0:T(8,128)(2,1)S(1)}, u32[]{:S(2)}, u32[]{:S(2)}) collective-permute-start(bf16[32,1024]{1,0:T(8,128)(2,1)S(1)} %collective-permute-done.8.refs_3_), channel_id=1, source_target_pairs={{0,16},{16,0},{32,48},{48,32},{64,80},{80,64},{96,112},{112,96},{1... | collective-permute-start | bytes 196616 | tf_op jit(solution)/shard_map/ppermute | solution.py:392
  88.9 3.0 %collective-permute-start.11 = (bf16[32,1024]{1,0:T(8,128)(2,1)S(1)}, bf16[32,1024]{1,0:T(8,128)(2,1)S(1)}, u32[]{:S(2)}, u32[]{:S(2)}) collective-permute-start(bf16[32,1024]{1,0:T(8,128)(2,1)S(1)} %collective-permute-done.7.refs_2_), channel_id=1, source_target_pairs={{0,16},{16,0},{32,48},{48,32},{64,80},{80,64},{96,112},{112,96},{1... | collective-permute-start | bytes 196616 | tf_op jit(solution)/shard_map/ppermute | solution.py:392
  88.9 3.8 %collective-permute-start.10 = (bf16[32,1024]{1,0:T(8,128)(2,1)S(1)}, bf16[32,1024]{1,0:T(8,128)(2,1)S(1)}, u32[]{:S(2)}, u32[]{:S(2)}) collective-permute-start(bf16[32,1024]{1,0:T(8,128)(2,1)S(1)} %collective-permute-done.6.refs_1_), channel_id=1, source_target_pairs={{0,16},{16,0},{32,48},{48,32},{64,80},{80,64},{96,112},{112,96},{1... | collective-permute-start | bytes 196616 | tf_op jit(solution)/shard_map/ppermute | solution.py:392

commit v4 on v3

--- a/solution.py
+++ b/solution.py
@@ -34,6 +34,7 @@
 OUT_ROWS = 32 * GROUP + 16
 LOW = -1e9
 DEAD = -1e30
+NOBODY = 255
 
 
 def pack_kernel(fill, pool, out, staged, ready, arrived, left):
@@ -96,24 +97,30 @@
     values[:, :, HEAD_DIM:] = jnp.ones((TOGETHER, TOKENS, HEAD_DIM), jnp.bfloat16)
     row_rollout = lax.broadcasted_iota(jnp.int32, (ROWS, HEAD_DIM), 0) // GROUP
     lane = lax.broadcasted_iota(jnp.int32, (ROWS, HEAD_DIM), 1)
-    member_lanes = jnp.where(row_rollout == lane, 1.0, 0.0).astype(jnp.bfloat16)
+
+    def member_lanes(parity):
+        mine = row_rollout + TILE * parity == lane
+        return jnp.where(mine, 1.0, 0.0).astype(jnp.bfloat16)
+
+    members = [member_lanes(parity) for parity in range(2)]
     pick = lax.broadcasted_iota(jnp.int32, (8, HEAD_DIM), 0)
     pick_lane = lax.broadcasted_iota(jnp.int32, (8, HEAD_DIM), 1)
     picked = jnp.where(pick == pick_lane, 1.0, 0.0).astype(jnp.bfloat16)
 
-    def chunk_scores(tile, chunk, lane_of, size=CHUNK):
+    def chunk_scores(tile, chunk, lane_of, size=CHUNK, member=None):
+        member = member_lanes(tile & 1) if member is None else member
         rows = query[pl.ds(pl.multiple_of(tile * ROWS, ROWS), ROWS), :]
-        left = jnp.concatenate([rows, member_lanes], axis=1)
+        left = jnp.concatenate([rows, member], axis=1)
         for slot in range(size):
             number = chunk * CHUNK + slot
-            code = codes[tile * BLOCKS + number]
+            code = codes[tile, number]
             row = pl.multiple_of(code * BLK_TOKENS, BLK_TOKENS)
             place = pl.ds(slot * BLK_TOKENS, BLK_TOKENS)
             key = kv[pl.ds(row, BLK_TOKENS), 0:HEAD_DIM].astype(jnp.float32)
-            live = (key < MARK) & (number < counts[tile])
+            live = (key < MARK) & (number < counts[0, tile])
             keys[lane_of, place, 0:HEAD_DIM] = jnp.where(live, key, 0.0).astype(jnp.bfloat16)
             keys[lane_of, place, HEAD_DIM:] = jnp.where(
-                live, barred[pl.ds(tile * BLOCKS + code, 1), :], DEAD
+                live, barred[pl.ds((tile >> 1) * BLOCKS + code, 1), :], DEAD
             ).astype(jnp.bfloat16)
             values[lane_of, place, 0:HEAD_DIM] = kv[pl.ds(row, BLK_TOKENS), HEAD_DIM:]
         return lax.dot_general(
@@ -160,7 +167,7 @@
             out[owner, count:, :] = both.astype(jnp.bfloat16)
 
     def long_tile(tile):
-        chunks = (counts[tile] + CHUNK - 1) // CHUNK
+        chunks = (counts[0, tile] + CHUNK - 1) // CHUNK
         found = chunk_scores(tile, 0, 0)
         peak = highest(found, LOW)
         peaks[...] = jnp.broadcast_to(peak, (ROWS, HEAD_DIM))
@@ -179,15 +186,17 @@
 
     def some_tiles(step, _):
         tiles = [step * TOGETHER + k for k in range(TOGETHER)]
-        most = counts[tiles[0]]
+        most = counts[0, tiles[0]]
         for tile in tiles[1:]:
-            most = jnp.maximum(most, counts[tile])
+            most = jnp.maximum(most, counts[0, tile])
 
         for fewer, size in zip((-1,) + SIZES, SIZES):
 
             @pl.when((most > fewer) & (most <= size))
             def _():
-                found = [chunk_scores(tile, 0, k, size) for k, tile in enumerate(tiles)]
+                found = [
+                    chunk_scores(tile, 0, k, size, members[k % 2]) for k, tile in enumerate(tiles)
+                ]
                 peak = [highest(one, LOW) for one in found]
                 added = [summed(found[k], peak[k], k) for k in range(TOGETHER)]
                 for k, tile in enumerate(tiles):
@@ -199,7 +208,7 @@
 
         return 0
 
-    lax.fori_loop(0, counts.shape[0] // TOGETHER, some_tiles, 0)
+    lax.fori_loop(0, codes.shape[0] // TOGETHER, some_tiles, 0)
 
 
 def attend(codes, counts, group, kv, query, barred):
@@ -311,30 +320,90 @@
     )(node.reshape(1).astype(jnp.int32), *mine, *other)
 
 
-def local_number(ids, column):
-    device = ids // OWN_BLOCKS
-    here = (device % 16) == column
-    return jnp.where(here, (device // 16) * OWN_BLOCKS + ids % OWN_BLOCKS, -1)
-
-
-def visits(root, lists):
-    tiles, _, rollouts = lists.shape
-    numbers = jnp.arange(BLOCKS, dtype=jnp.int32)
-    everyone = jnp.any(root[:, None] == numbers, axis=0)
-    member = jnp.any(lists[:, :, None, :] == numbers[None, None, :, None], axis=1)
-    member = member | everyone[None, :, None]
-    hit = jnp.any(member, axis=2)
-    counts = jnp.sum(hit, axis=1, dtype=jnp.int32)
-    before = (numbers[:, None] < numbers[None, :]).astype(jnp.bfloat16)
-    place = jnp.dot(hit.astype(jnp.bfloat16), before, preferred_element_type=jnp.float32)
-    place = jnp.where(hit, place.astype(jnp.int32), -1)
-    codes = jnp.sum(jnp.where(place[:, None, :] == numbers[None, :, None], numbers, 0), axis=2)
-    barred = jnp.pad(jnp.where(member, 0.0, DEAD), ((0, 0), (0, 0), (0, HEAD_DIM - rollouts)))
-    return (
-        codes.astype(jnp.int32).reshape(tiles * BLOCKS),
-        counts,
-        barred.reshape(tiles * BLOCKS, HEAD_DIM),
+def visits_kernel(column, told, root, codes, counts, barred, hits, places):
+    entries = LIST - ROOT_BLOCKS
+    entry = lax.broadcasted_iota(jnp.int32, (2 * entries, HEAD_DIM), 0)
+    lane = lax.broadcasted_iota(jnp.int32, (2 * entries, HEAD_DIM), 1)
+    picked = jnp.where(entry == lane, 1.0, 0.0).astype(jnp.bfloat16)
+    dims = (((1,), (1,)), ((), ()))
+    turned = lax.dot_general(picked, told[...], dims, preferred_element_type=jnp.float32)
+    turned = turned.astype(jnp.int32)
+
+    def local(device, place):
+        here = ((device & 15) == column[0]) & (device < NOBODY)
+        return jnp.where(here, (device >> 4) * OWN_BLOCKS + place, -1)
+
+    listed = local(turned[0:entries], turned[entries:])
+    root_row = local(root[0:1, :], root[1:2, :])
+    span = 64
+    for part in range(BLOCKS // span):
+        rows = slice(part * span, (part + 1) * span)
+        number = lax.broadcasted_iota(jnp.int32, (span, HEAD_DIM), 0) + part * span
+        lane = lax.broadcasted_iota(jnp.int32, (span, HEAD_DIM), 1)
+        everyone = jnp.max(jnp.where(root_row == number, 1.0, 0.0), axis=1, keepdims=True)
+        found = jnp.zeros((span, HEAD_DIM), jnp.float32)
+        for pair in range(told.shape[0] // HEAD_DIM):
+            member = jnp.broadcast_to(everyone, (span, HEAD_DIM))
+            for index in range(entries):
+                row = listed[index : index + 1, pair * HEAD_DIM : (pair + 1) * HEAD_DIM]
+                member = jnp.where(row == number, 1.0, member)
+            barred[pl.ds(pair * BLOCKS + part * span, span), :] = jnp.where(
+                member > 0.5, 0.0, DEAD
+            )
+            for parity in range(2):
+                mine = (lane < TILE) if parity == 0 else (lane >= TILE)
+                hit = jnp.max(jnp.where(mine, member, 0.0), axis=1, keepdims=True)
+                found = jnp.where(lane == 2 * pair + parity, hit, found)
+        hits[rows, :] = found
+    hit = hits[...]
+    counts[...] = jnp.broadcast_to(jnp.sum(hit, axis=0, keepdims=True), counts.shape).astype(
+        jnp.int32
     )
+    row = lax.broadcasted_iota(jnp.int32, (BLOCKS, BLOCKS), 0)
+    col = lax.broadcasted_iota(jnp.int32, (BLOCKS, BLOCKS), 1)
+    before = jnp.where(col < row, 1.0, 0.0).astype(jnp.bfloat16)
+    place = jnp.dot(before, hit.astype(jnp.bfloat16), preferred_element_type=jnp.float32)
+    places[...] = jnp.where(hit > 0.5, place, -1.0)
+    most = jnp.max(jnp.sum(hit, axis=0, keepdims=True))
+
+    def listing(width):
+        wide = lax.broadcasted_iota(jnp.int32, (BLOCKS, width), 1).astype(jnp.float32)
+        number = lax.broadcasted_iota(jnp.int32, (BLOCKS, width), 0)
+        for tile in range(codes.shape[0]):
+            there = places[:, tile : tile + 1] == wide
+            found = jnp.sum(jnp.where(there, number, 0), axis=0, keepdims=True)
+            codes[tile : tile + 1, 0:width] = found
+
+    @pl.when(most <= HEAD_DIM)
+    def _():
+        listing(HEAD_DIM)
+        codes[:, HEAD_DIM:] = jnp.zeros((codes.shape[0], BLOCKS - HEAD_DIM), jnp.int32)
+
+    @pl.when(most > HEAD_DIM)
+    def _():
+        listing(BLOCKS)
+
+
+def visits(column, told, root):
+    tiles = told.shape[0] // TILE
+    vmem = pl.BlockSpec(memory_space=pltpu.VMEM)
+    return pl.pallas_call(
+        visits_kernel,
+        out_shape=[
+            jax.ShapeDtypeStruct((tiles, BLOCKS), jnp.int32),
+            jax.ShapeDtypeStruct((8, HEAD_DIM), jnp.int32),
+            jax.ShapeDtypeStruct((tiles // 2 * BLOCKS, HEAD_DIM), jnp.float32),
+        ],
+        in_specs=[pl.BlockSpec(memory_space=pltpu.SMEM), vmem, vmem],
+        out_specs=[vmem] * 3,
+        scratch_shapes=[
+            pltpu.VMEM((BLOCKS, HEAD_DIM), jnp.float32),
+            pltpu.VMEM((BLOCKS, HEAD_DIM), jnp.float32),
+        ],
+        compiler_params=pltpu.CompilerParams(vmem_limit_bytes=26 * 1024 * 1024),
+        cost_estimate=pl.CostEstimate(flops=10**8, bytes_accessed=2 << 20, transcendentals=0),
+        name="visits",
+    )(column, told, root)
 
 
 def per_device(queries, new_entry, block_lists, list_lengths, block_fill, cache_pool):
@@ -349,8 +418,10 @@
 
     head_query = lax.dynamic_slice_in_dim(queries, node * WIDTH, WIDTH, axis=1)
     entries = jnp.arange(LIST, dtype=jnp.int32)[None, :]
-    tail = jnp.where(entries < list_lengths[:, None], block_lists, 8191)[:, ROOT_BLOCKS:]
-    coded = jnp.concatenate([tail // 128, tail % 128], axis=1).astype(jnp.bfloat16)
+    listed = entries < list_lengths[:, None]
+    device = jnp.where(listed, block_lists // OWN_BLOCKS, NOBODY)[:, ROOT_BLOCKS:]
+    place = (block_lists % OWN_BLOCKS)[:, ROOT_BLOCKS:]
+    coded = jnp.concatenate([device, place], axis=1).astype(jnp.bfloat16)
     coded = jnp.pad(coded, ((0, 0), (0, HEAD_DIM - coded.shape[1])))
     told = jnp.concatenate([head_query, coded], axis=1)
     sent, told = lax.optimization_barrier((sent, told))
@@ -367,16 +438,12 @@
     told = jnp.stack([line] + [shifted(line, hop, 0) for hop in range(1, side)])
     told = told.reshape((groups,) + told.shape[2:])
     all_query = told[:, :, :WIDTH].reshape(groups * own_rows * GROUP, HEAD_DIM)
-    coded = told[:, :, WIDTH:].astype(jnp.int32).reshape(groups * own_rows, HEAD_DIM)
-    count = LIST - ROOT_BLOCKS
-    ids = coded[:, :count] * 128 + coded[:, count : 2 * count]
-    tail = jnp.where(ids < 8191, local_number(ids, column), -1)
-    root = local_number(block_lists[0, :ROOT_BLOCKS], column)
-    tiles = groups * own_rows // TILE
-    codes, counts, barred = visits(
-        root, jnp.transpose(tail.reshape(tiles, TILE, count), (0, 2, 1))
-    )
+    coded = told[:, :, WIDTH:].reshape(groups * own_rows, HEAD_DIM)
+    root = block_lists[0, :ROOT_BLOCKS]
+    root = jnp.stack([root // OWN_BLOCKS, root % OWN_BLOCKS])
+    root = jnp.pad(root, ((0, 6), (0, HEAD_DIM - ROOT_BLOCKS)), constant_values=NOBODY)
     group = column.reshape(1).astype(jnp.int32)
+    codes, counts, barred = visits(group, coded, root)
     partial = attend(codes, counts, group, kv, all_query, barred)
     parts = lax.all_to_all(partial, "group", split_axis=0, concat_axis=0, tiled=True)
     key = lax.dynamic_slice_in_dim(new_entry, node * HEAD_DIM, HEAD_DIM, axis=1)

time: 94 us -> 94.1 us (level)
  other arithmetic: 5.17 us -> 0.46 us
  waiting for transfers between devices: 34.5 us -> 37.8 us
  Pallas kernels: 13.4 us -> 15.7 us
  local copies, waits for them, and re-layouts: 4.68 us -> 3.44 us
    reduce_or x3 -> x0, other arithmetic: 3.27 us -> none  [the longest x1 3.06 us: visits(): jnp.any(lists[:, :, None, :] == numbers[None, None, :, None], axis=1)]
    all_to_all x1, waiting for transfers between devices: 0.88 us -> 4.1 us  [per_device(): kv = lax.all_to_all(sent, 'node', split_axis=0, concat_axis=0, tiled=True)]
    pallas_call x0 -> x1, Pallas kernels: none -> 2.8 us  [visits(): pl.pallas_call(visits_kernel, out_shape=[jax.ShapeDtypeStruct((tiles, BLO...]
    unnamed x7 -> x6, local copies, waits for them, and re-layouts: 1.63 us -> 0.02 us
    pad x1, local copies, waits for them, and re-layouts: 1.51 us -> 0.01 us  [per_device(): jnp.pad(root, ((0, 6), (0, HEAD_DIM - ROOT_BLOCKS)), constant_values=NOBODY)]
    reshape x1, local copies, waits for them, and re-layouts: 0.49 us -> 1.51 us  [per_device(): all_query = told[:, :, :WIDTH].reshape(groups * own_rows * GROUP, HEAD_DIM)]
    slice x1, local copies, waits for them, and re-layouts: 0.14 us -> 1.12 us  [per_device(): all_query = told[:, :, :WIDTH].reshape(groups * own_rows * GROUP, HEAD_DIM)]
  transfers between devices with their start and end apart: 15 -> 15, of which waited for: 8 -> 8; matrix products, arithmetic and copies ran while one was open for 11% -> 4% of each run, Pallas kernels for 0% -> 3%
where the time goes in v4:
time: 94.1 us; the launch traced here: 93.6 us
  waiting for transfers between devices  37.8 us (40%)
  starting transfers between devices  36 us (38%)
  Pallas kernels  15.7 us (17%)
  local copies, waits for them, and re-layouts  3.44 us (4%)
    ppermute x6, waiting for transfers between devices, shifted(): return lax.ppermute(value, 'group', pairs)  17.5 us
    all_to_all x1, waiting for transfers between devices, per_device(): lax.all_to_all(partial, 'group', split_axis=0, concat_axis=0, tiled=True)  15.3 us
    ppermute x7, starting transfers between devices, from_node(): return lax.ppermute(value, 'node', [(i, to(i)) for i in range(nodes)])  12.1 us
    ppermute x6, starting transfers between devices, shifted(): return lax.ppermute(value, 'group', pairs)  10 us
    all_to_all x1, starting transfers between devices, per_device(): lax.all_to_all(partial, 'group', split_axis=0, concat_axis=0, tiled=True)  7.94 us
    pallas_call x1, Pallas kernels, attend(): pl.pallas_call(attend_kernel, out_shape=jax.ShapeDtypeStruct((sources, OU...  6.79 us
    all_to_all x1, starting transfers between devices, per_device(): kv = lax.all_to_all(sent, 'node', split_axis=0, concat_axis=0, tiled=True)  5.98 us
    all_to_all x1, waiting for transfers between devices, per_device(): kv = lax.all_to_all(sent, 'node', split_axis=0, concat_axis=0, tiled=True)  4.1 us
  transfers between devices with their start and end apart: 15, of which 8 were waited for; matrix products, arithmetic and copies ran while one was open for 4% of the time, Pallas kernels for 3%

profile of v4, /device:TPU:1, one launch (start us, length us, event | category | flops | bytes accessed | tf_op | source)
XLA Modules:
  0.0 93.6 jit_solution(12291303166981316753)
XLA Ops:
  0.0 4.0 %pack.1 = bf16[8,768,256]{2,1,0:T(8,128)(2,1)} custom-call(s32[48]{0:T(128)} %fill.1, bf16[768,2048]{1,0:T(8,128)(2,1)} %bitcast.18), custom_call_target="tpu_custom_call" | custom-call | tf_op jit(solution)/shard_map/pack/pallas_call | solution.py:80
  4.0 6.0 %all-to-all-start = ((bf16[8,768,256]{2,1,0:T(8,128)(2,1)}), bf16[8,768,256]{2,1,0:T(8,128)(2,1)}, u32[]{:S(2)}, u32[]{:S(2)}) async-start(bf16[8,768,256]{2,1,0:T(8,128)(2,1)} %pack.1), calls=%async_computation | async-start | bytes 6291456 | tf_op jit(solution)/shard_map/all_to_all | solution.py:416
  10.0 0.1 fusion.1
  10.1 0.1 fusion.6
  10.2 3.8 %collective-permute-start.2 = (bf16[32,1152]{1,0:T(8,128)(2,1)S(1)}, bf16[32,1152]{1,0:T(8,128)(2,1)S(1)}, u32[]{:S(2)}, u32[]{:S(2)}) collective-permute-start(bf16[32,1152]{1,0:T(8,128)(2,1)S(1)} %pad_maximum_fusion.2), channel_id=1, source_target_pairs={{0,3},{1,0},{2,1},{3,2},{4,7},{5,4},{6,5},{7,6},{8,11},{9,8},{10,9... | collective-permute-start | bytes 221192 | tf_op jit(solution)/shard_map/ppermute | solution.py:435
  14.1 0.7 collective-permute-start
  14.8 2.4 %collective-permute-done.2 = bf16[32,1152]{1,0:T(8,128)(2,1)S(1)} collective-permute-done((bf16[32,1152]{1,0:T(8,128)(2,1)S(1)}, bf16[32,1152]{1,0:T(8,128)(2,1)S(1)}, u32[]{:S(2)}, u32[]{:S(2)}) %collective-permute-start.2) | collective-permute-done | bytes 73760 | tf_op jit(solution)/shard_map/ppermute | solution.py:435
  17.2 2.0 %collective-permute-done.1 = bf16[32,1152]{1,0:T(8,128)(2,1)S(1)} collective-permute-done((bf16[32,1152]{1,0:T(8,128)(2,1)S(1)}, bf16[32,1152]{1,0:T(8,128)(2,1)S(1)}, u32[]{:S(2)}, u32[]{:S(2)}) %collective-permute-start.1) | collective-permute-done | bytes 73760 | tf_op jit(solution)/shard_map/ppermute | solution.py:435
  19.2 1.7 %collective-permute-done = bf16[32,1152]{1,0:T(8,128)(2,1)S(1)} collective-permute-done((bf16[32,1152]{1,0:T(8,128)(2,1)S(1)}, bf16[32,1152]{1,0:T(8,128)(2,1)S(1)}, u32[]{:S(2)}, u32[]{:S(2)}) %collective-permute-start) | collective-permute-done | bytes 73760 | tf_op jit(solution)/shard_map/ppermute | solution.py:435
  20.9 0.1 fusion.7
  21.0 2.8 %collective-permute-start.4 = (bf16[4,32,1152]{2,1,0:T(8,128)(2,1)S(1)}, bf16[4,32,1152]{2,1,0:T(8,128)(2,1)S(1)}, u32[]{:S(2)}, u32[]{:S(2)}) collective-permute-start(bf16[4,32,1152]{2,1,0:T(8,128)(2,1)S(1)} %get-tuple-element.14), channel_id=1, source_target_pairs={{0,8},{1,9},{2,10},{3,11},{4,12},{5,13},{6,14},{7,15},{8,0},{9,1},... | collective-permute-start | bytes 884744 | tf_op jit(solution)/shard_map/ppermute | solution.py:435
  23.8 0.3 collective-permute-start.3
  24.1 2.4 %collective-permute-start.5 = (bf16[4,32,1152]{2,1,0:T(8,128)(2,1)S(1)}, bf16[4,32,1152]{2,1,0:T(8,128)(2,1)S(1)}, u32[]{:S(2)}, u32[]{:S(2)}) collective-permute-start(bf16[4,32,1152]{2,1,0:T(8,128)(2,1)S(1)} %get-tuple-element.14), channel_id=1, source_target_pairs={{0,12},{1,13},{2,14},{3,15},{4,0},{5,1},{6,2},{7,3},{8,4},{9,5},{1... | collective-permute-start | bytes 884744 | tf_op jit(solution)/shard_map/ppermute | solution.py:435
  26.5 4.0 %collective-permute-done.4 = bf16[4,32,1152]{2,1,0:T(8,128)(2,1)S(1)} collective-permute-done((bf16[4,32,1152]{2,1,0:T(8,128)(2,1)S(1)}, bf16[4,32,1152]{2,1,0:T(8,128)(2,1)S(1)}, u32[]{:S(2)}, u32[]{:S(2)}) %collective-permute-start.4) | collective-permute-done | bytes 294944 | tf_op jit(solution)/shard_map/ppermute | solution.py:435
  30.5 7.4 %collective-permute-done.3 = bf16[4,32,1152]{2,1,0:T(8,128)(2,1)S(1)} collective-permute-done((bf16[4,32,1152]{2,1,0:T(8,128)(2,1)S(1)}, bf16[4,32,1152]{2,1,0:T(8,128)(2,1)S(1)}, u32[]{:S(2)}, u32[]{:S(2)}) %collective-permute-start.3) | collective-permute-done | bytes 294944 | tf_op jit(solution)/shard_map/ppermute | solution.py:435
  37.9 0.2 pad_maximum_fusion
  38.1 1.1 %slice.27 = bf16[16,32,1024]{2,1,0:T(8,128)(2,1)} slice(bf16[16,32,1152]{2,1,0:T(8,128)(2,1)S(1)} %bitcast.17), slice={[0:16], [0:32], [0:1024]} | slice | bytes 2097152 | tf_op jit(solution)/shard_map/slice | solution.py:440
  39.2 1.5 %reshape.31.query = bf16[4096,128]{1,0:T(8,128)(2,1)S(1)} reshape(bf16[16,32,1024]{2,1,0:T(8,128)(2,1)} %slice.27) | data formatting | bytes 2097152 | tf_op jit(solution)/shard_map/reshape | solution.py:440
  40.8 2.8 %visits.1 = (s32[8,384]{1,0:T(8,128)S(1)}, s32[8,128]{1,0:T(8,128)S(1)}, f32[1536,128]{1,0:T(8,128)S(1)}) custom-call(s32[1]{0:T(128)} %bitcast.1.column.group, bf16[512,128]{1,0:T(8,128)(2,1)S(1)} %bitcast.15, s32[8,128]{1,0:T(8,128)S(1)} %pad.9.root), custom_call_target="tpu_custom_call" | custom-call | flops 100000000 | bytes 2097152 | tf_op jit(solution)/shard_map/visits/pallas_call | solution.py:390
  43.6 4.1 %all-to-all-done = bf16[8,768,256]{2,1,0:T(8,128)(2,1)} async-done(((bf16[8,768,256]{2,1,0:T(8,128)(2,1)}), bf16[8,768,256]{2,1,0:T(8,128)(2,1)}, u32[]{:S(2)}, u32[]{:S(2)}) %all-to-all-start) | async-done | bytes 3145760 | tf_op jit(solution)/shard_map/all_to_all | solution.py:416
  47.7 6.8 %attend.1 = bf16[16,272,128]{2,1,0:T(8,128)(2,1)} custom-call(s32[8,384]{1,0:T(8,128)S(1)} %get-tuple-element.10.codes, s32[8,128]{1,0:T(8,128)S(1)} %get-tuple-element.11.counts, s32[1]{0:T(128)} %bitcast.1.column.group, bf16[6144,256]{1,0:T(8,128)(2,1)} %bitcast.13.kv, bf16[4096,128]{1,0:T(8,128)(2,1)S(1)} %reshape.31.query, ...), custom_call_target="tpu_custom_call" | custom-call | flops 2147483648 | bytes 6291456 | tf_op jit(solution)/shard_map/attend/pallas_call | solution.py:218
  54.5 7.9 %all-to-all-start.1 = ((bf16[16,272,128]{2,1,0:T(8,128)(2,1)}), bf16[16,272,128]{2,1,0:T(8,128)(2,1)S(1)}, u32[]{:S(2)}, u32[]{:S(2)}) async-start(bf16[16,272,128]{2,1,0:T(8,128)(2,1)} %attend.1), calls=%async_computation.1 | async-start | bytes 2228224 | tf_op jit(solution)/shard_map/all_to_all | solution.py:448
  62.4 0.7 constant_dynamic-slice_fusion.1
  63.2 15.3 %all-to-all-done.1.parts = bf16[16,272,128]{2,1,0:T(8,128)(2,1)S(1)} async-done(((bf16[16,272,128]{2,1,0:T(8,128)(2,1)}), bf16[16,272,128]{2,1,0:T(8,128)(2,1)S(1)}, u32[]{:S(2)}, u32[]{:S(2)}) %all-to-all-start.1) | async-done | bytes 1114144 | tf_op jit(solution)/shard_map/all_to_all | solution.py:448
  78.5 1.3 %finish.1.refs_0_ = bf16[32,1024]{1,0:T(8,128)(2,1)S(1)} custom-call(bf16[16,272,128]{2,1,0:T(8,128)(2,1)S(1)} %all-to-all-done.1.parts, bf16[256,128]{1,0:T(8,128)(2,1)S(1)} %reshape.32.query, bf16[32,256]{1,0:T(8,128)(2,1)S(1)} %pad_maximum_fusion.3.entry), custom_call_target="tpu_custom_call" | custom-call | tf_op jit(solution)/shard_map/finish/pallas_call | solution.py:284
  79.7 0.6 collective-permute-start.8
  80.4 2.1 %collective-permute-start.7 = (bf16[32,1024]{1,0:T(8,128)(2,1)S(1)}, bf16[32,1024]{1,0:T(8,128)(2,1)S(1)}, u32[]{:S(2)}, u32[]{:S(2)}) collective-permute-start(bf16[32,1024]{1,0:T(8,128)(2,1)S(1)} %finish.1.refs_0_), channel_id=1, source_target_pairs={{0,96},{16,112},{32,0},{48,16},{64,32},{80,48},{96,64},{112,80},{1... | collective-permute-start | bytes 196616 | tf_op jit(solution)/shard_map/ppermute | solution.py:459
  82.5 3.9 %collective-permute-start.9 = (bf16[32,1024]{1,0:T(8,128)(2,1)S(1)}, bf16[32,1024]{1,0:T(8,128)(2,1)S(1)}, u32[]{:S(2)}, u32[]{:S(2)}) collective-permute-start(bf16[32,1024]{1,0:T(8,128)(2,1)S(1)} %finish.1.refs_0_), channel_id=1, source_target_pairs={{0,16},{16,0},{32,48},{48,32},{64,80},{80,64},{96,112},{112,96},{1... | collective-permute-start | bytes 196616 | tf_op jit(solution)/shard_map/ppermute | solution.py:459
  86.4 2.5 %collective-permute-start.12 = (bf16[32,1024]{1,0:T(8,128)(2,1)S(1)}, bf16[32,1024]{1,0:T(8,128)(2,1)S(1)}, u32[]{:S(2)}, u32[]{:S(2)}) collective-permute-start(bf16[32,1024]{1,0:T(8,128)(2,1)S(1)} %collective-permute-done.8.refs_3_), channel_id=1, source_target_pairs={{0,16},{16,0},{32,48},{48,32},{64,80},{80,64},{96,112},{112,96},{1... | collective-permute-start | bytes 196616 | tf_op jit(solution)/shard_map/ppermute | solution.py:459
  88.9 2.9 %collective-permute-start.10 = (bf16[32,1024]{1,0:T(8,128)(2,1)S(1)}, bf16[32,1024]{1,0:T(8,128)(2,1)S(1)}, u32[]{:S(2)}, u32[]{:S(2)}) collective-permute-start(bf16[32,1024]{1,0:T(8,128)(2,1)S(1)} %collective-permute-done.6.refs_1_), channel_id=1, source_target_pairs={{0,16},{16,0},{32,48},{48,32},{64,80},{80,64},{96,112},{112,96},{1... | collective-permute-start | bytes 196616 | tf_op jit(solution)/shard_map/ppermute | solution.py:459
  91.8 0.9 collective-permute-done.10.refs_5_
  92.7 0.8 place_heads.1
  (26 shorter events, 0.2 us)
Async XLA Ops:
  0.0 10.2 %copy-start = (bf16[32,8192]{1,0:T(8,128)(2,1)S(1)}, bf16[32,8192]{1,0:T(8,128)(2,1)}, u32[]{:S(2)}) copy-start(bf16[32,8192]{1,0:T(8,128)(2,1)} %param.6) | copy-start | bytes 1572868
  4.0 6.0 %copy-start.1 = (s32[32,64]{1,0:T(8,128)S(1)}, s32[32,64]{1,0:T(8,128)}, u32[]{:S(2)}) copy-start(s32[32,64]{1,0:T(8,128)} %param.8) | copy-start | bytes 24580
  4.0 6.0 %copy-start.2 = (s32[32]{0:T(128)S(1)}, s32[32]{0:T(128)}, u32[]{:S(2)}) copy-start(s32[32]{0:T(128)} %param.9) | copy-start | bytes 388
  4.0 43.7 %all-to-all-start = ((bf16[8,768,256]{2,1,0:T(8,128)(2,1)}), bf16[8,768,256]{2,1,0:T(8,128)(2,1)}, u32[]{:S(2)}, u32[]{:S(2)}) async-start(bf16[8,768,256]{2,1,0:T(8,128)(2,1)} %pack.1), calls=%async_computation | async-start | bytes 6291456 | tf_op jit(solution)/shard_map/all_to_all | solution.py:416
  10.2 7.0 %collective-permute-start.2 = (bf16[32,1152]{1,0:T(8,128)(2,1)S(1)}, bf16[32,1152]{1,0:T(8,128)(2,1)S(1)}, u32[]{:S(2)}, u32[]{:S(2)}) collective-permute-start(bf16[32,1152]{1,0:T(8,128)(2,1)S(1)} %pad_maximum_fusion.2), channel_id=1, source_target_pairs={{0,3},{1,0},{2,1},{3,2},{4,7},{5,4},{6,5},{7,6},{8,11},{9,8},{10,9... | collective-permute-start | bytes 221192 | tf_op jit(solution)/shard_map/ppermute | solution.py:435
  14.1 5.2 %collective-permute-start.1 = (bf16[32,1152]{1,0:T(8,128)(2,1)S(1)}, bf16[32,1152]{1,0:T(8,128)(2,1)S(1)}, u32[]{:S(2)}, u32[]{:S(2)}) collective-permute-start(bf16[32,1152]{1,0:T(8,128)(2,1)S(1)} %pad_maximum_fusion.2), channel_id=1, source_target_pairs={{0,2},{1,3},{2,0},{3,1},{4,6},{5,7},{6,4},{7,5},{8,10},{9,11},{10,... | collective-permute-start | bytes 221192 | tf_op jit(solution)/shard_map/ppermute | solution.py:435
  14.1 6.8 %collective-permute-start = (bf16[32,1152]{1,0:T(8,128)(2,1)S(1)}, bf16[32,1152]{1,0:T(8,128)(2,1)S(1)}, u32[]{:S(2)}, u32[]{:S(2)}) collective-permute-start(bf16[32,1152]{1,0:T(8,128)(2,1)S(1)} %pad_maximum_fusion.2), channel_id=1, source_target_pairs={{0,1},{1,2},{2,3},{3,0},{4,5},{5,6},{6,7},{7,4},{8,9},{9,10},{10,1... | collective-permute-start | bytes 221192 | tf_op jit(solution)/shard_map/ppermute | solution.py:435
  21.0 9.5 %collective-permute-start.4 = (bf16[4,32,1152]{2,1,0:T(8,128)(2,1)S(1)}, bf16[4,32,1152]{2,1,0:T(8,128)(2,1)S(1)}, u32[]{:S(2)}, u32[]{:S(2)}) collective-permute-start(bf16[4,32,1152]{2,1,0:T(8,128)(2,1)S(1)} %get-tuple-element.14), channel_id=1, source_target_pairs={{0,8},{1,9},{2,10},{3,11},{4,12},{5,13},{6,14},{7,15},{8,0},{9,1},... | collective-permute-start | bytes 884744 | tf_op jit(solution)/shard_map/ppermute | solution.py:435
  23.8 14.1 %collective-permute-start.3 = (bf16[4,32,1152]{2,1,0:T(8,128)(2,1)S(1)}, bf16[4,32,1152]{2,1,0:T(8,128)(2,1)S(1)}, u32[]{:S(2)}, u32[]{:S(2)}) collective-permute-start(bf16[4,32,1152]{2,1,0:T(8,128)(2,1)S(1)} %get-tuple-element.14), channel_id=1, source_target_pairs={{0,4},{1,5},{2,6},{3,7},{4,8},{5,9},{6,10},{7,11},{8,12},{9,13},{1... | collective-permute-start | bytes 884744 | tf_op jit(solution)/shard_map/ppermute | solution.py:435
  24.1 13.8 %collective-permute-start.5 = (bf16[4,32,1152]{2,1,0:T(8,128)(2,1)S(1)}, bf16[4,32,1152]{2,1,0:T(8,128)(2,1)S(1)}, u32[]{:S(2)}, u32[]{:S(2)}) collective-permute-start(bf16[4,32,1152]{2,1,0:T(8,128)(2,1)S(1)} %get-tuple-element.14), channel_id=1, source_target_pairs={{0,12},{1,13},{2,14},{3,15},{4,0},{5,1},{6,2},{7,3},{8,4},{9,5},{1... | collective-permute-start | bytes 884744 | tf_op jit(solution)/shard_map/ppermute | solution.py:435
  54.5 24.0 %all-to-all-start.1 = ((bf16[16,272,128]{2,1,0:T(8,128)(2,1)}), bf16[16,272,128]{2,1,0:T(8,128)(2,1)S(1)}, u32[]{:S(2)}, u32[]{:S(2)}) async-start(bf16[16,272,128]{2,1,0:T(8,128)(2,1)} %attend.1), calls=%async_computation.1 | async-start | bytes 2228224 | tf_op jit(solution)/shard_map/all_to_all | solution.py:448
  79.7 6.6 %collective-permute-start.8 = (bf16[32,1024]{1,0:T(8,128)(2,1)S(1)}, bf16[32,1024]{1,0:T(8,128)(2,1)S(1)}, u32[]{:S(2)}, u32[]{:S(2)}) collective-permute-start(bf16[32,1024]{1,0:T(8,128)(2,1)S(1)} %finish.1.refs_0_), channel_id=1, source_target_pairs={{0,64},{16,80},{32,96},{48,112},{64,0},{80,16},{96,32},{112,48},{1... | collective-permute-start | bytes 196616 | tf_op jit(solution)/shard_map/ppermute | solution.py:459
  80.4 8.5 %collective-permute-start.7 = (bf16[32,1024]{1,0:T(8,128)(2,1)S(1)}, bf16[32,1024]{1,0:T(8,128)(2,1)S(1)}, u32[]{:S(2)}, u32[]{:S(2)}) collective-permute-start(bf16[32,1024]{1,0:T(8,128)(2,1)S(1)} %finish.1.refs_0_), channel_id=1, source_target_pairs={{0,96},{16,112},{32,0},{48,16},{64,32},{80,48},{96,64},{112,80},{1... | collective-permute-start | bytes 196616 | tf_op jit(solution)/shard_map/ppermute | solution.py:459
  82.5 6.4 %collective-permute-start.6 = (bf16[32,1024]{1,0:T(8,128)(2,1)S(1)}, bf16[32,1024]{1,0:T(8,128)(2,1)S(1)}, u32[]{:S(2)}, u32[]{:S(2)}) collective-permute-start(bf16[32,1024]{1,0:T(8,128)(2,1)S(1)} %finish.1.refs_0_), channel_id=1, source_target_pairs={{0,32},{16,48},{32,64},{48,80},{64,96},{80,112},{96,0},{112,16},{1... | collective-permute-start | bytes 196616 | tf_op jit(solution)/shard_map/ppermute | solution.py:459
  82.5 9.3 %collective-permute-start.9 = (bf16[32,1024]{1,0:T(8,128)(2,1)S(1)}, bf16[32,1024]{1,0:T(8,128)(2,1)S(1)}, u32[]{:S(2)}, u32[]{:S(2)}) collective-permute-start(bf16[32,1024]{1,0:T(8,128)(2,1)S(1)} %finish.1.refs_0_), channel_id=1, source_target_pairs={{0,16},{16,0},{32,48},{48,32},{64,80},{80,64},{96,112},{112,96},{1... | collective-permute-start | bytes 196616 | tf_op jit(solution)/shard_map/ppermute | solution.py:459
  86.4 5.5 %collective-permute-start.12 = (bf16[32,1024]{1,0:T(8,128)(2,1)S(1)}, bf16[32,1024]{1,0:T(8,128)(2,1)S(1)}, u32[]{:S(2)}, u32[]{:S(2)}) collective-permute-start(bf16[32,1024]{1,0:T(8,128)(2,1)S(1)} %collective-permute-done.8.refs_3_), channel_id=1, source_target_pairs={{0,16},{16,0},{32,48},{48,32},{64,80},{80,64},{96,112},{112,96},{1... | collective-permute-start | bytes 196616 | tf_op jit(solution)/shard_map/ppermute | solution.py:459
  88.9 2.9 %collective-permute-start.11 = (bf16[32,1024]{1,0:T(8,128)(2,1)S(1)}, bf16[32,1024]{1,0:T(8,128)(2,1)S(1)}, u32[]{:S(2)}, u32[]{:S(2)}) collective-permute-start(bf16[32,1024]{1,0:T(8,128)(2,1)S(1)} %collective-permute-done.7.refs_2_), channel_id=1, source_target_pairs={{0,16},{16,0},{32,48},{48,32},{64,80},{80,64},{96,112},{112,96},{1... | collective-permute-start | bytes 196616 | tf_op jit(solution)/shard_map/ppermute | solution.py:459
  88.9 3.8 %collective-permute-start.10 = (bf16[32,1024]{1,0:T(8,128)(2,1)S(1)}, bf16[32,1024]{1,0:T(8,128)(2,1)S(1)}, u32[]{:S(2)}, u32[]{:S(2)}) collective-permute-start(bf16[32,1024]{1,0:T(8,128)(2,1)S(1)} %collective-permute-done.6.refs_1_), channel_id=1, source_target_pairs={{0,16},{16,0},{32,48},{48,32},{64,80},{80,64},{96,112},{112,96},{1... | collective-permute-start | bytes 196616 | tf_op jit(solution)/shard_map/ppermute | solution.py:459

commit v5 on v4

--- a/solution.py
+++ b/solution.py
@@ -301,7 +301,7 @@
     chips = len(heads) // 2
     for which in range(2):
         core = lax.rem(node[0] + which, 2)
-        for hop, ref in zip((0, 1, 3, 2), heads[which * chips : (which + 1) * chips]):
+        for hop, ref in zip((0, 3, 1, 2), heads[which * chips : (which + 1) * chips]):
             chip = lax.rem(node[0] // 2 - hop + chips, chips)
             start = pl.multiple_of((chip * 2 + core) * WIDTH, WIDTH)
             out[:, pl.ds(start, WIDTH)] = ref[...]
@@ -461,7 +461,7 @@
     def along(hop):
         return lambda i: (i + 2 * hop) % nodes
 
-    mine = [done] + [from_node(done, along(hop)) for hop in (1, 3, 2)]
+    mine = [done] + [from_node(done, along(hop)) for hop in (3, 1, 2)]
     other = [from_node(value, lambda i: i ^ 1) for value in mine]
     return place_heads(node, mine, other)
 

time: 94.1 us -> 92.4 us (0.982)
  starting transfers between devices: 36 us -> 33.8 us
    ppermute x7, starting transfers between devices: 12.1 us -> 9.85 us  [from_node(): return lax.ppermute(value, 'node', [(i, to(i)) for i in range(nodes)])]
  transfers between devices with their start and end apart: 15 -> 15, of which waited for: 8 -> 10; matrix products, arithmetic and copies ran while one was open for 4% -> 4% of each run, Pallas kernels for 3% -> 3%
where the time goes in v5:
time: 92.4 us; the launch traced here: 92.2 us
  waiting for transfers between devices  38.2 us (41%)
  starting transfers between devices  33.8 us (37%)
  Pallas kernels  16.2 us (18%)
  local copies, waits for them, and re-layouts  3.44 us (4%)
    ppermute x6, waiting for transfers between devices, shifted(): return lax.ppermute(value, 'group', pairs)  17.5 us
    all_to_all x1, waiting for transfers between devices, per_device(): lax.all_to_all(partial, 'group', split_axis=0, concat_axis=0, tiled=True)  15.3 us
    ppermute x6, starting transfers between devices, shifted(): return lax.ppermute(value, 'group', pairs)  10 us
    ppermute x7, starting transfers between devices, from_node(): return lax.ppermute(value, 'node', [(i, to(i)) for i in range(nodes)])  9.85 us
    all_to_all x1, starting transfers between devices, per_device(): lax.all_to_all(partial, 'group', split_axis=0, concat_axis=0, tiled=True)  7.97 us
    pallas_call x1, Pallas kernels, attend(): pl.pallas_call(attend_kernel, out_shape=jax.ShapeDtypeStruct((sources, OU...  7.29 us
    all_to_all x1, starting transfers between devices, per_device(): kv = lax.all_to_all(sent, 'node', split_axis=0, concat_axis=0, tiled=True)  5.98 us
    all_to_all x1, waiting for transfers between devices, per_device(): kv = lax.all_to_all(sent, 'node', split_axis=0, concat_axis=0, tiled=True)  4.1 us
  transfers between devices with their start and end apart: 15, of which 10 were waited for; matrix products, arithmetic and copies ran while one was open for 4% of the time, Pallas kernels for 3%

profile of v5, /device:TPU:1, one launch (start us, length us, event | category | flops | bytes accessed | tf_op | source)
XLA Modules:
  0.0 92.2 jit_solution(14587840051401214425)
XLA Ops:
  0.0 4.0 %pack.1 = bf16[8,768,256]{2,1,0:T(8,128)(2,1)} custom-call(s32[48]{0:T(128)} %fill.1, bf16[768,2048]{1,0:T(8,128)(2,1)} %bitcast.18), custom_call_target="tpu_custom_call" | custom-call | tf_op jit(solution)/shard_map/pack/pallas_call | solution.py:80
  4.0 6.0 %all-to-all-start = ((bf16[8,768,256]{2,1,0:T(8,128)(2,1)}), bf16[8,768,256]{2,1,0:T(8,128)(2,1)}, u32[]{:S(2)}, u32[]{:S(2)}) async-start(bf16[8,768,256]{2,1,0:T(8,128)(2,1)} %pack.1), calls=%async_computation | async-start | bytes 6291456 | tf_op jit(solution)/shard_map/all_to_all | solution.py:416
  10.2 3.8 %collective-permute-start.2 = (bf16[32,1152]{1,0:T(8,128)(2,1)S(1)}, bf16[32,1152]{1,0:T(8,128)(2,1)S(1)}, u32[]{:S(2)}, u32[]{:S(2)}) collective-permute-start(bf16[32,1152]{1,0:T(8,128)(2,1)S(1)} %pad_maximum_fusion.2), channel_id=1, source_target_pairs={{0,3},{1,0},{2,1},{3,2},{4,7},{5,4},{6,5},{7,6},{8,11},{9,8},{10,9... | collective-permute-start | bytes 221192 | tf_op jit(solution)/shard_map/ppermute | solution.py:435
  14.1 0.7 collective-permute-start
  14.8 2.4 %collective-permute-done.2 = bf16[32,1152]{1,0:T(8,128)(2,1)S(1)} collective-permute-done((bf16[32,1152]{1,0:T(8,128)(2,1)S(1)}, bf16[32,1152]{1,0:T(8,128)(2,1)S(1)}, u32[]{:S(2)}, u32[]{:S(2)}) %collective-permute-start.2) | collective-permute-done | bytes 73760 | tf_op jit(solution)/shard_map/ppermute | solution.py:435
  17.2 2.0 %collective-permute-done.1 = bf16[32,1152]{1,0:T(8,128)(2,1)S(1)} collective-permute-done((bf16[32,1152]{1,0:T(8,128)(2,1)S(1)}, bf16[32,1152]{1,0:T(8,128)(2,1)S(1)}, u32[]{:S(2)}, u32[]{:S(2)}) %collective-permute-start.1) | collective-permute-done | bytes 73760 | tf_op jit(solution)/shard_map/ppermute | solution.py:435
  19.2 1.7 %collective-permute-done = bf16[32,1152]{1,0:T(8,128)(2,1)S(1)} collective-permute-done((bf16[32,1152]{1,0:T(8,128)(2,1)S(1)}, bf16[32,1152]{1,0:T(8,128)(2,1)S(1)}, u32[]{:S(2)}, u32[]{:S(2)}) %collective-permute-start) | collective-permute-done | bytes 73760 | tf_op jit(solution)/shard_map/ppermute | solution.py:435
  21.0 2.8 %collective-permute-start.4 = (bf16[4,32,1152]{2,1,0:T(8,128)(2,1)S(1)}, bf16[4,32,1152]{2,1,0:T(8,128)(2,1)S(1)}, u32[]{:S(2)}, u32[]{:S(2)}) collective-permute-start(bf16[4,32,1152]{2,1,0:T(8,128)(2,1)S(1)} %get-tuple-element.14), channel_id=1, source_target_pairs={{0,8},{1,9},{2,10},{3,11},{4,12},{5,13},{6,14},{7,15},{8,0},{9,1},... | collective-permute-start | bytes 884744 | tf_op jit(solution)/shard_map/ppermute | solution.py:435
  23.8 0.3 collective-permute-start.3
  24.1 2.4 %collective-permute-start.5 = (bf16[4,32,1152]{2,1,0:T(8,128)(2,1)S(1)}, bf16[4,32,1152]{2,1,0:T(8,128)(2,1)S(1)}, u32[]{:S(2)}, u32[]{:S(2)}) collective-permute-start(bf16[4,32,1152]{2,1,0:T(8,128)(2,1)S(1)} %get-tuple-element.14), channel_id=1, source_target_pairs={{0,12},{1,13},{2,14},{3,15},{4,0},{5,1},{6,2},{7,3},{8,4},{9,5},{1... | collective-permute-start | bytes 884744 | tf_op jit(solution)/shard_map/ppermute | solution.py:435
  26.5 4.0 %collective-permute-done.4 = bf16[4,32,1152]{2,1,0:T(8,128)(2,1)S(1)} collective-permute-done((bf16[4,32,1152]{2,1,0:T(8,128)(2,1)S(1)}, bf16[4,32,1152]{2,1,0:T(8,128)(2,1)S(1)}, u32[]{:S(2)}, u32[]{:S(2)}) %collective-permute-start.4) | collective-permute-done | bytes 294944 | tf_op jit(solution)/shard_map/ppermute | solution.py:435
  30.5 7.4 %collective-permute-done.3 = bf16[4,32,1152]{2,1,0:T(8,128)(2,1)S(1)} collective-permute-done((bf16[4,32,1152]{2,1,0:T(8,128)(2,1)S(1)}, bf16[4,32,1152]{2,1,0:T(8,128)(2,1)S(1)}, u32[]{:S(2)}, u32[]{:S(2)}) %collective-permute-start.3) | collective-permute-done | bytes 294944 | tf_op jit(solution)/shard_map/ppermute | solution.py:435
  37.9 0.2 pad_maximum_fusion
  38.1 1.1 %slice.27 = bf16[16,32,1024]{2,1,0:T(8,128)(2,1)} slice(bf16[16,32,1152]{2,1,0:T(8,128)(2,1)S(1)} %bitcast.17), slice={[0:16], [0:32], [0:1024]} | slice | bytes 2097152 | tf_op jit(solution)/shard_map/slice | solution.py:440
  39.2 1.5 %reshape.31.query = bf16[4096,128]{1,0:T(8,128)(2,1)S(1)} reshape(bf16[16,32,1024]{2,1,0:T(8,128)(2,1)} %slice.27) | data formatting | bytes 2097152 | tf_op jit(solution)/shard_map/reshape | solution.py:440
  40.8 2.8 %visits.1 = (s32[8,384]{1,0:T(8,128)S(1)}, s32[8,128]{1,0:T(8,128)S(1)}, f32[1536,128]{1,0:T(8,128)S(1)}) custom-call(s32[1]{0:T(128)} %bitcast.1.column.group, bf16[512,128]{1,0:T(8,128)(2,1)S(1)} %bitcast.15, s32[8,128]{1,0:T(8,128)S(1)} %pad.9.root), custom_call_target="tpu_custom_call" | custom-call | flops 100000000 | bytes 2097152 | tf_op jit(solution)/shard_map/visits/pallas_call | solution.py:390
  43.6 4.1 %all-to-all-done = bf16[8,768,256]{2,1,0:T(8,128)(2,1)} async-done(((bf16[8,768,256]{2,1,0:T(8,128)(2,1)}), bf16[8,768,256]{2,1,0:T(8,128)(2,1)}, u32[]{:S(2)}, u32[]{:S(2)}) %all-to-all-start) | async-done | bytes 3145760 | tf_op jit(solution)/shard_map/all_to_all | solution.py:416
  47.7 7.3 %attend.1 = bf16[16,272,128]{2,1,0:T(8,128)(2,1)} custom-call(s32[8,384]{1,0:T(8,128)S(1)} %get-tuple-element.10.codes, s32[8,128]{1,0:T(8,128)S(1)} %get-tuple-element.11.counts, s32[1]{0:T(128)} %bitcast.1.column.group, bf16[6144,256]{1,0:T(8,128)(2,1)} %bitcast.13.kv, bf16[4096,128]{1,0:T(8,128)(2,1)S(1)} %reshape.31.query, ...), custom_call_target="tpu_custom_call" | custom-call | flops 2147483648 | bytes 6291456 | tf_op jit(solution)/shard_map/attend/pallas_call | solution.py:218
  55.0 8.0 %all-to-all-start.1 = ((bf16[16,272,128]{2,1,0:T(8,128)(2,1)}), bf16[16,272,128]{2,1,0:T(8,128)(2,1)S(1)}, u32[]{:S(2)}, u32[]{:S(2)}) async-start(bf16[16,272,128]{2,1,0:T(8,128)(2,1)} %attend.1), calls=%async_computation.1 | async-start | bytes 2228224 | tf_op jit(solution)/shard_map/all_to_all | solution.py:448
  63.0 0.7 constant_dynamic-slice_fusion.1
  63.7 15.3 %all-to-all-done.1.parts = bf16[16,272,128]{2,1,0:T(8,128)(2,1)S(1)} async-done(((bf16[16,272,128]{2,1,0:T(8,128)(2,1)}), bf16[16,272,128]{2,1,0:T(8,128)(2,1)S(1)}, u32[]{:S(2)}, u32[]{:S(2)}) %all-to-all-start.1) | async-done | bytes 1114144 | tf_op jit(solution)/shard_map/all_to_all | solution.py:448
  79.0 1.3 %finish.1.refs_0_ = bf16[32,1024]{1,0:T(8,128)(2,1)S(1)} custom-call(bf16[16,272,128]{2,1,0:T(8,128)(2,1)S(1)} %all-to-all-done.1.parts, bf16[256,128]{1,0:T(8,128)(2,1)S(1)} %reshape.32.query, bf16[32,256]{1,0:T(8,128)(2,1)S(1)} %pad_maximum_fusion.3.entry), custom_call_target="tpu_custom_call" | custom-call | tf_op jit(solution)/shard_map/finish/pallas_call | solution.py:284
  80.3 0.6 collective-permute-start.8
  80.9 0.9 collective-permute-start.7
  81.8 1.8 %collective-permute-start.6 = (bf16[32,1024]{1,0:T(8,128)(2,1)S(1)}, bf16[32,1024]{1,0:T(8,128)(2,1)S(1)}, u32[]{:S(2)}, u32[]{:S(2)}) collective-permute-start(bf16[32,1024]{1,0:T(8,128)(2,1)S(1)} %finish.1.refs_0_), channel_id=1, source_target_pairs={{0,96},{16,112},{32,0},{48,16},{64,32},{80,48},{96,64},{112,80},{1... | collective-permute-start | bytes 196616 | tf_op jit(solution)/shard_map/ppermute | solution.py:459
  83.6 4.1 %collective-permute-start.9 = (bf16[32,1024]{1,0:T(8,128)(2,1)S(1)}, bf16[32,1024]{1,0:T(8,128)(2,1)S(1)}, u32[]{:S(2)}, u32[]{:S(2)}) collective-permute-start(bf16[32,1024]{1,0:T(8,128)(2,1)S(1)} %finish.1.refs_0_), channel_id=1, source_target_pairs={{0,16},{16,0},{32,48},{48,32},{64,80},{80,64},{96,112},{112,96},{1... | collective-permute-start | bytes 196616 | tf_op jit(solution)/shard_map/ppermute | solution.py:459
  87.7 1.7 %collective-permute-start.12 = (bf16[32,1024]{1,0:T(8,128)(2,1)S(1)}, bf16[32,1024]{1,0:T(8,128)(2,1)S(1)}, u32[]{:S(2)}, u32[]{:S(2)}) collective-permute-start(bf16[32,1024]{1,0:T(8,128)(2,1)S(1)} %collective-permute-done.8.refs_3_), channel_id=1, source_target_pairs={{0,16},{16,0},{32,48},{48,32},{64,80},{80,64},{96,112},{112,96},{1... | collective-permute-start | bytes 196616 | tf_op jit(solution)/shard_map/ppermute | solution.py:459
  89.4 0.7 collective-permute-start.11
  90.1 0.2 collective-permute-done.12.refs_7_
  90.3 0.7 collective-permute-done.11.refs_6_
  91.0 0.4 collective-permute-done.10.refs_5_
  91.4 0.8 place_heads.1
  (26 shorter events, 0.4 us)
Async XLA Ops:
  0.0 10.2 %copy-start = (bf16[32,8192]{1,0:T(8,128)(2,1)S(1)}, bf16[32,8192]{1,0:T(8,128)(2,1)}, u32[]{:S(2)}) copy-start(bf16[32,8192]{1,0:T(8,128)(2,1)} %param.6) | copy-start | bytes 1572868
  4.0 6.0 %copy-start.1 = (s32[32,64]{1,0:T(8,128)S(1)}, s32[32,64]{1,0:T(8,128)}, u32[]{:S(2)}) copy-start(s32[32,64]{1,0:T(8,128)} %param.8) | copy-start | bytes 24580
  4.0 6.0 %copy-start.2 = (s32[32]{0:T(128)S(1)}, s32[32]{0:T(128)}, u32[]{:S(2)}) copy-start(s32[32]{0:T(128)} %param.9) | copy-start | bytes 388
  4.0 43.7 %all-to-all-start = ((bf16[8,768,256]{2,1,0:T(8,128)(2,1)}), bf16[8,768,256]{2,1,0:T(8,128)(2,1)}, u32[]{:S(2)}, u32[]{:S(2)}) async-start(bf16[8,768,256]{2,1,0:T(8,128)(2,1)} %pack.1), calls=%async_computation | async-start | bytes 6291456 | tf_op jit(solution)/shard_map/all_to_all | solution.py:416
  10.2 7.0 %collective-permute-start.2 = (bf16[32,1152]{1,0:T(8,128)(2,1)S(1)}, bf16[32,1152]{1,0:T(8,128)(2,1)S(1)}, u32[]{:S(2)}, u32[]{:S(2)}) collective-permute-start(bf16[32,1152]{1,0:T(8,128)(2,1)S(1)} %pad_maximum_fusion.2), channel_id=1, source_target_pairs={{0,3},{1,0},{2,1},{3,2},{4,7},{5,4},{6,5},{7,6},{8,11},{9,8},{10,9... | collective-permute-start | bytes 221192 | tf_op jit(solution)/shard_map/ppermute | solution.py:435
  14.1 5.2 %collective-permute-start.1 = (bf16[32,1152]{1,0:T(8,128)(2,1)S(1)}, bf16[32,1152]{1,0:T(8,128)(2,1)S(1)}, u32[]{:S(2)}, u32[]{:S(2)}) collective-permute-start(bf16[32,1152]{1,0:T(8,128)(2,1)S(1)} %pad_maximum_fusion.2), channel_id=1, source_target_pairs={{0,2},{1,3},{2,0},{3,1},{4,6},{5,7},{6,4},{7,5},{8,10},{9,11},{10,... | collective-permute-start | bytes 221192 | tf_op jit(solution)/shard_map/ppermute | solution.py:435
  14.1 6.8 %collective-permute-start = (bf16[32,1152]{1,0:T(8,128)(2,1)S(1)}, bf16[32,1152]{1,0:T(8,128)(2,1)S(1)}, u32[]{:S(2)}, u32[]{:S(2)}) collective-permute-start(bf16[32,1152]{1,0:T(8,128)(2,1)S(1)} %pad_maximum_fusion.2), channel_id=1, source_target_pairs={{0,1},{1,2},{2,3},{3,0},{4,5},{5,6},{6,7},{7,4},{8,9},{9,10},{10,1... | collective-permute-start | bytes 221192 | tf_op jit(solution)/shard_map/ppermute | solution.py:435
  21.0 9.5 %collective-permute-start.4 = (bf16[4,32,1152]{2,1,0:T(8,128)(2,1)S(1)}, bf16[4,32,1152]{2,1,0:T(8,128)(2,1)S(1)}, u32[]{:S(2)}, u32[]{:S(2)}) collective-permute-start(bf16[4,32,1152]{2,1,0:T(8,128)(2,1)S(1)} %get-tuple-element.14), channel_id=1, source_target_pairs={{0,8},{1,9},{2,10},{3,11},{4,12},{5,13},{6,14},{7,15},{8,0},{9,1},... | collective-permute-start | bytes 884744 | tf_op jit(solution)/shard_map/ppermute | solution.py:435
  23.8 14.1 %collective-permute-start.3 = (bf16[4,32,1152]{2,1,0:T(8,128)(2,1)S(1)}, bf16[4,32,1152]{2,1,0:T(8,128)(2,1)S(1)}, u32[]{:S(2)}, u32[]{:S(2)}) collective-permute-start(bf16[4,32,1152]{2,1,0:T(8,128)(2,1)S(1)} %get-tuple-element.14), channel_id=1, source_target_pairs={{0,4},{1,5},{2,6},{3,7},{4,8},{5,9},{6,10},{7,11},{8,12},{9,13},{1... | collective-permute-start | bytes 884744 | tf_op jit(solution)/shard_map/ppermute | solution.py:435
  24.1 13.8 %collective-permute-start.5 = (bf16[4,32,1152]{2,1,0:T(8,128)(2,1)S(1)}, bf16[4,32,1152]{2,1,0:T(8,128)(2,1)S(1)}, u32[]{:S(2)}, u32[]{:S(2)}) collective-permute-start(bf16[4,32,1152]{2,1,0:T(8,128)(2,1)S(1)} %get-tuple-element.14), channel_id=1, source_target_pairs={{0,12},{1,13},{2,14},{3,15},{4,0},{5,1},{6,2},{7,3},{8,4},{9,5},{1... | collective-permute-start | bytes 884744 | tf_op jit(solution)/shard_map/ppermute | solution.py:435
  55.0 24.0 %all-to-all-start.1 = ((bf16[16,272,128]{2,1,0:T(8,128)(2,1)}), bf16[16,272,128]{2,1,0:T(8,128)(2,1)S(1)}, u32[]{:S(2)}, u32[]{:S(2)}) async-start(bf16[16,272,128]{2,1,0:T(8,128)(2,1)} %attend.1), calls=%async_computation.1 | async-start | bytes 2228224 | tf_op jit(solution)/shard_map/all_to_all | solution.py:448
  80.3 7.4 %collective-permute-start.8 = (bf16[32,1024]{1,0:T(8,128)(2,1)S(1)}, bf16[32,1024]{1,0:T(8,128)(2,1)S(1)}, u32[]{:S(2)}, u32[]{:S(2)}) collective-permute-start(bf16[32,1024]{1,0:T(8,128)(2,1)S(1)} %finish.1.refs_0_), channel_id=1, source_target_pairs={{0,64},{16,80},{32,96},{48,112},{64,0},{80,16},{96,32},{112,48},{1... | collective-permute-start | bytes 196616 | tf_op jit(solution)/shard_map/ppermute | solution.py:459
  80.9 8.5 %collective-permute-start.7 = (bf16[32,1024]{1,0:T(8,128)(2,1)S(1)}, bf16[32,1024]{1,0:T(8,128)(2,1)S(1)}, u32[]{:S(2)}, u32[]{:S(2)}) collective-permute-start(bf16[32,1024]{1,0:T(8,128)(2,1)S(1)} %finish.1.refs_0_), channel_id=1, source_target_pairs={{0,32},{16,48},{32,64},{48,80},{64,96},{80,112},{96,0},{112,16},{1... | collective-permute-start | bytes 196616 | tf_op jit(solution)/shard_map/ppermute | solution.py:459
  81.8 8.3 %collective-permute-start.6 = (bf16[32,1024]{1,0:T(8,128)(2,1)S(1)}, bf16[32,1024]{1,0:T(8,128)(2,1)S(1)}, u32[]{:S(2)}, u32[]{:S(2)}) collective-permute-start(bf16[32,1024]{1,0:T(8,128)(2,1)S(1)} %finish.1.refs_0_), channel_id=1, source_target_pairs={{0,96},{16,112},{32,0},{48,16},{64,32},{80,48},{96,64},{112,80},{1... | collective-permute-start | bytes 196616 | tf_op jit(solution)/shard_map/ppermute | solution.py:459
  83.6 6.6 %collective-permute-start.9 = (bf16[32,1024]{1,0:T(8,128)(2,1)S(1)}, bf16[32,1024]{1,0:T(8,128)(2,1)S(1)}, u32[]{:S(2)}, u32[]{:S(2)}) collective-permute-start(bf16[32,1024]{1,0:T(8,128)(2,1)S(1)} %finish.1.refs_0_), channel_id=1, source_target_pairs={{0,16},{16,0},{32,48},{48,32},{64,80},{80,64},{96,112},{112,96},{1... | collective-permute-start | bytes 196616 | tf_op jit(solution)/shard_map/ppermute | solution.py:459
  87.7 2.6 %collective-permute-start.12 = (bf16[32,1024]{1,0:T(8,128)(2,1)S(1)}, bf16[32,1024]{1,0:T(8,128)(2,1)S(1)}, u32[]{:S(2)}, u32[]{:S(2)}) collective-permute-start(bf16[32,1024]{1,0:T(8,128)(2,1)S(1)} %collective-permute-done.8.refs_3_), channel_id=1, source_target_pairs={{0,16},{16,0},{32,48},{48,32},{64,80},{80,64},{96,112},{112,96},{1... | collective-permute-start | bytes 196616 | tf_op jit(solution)/shard_map/ppermute | solution.py:459
  89.4 1.6 %collective-permute-start.11 = (bf16[32,1024]{1,0:T(8,128)(2,1)S(1)}, bf16[32,1024]{1,0:T(8,128)(2,1)S(1)}, u32[]{:S(2)}, u32[]{:S(2)}) collective-permute-start(bf16[32,1024]{1,0:T(8,128)(2,1)S(1)} %collective-permute-done.7.refs_2_), channel_id=1, source_target_pairs={{0,16},{16,0},{32,48},{48,32},{64,80},{80,64},{96,112},{112,96},{1... | collective-permute-start | bytes 196616 | tf_op jit(solution)/shard_map/ppermute | solution.py:459
  90.1 1.3 %collective-permute-start.10 = (bf16[32,1024]{1,0:T(8,128)(2,1)S(1)}, bf16[32,1024]{1,0:T(8,128)(2,1)S(1)}, u32[]{:S(2)}, u32[]{:S(2)}) collective-permute-start(bf16[32,1024]{1,0:T(8,128)(2,1)S(1)} %collective-permute-done.6.refs_1_), channel_id=1, source_target_pairs={{0,16},{16,0},{32,48},{48,32},{64,80},{80,64},{96,112},{112,96},{1... | collective-permute-start | bytes 196616 | tf_op jit(solution)/shard_map/ppermute | solution.py:459

commit v6 on v5

--- a/solution.py
+++ b/solution.py
@@ -434,8 +434,10 @@
         ]
         return lax.ppermute(value, "group", pairs)
 
-    line = jnp.stack([told] + [shifted(told, 0, hop) for hop in range(1, side)])
-    told = jnp.stack([line] + [shifted(line, hop, 0) for hop in range(1, side)])
+    along_z = {hop: shifted(told, 0, hop) for hop in (3, 1, 2)}
+    line = jnp.stack([told] + [along_z[hop] for hop in range(1, side)])
+    along_x = {hop: shifted(line, hop, 0) for hop in (3, 1, 2)}
+    told = jnp.stack([line] + [along_x[hop] for hop in range(1, side)])
     told = told.reshape((groups,) + told.shape[2:])
     all_query = told[:, :, :WIDTH].reshape(groups * own_rows * GROUP, HEAD_DIM)
     coded = told[:, :, WIDTH:].reshape(groups * own_rows, HEAD_DIM)

time: 92.4 us -> 92.1 us (level)
  no operation moved by 1% of the time
where the time goes in v6:
time: 92.1 us; the launch traced here: 91.8 us
  waiting for transfers between devices  38.2 us (41%)
  starting transfers between devices  33.7 us (37%)
  Pallas kernels  15.9 us (17%)
  local copies, waits for them, and re-layouts  3.44 us (4%)
    ppermute x6, waiting for transfers between devices, shifted(): return lax.ppermute(value, 'group', pairs)  17.5 us
    all_to_all x1, waiting for transfers between devices, per_device(): lax.all_to_all(partial, 'group', split_axis=0, concat_axis=0, tiled=True)  15.3 us
    ppermute x6, starting transfers between devices, shifted(): return lax.ppermute(value, 'group', pairs)  10 us
    ppermute x7, starting transfers between devices, from_node(): return lax.ppermute(value, 'node', [(i, to(i)) for i in range(nodes)])  9.86 us
    all_to_all x1, starting transfers between devices, per_device(): lax.all_to_all(partial, 'group', split_axis=0, concat_axis=0, tiled=True)  7.82 us
    pallas_call x1, Pallas kernels, attend(): pl.pallas_call(attend_kernel, out_shape=jax.ShapeDtypeStruct((sources, OU...  7.05 us
    all_to_all x1, starting transfers between devices, per_device(): kv = lax.all_to_all(sent, 'node', split_axis=0, concat_axis=0, tiled=True)  5.98 us
    all_to_all x1, waiting for transfers between devices, per_device(): kv = lax.all_to_all(sent, 'node', split_axis=0, concat_axis=0, tiled=True)  4.1 us
  transfers between devices with their start and end apart: 15, of which 10 were waited for; matrix products, arithmetic and copies ran while one was open for 4% of the time, Pallas kernels for 3%

profile of v6, /device:TPU:1, one launch (start us, length us, event | category | flops | bytes accessed | tf_op | source)
XLA Modules:
  0.0 91.8 jit_solution(14587840051401214425)
XLA Ops:
  0.0 4.0 %pack.1 = bf16[8,768,256]{2,1,0:T(8,128)(2,1)} custom-call(s32[48]{0:T(128)} %fill.1, bf16[768,2048]{1,0:T(8,128)(2,1)} %bitcast.18), custom_call_target="tpu_custom_call" | custom-call | tf_op jit(solution)/shard_map/pack/pallas_call | solution.py:80
  4.0 6.0 %all-to-all-start = ((bf16[8,768,256]{2,1,0:T(8,128)(2,1)}), bf16[8,768,256]{2,1,0:T(8,128)(2,1)}, u32[]{:S(2)}, u32[]{:S(2)}) async-start(bf16[8,768,256]{2,1,0:T(8,128)(2,1)} %pack.1), calls=%async_computation | async-start | bytes 6291456 | tf_op jit(solution)/shard_map/all_to_all | solution.py:416
  10.2 3.8 %collective-permute-start.2 = (bf16[32,1152]{1,0:T(8,128)(2,1)S(1)}, bf16[32,1152]{1,0:T(8,128)(2,1)S(1)}, u32[]{:S(2)}, u32[]{:S(2)}) collective-permute-start(bf16[32,1152]{1,0:T(8,128)(2,1)S(1)} %pad_maximum_fusion.2), channel_id=1, source_target_pairs={{0,3},{1,0},{2,1},{3,2},{4,7},{5,4},{6,5},{7,6},{8,11},{9,8},{10,9... | collective-permute-start | bytes 221192 | tf_op jit(solution)/shard_map/ppermute | solution.py:435
  14.1 0.7 collective-permute-start
  14.8 2.4 %collective-permute-done.2 = bf16[32,1152]{1,0:T(8,128)(2,1)S(1)} collective-permute-done((bf16[32,1152]{1,0:T(8,128)(2,1)S(1)}, bf16[32,1152]{1,0:T(8,128)(2,1)S(1)}, u32[]{:S(2)}, u32[]{:S(2)}) %collective-permute-start.2) | collective-permute-done | bytes 73760 | tf_op jit(solution)/shard_map/ppermute | solution.py:435
  17.2 2.0 %collective-permute-done.1 = bf16[32,1152]{1,0:T(8,128)(2,1)S(1)} collective-permute-done((bf16[32,1152]{1,0:T(8,128)(2,1)S(1)}, bf16[32,1152]{1,0:T(8,128)(2,1)S(1)}, u32[]{:S(2)}, u32[]{:S(2)}) %collective-permute-start.1) | collective-permute-done | bytes 73760 | tf_op jit(solution)/shard_map/ppermute | solution.py:435
  19.2 1.7 %collective-permute-done = bf16[32,1152]{1,0:T(8,128)(2,1)S(1)} collective-permute-done((bf16[32,1152]{1,0:T(8,128)(2,1)S(1)}, bf16[32,1152]{1,0:T(8,128)(2,1)S(1)}, u32[]{:S(2)}, u32[]{:S(2)}) %collective-permute-start) | collective-permute-done | bytes 73760 | tf_op jit(solution)/shard_map/ppermute | solution.py:435
  21.0 2.8 %collective-permute-start.4 = (bf16[4,32,1152]{2,1,0:T(8,128)(2,1)S(1)}, bf16[4,32,1152]{2,1,0:T(8,128)(2,1)S(1)}, u32[]{:S(2)}, u32[]{:S(2)}) collective-permute-start(bf16[4,32,1152]{2,1,0:T(8,128)(2,1)S(1)} %get-tuple-element.14), channel_id=1, source_target_pairs={{0,8},{1,9},{2,10},{3,11},{4,12},{5,13},{6,14},{7,15},{8,0},{9,1},... | collective-permute-start | bytes 884744 | tf_op jit(solution)/shard_map/ppermute | solution.py:435
  23.8 0.3 collective-permute-start.3
  24.1 2.4 %collective-permute-start.5 = (bf16[4,32,1152]{2,1,0:T(8,128)(2,1)S(1)}, bf16[4,32,1152]{2,1,0:T(8,128)(2,1)S(1)}, u32[]{:S(2)}, u32[]{:S(2)}) collective-permute-start(bf16[4,32,1152]{2,1,0:T(8,128)(2,1)S(1)} %get-tuple-element.14), channel_id=1, source_target_pairs={{0,12},{1,13},{2,14},{3,15},{4,0},{5,1},{6,2},{7,3},{8,4},{9,5},{1... | collective-permute-start | bytes 884744 | tf_op jit(solution)/shard_map/ppermute | solution.py:435
  26.5 4.0 %collective-permute-done.4 = bf16[4,32,1152]{2,1,0:T(8,128)(2,1)S(1)} collective-permute-done((bf16[4,32,1152]{2,1,0:T(8,128)(2,1)S(1)}, bf16[4,32,1152]{2,1,0:T(8,128)(2,1)S(1)}, u32[]{:S(2)}, u32[]{:S(2)}) %collective-permute-start.4) | collective-permute-done | bytes 294944 | tf_op jit(solution)/shard_map/ppermute | solution.py:435
  30.5 7.4 %collective-permute-done.3 = bf16[4,32,1152]{2,1,0:T(8,128)(2,1)S(1)} collective-permute-done((bf16[4,32,1152]{2,1,0:T(8,128)(2,1)S(1)}, bf16[4,32,1152]{2,1,0:T(8,128)(2,1)S(1)}, u32[]{:S(2)}, u32[]{:S(2)}) %collective-permute-start.3) | collective-permute-done | bytes 294944 | tf_op jit(solution)/shard_map/ppermute | solution.py:435
  37.9 0.2 pad_maximum_fusion
  38.1 1.1 %slice.27 = bf16[16,32,1024]{2,1,0:T(8,128)(2,1)} slice(bf16[16,32,1152]{2,1,0:T(8,128)(2,1)S(1)} %bitcast.17), slice={[0:16], [0:32], [0:1024]} | slice | bytes 2097152 | tf_op jit(solution)/shard_map/slice | solution.py:442
  39.2 1.5 %reshape.31.query = bf16[4096,128]{1,0:T(8,128)(2,1)S(1)} reshape(bf16[16,32,1024]{2,1,0:T(8,128)(2,1)} %slice.27) | data formatting | bytes 2097152 | tf_op jit(solution)/shard_map/reshape | solution.py:442
  40.8 2.8 %visits.1 = (s32[8,384]{1,0:T(8,128)S(1)}, s32[8,128]{1,0:T(8,128)S(1)}, f32[1536,128]{1,0:T(8,128)S(1)}) custom-call(s32[1]{0:T(128)} %bitcast.1.column.group, bf16[512,128]{1,0:T(8,128)(2,1)S(1)} %bitcast.15, s32[8,128]{1,0:T(8,128)S(1)} %pad.9.root), custom_call_target="tpu_custom_call" | custom-call | flops 100000000 | bytes 2097152 | tf_op jit(solution)/shard_map/visits/pallas_call | solution.py:390
  43.6 4.1 %all-to-all-done = bf16[8,768,256]{2,1,0:T(8,128)(2,1)} async-done(((bf16[8,768,256]{2,1,0:T(8,128)(2,1)}), bf16[8,768,256]{2,1,0:T(8,128)(2,1)}, u32[]{:S(2)}, u32[]{:S(2)}) %all-to-all-start) | async-done | bytes 3145760 | tf_op jit(solution)/shard_map/all_to_all | solution.py:416
  47.7 7.1 %attend.1 = bf16[16,272,128]{2,1,0:T(8,128)(2,1)} custom-call(s32[8,384]{1,0:T(8,128)S(1)} %get-tuple-element.10.codes, s32[8,128]{1,0:T(8,128)S(1)} %get-tuple-element.11.counts, s32[1]{0:T(128)} %bitcast.1.column.group, bf16[6144,256]{1,0:T(8,128)(2,1)} %bitcast.13.kv, bf16[4096,128]{1,0:T(8,128)(2,1)S(1)} %reshape.31.query, ...), custom_call_target="tpu_custom_call" | custom-call | flops 2147483648 | bytes 6291456 | tf_op jit(solution)/shard_map/attend/pallas_call | solution.py:218
  54.7 7.8 %all-to-all-start.1 = ((bf16[16,272,128]{2,1,0:T(8,128)(2,1)}), bf16[16,272,128]{2,1,0:T(8,128)(2,1)S(1)}, u32[]{:S(2)}, u32[]{:S(2)}) async-start(bf16[16,272,128]{2,1,0:T(8,128)(2,1)} %attend.1), calls=%async_computation.1 | async-start | bytes 2228224 | tf_op jit(solution)/shard_map/all_to_all | solution.py:450
  62.6 0.7 constant_dynamic-slice_fusion.1
  63.3 15.3 %all-to-all-done.1.parts = bf16[16,272,128]{2,1,0:T(8,128)(2,1)S(1)} async-done(((bf16[16,272,128]{2,1,0:T(8,128)(2,1)}), bf16[16,272,128]{2,1,0:T(8,128)(2,1)S(1)}, u32[]{:S(2)}, u32[]{:S(2)}) %all-to-all-start.1) | async-done | bytes 1114144 | tf_op jit(solution)/shard_map/all_to_all | solution.py:450
  78.6 1.3 %finish.1.refs_0_ = bf16[32,1024]{1,0:T(8,128)(2,1)S(1)} custom-call(bf16[16,272,128]{2,1,0:T(8,128)(2,1)S(1)} %all-to-all-done.1.parts, bf16[256,128]{1,0:T(8,128)(2,1)S(1)} %reshape.32.query, bf16[32,256]{1,0:T(8,128)(2,1)S(1)} %pad_maximum_fusion.3.entry), custom_call_target="tpu_custom_call" | custom-call | tf_op jit(solution)/shard_map/finish/pallas_call | solution.py:284
  79.9 0.6 collective-permute-start.8
  80.5 0.9 collective-permute-start.7
  81.4 1.8 %collective-permute-start.6 = (bf16[32,1024]{1,0:T(8,128)(2,1)S(1)}, bf16[32,1024]{1,0:T(8,128)(2,1)S(1)}, u32[]{:S(2)}, u32[]{:S(2)}) collective-permute-start(bf16[32,1024]{1,0:T(8,128)(2,1)S(1)} %finish.1.refs_0_), channel_id=1, source_target_pairs={{0,96},{16,112},{32,0},{48,16},{64,32},{80,48},{96,64},{112,80},{1... | collective-permute-start | bytes 196616 | tf_op jit(solution)/shard_map/ppermute | solution.py:461
  83.2 4.1 %collective-permute-start.9 = (bf16[32,1024]{1,0:T(8,128)(2,1)S(1)}, bf16[32,1024]{1,0:T(8,128)(2,1)S(1)}, u32[]{:S(2)}, u32[]{:S(2)}) collective-permute-start(bf16[32,1024]{1,0:T(8,128)(2,1)S(1)} %finish.1.refs_0_), channel_id=1, source_target_pairs={{0,16},{16,0},{32,48},{48,32},{64,80},{80,64},{96,112},{112,96},{1... | collective-permute-start | bytes 196616 | tf_op jit(solution)/shard_map/ppermute | solution.py:461
  87.3 1.7 %collective-permute-start.12 = (bf16[32,1024]{1,0:T(8,128)(2,1)S(1)}, bf16[32,1024]{1,0:T(8,128)(2,1)S(1)}, u32[]{:S(2)}, u32[]{:S(2)}) collective-permute-start(bf16[32,1024]{1,0:T(8,128)(2,1)S(1)} %collective-permute-done.8.refs_3_), channel_id=1, source_target_pairs={{0,16},{16,0},{32,48},{48,32},{64,80},{80,64},{96,112},{112,96},{1... | collective-permute-start | bytes 196616 | tf_op jit(solution)/shard_map/ppermute | solution.py:461
  89.0 0.7 collective-permute-start.11
  89.7 0.2 collective-permute-done.12.refs_7_
  89.9 0.7 collective-permute-done.11.refs_6_
  90.6 0.4 collective-permute-done.10.refs_5_
  91.0 0.8 place_heads.1
  (26 shorter events, 0.4 us)
Async XLA Ops:
  0.0 10.2 %copy-start = (bf16[32,8192]{1,0:T(8,128)(2,1)S(1)}, bf16[32,8192]{1,0:T(8,128)(2,1)}, u32[]{:S(2)}) copy-start(bf16[32,8192]{1,0:T(8,128)(2,1)} %param.6) | copy-start | bytes 1572868
  4.0 6.0 %copy-start.1 = (s32[32,64]{1,0:T(8,128)S(1)}, s32[32,64]{1,0:T(8,128)}, u32[]{:S(2)}) copy-start(s32[32,64]{1,0:T(8,128)} %param.8) | copy-start | bytes 24580
  4.0 6.0 %copy-start.2 = (s32[32]{0:T(128)S(1)}, s32[32]{0:T(128)}, u32[]{:S(2)}) copy-start(s32[32]{0:T(128)} %param.9) | copy-start | bytes 388
  4.0 43.7 %all-to-all-start = ((bf16[8,768,256]{2,1,0:T(8,128)(2,1)}), bf16[8,768,256]{2,1,0:T(8,128)(2,1)}, u32[]{:S(2)}, u32[]{:S(2)}) async-start(bf16[8,768,256]{2,1,0:T(8,128)(2,1)} %pack.1), calls=%async_computation | async-start | bytes 6291456 | tf_op jit(solution)/shard_map/all_to_all | solution.py:416
  10.2 7.0 %collective-permute-start.2 = (bf16[32,1152]{1,0:T(8,128)(2,1)S(1)}, bf16[32,1152]{1,0:T(8,128)(2,1)S(1)}, u32[]{:S(2)}, u32[]{:S(2)}) collective-permute-start(bf16[32,1152]{1,0:T(8,128)(2,1)S(1)} %pad_maximum_fusion.2), channel_id=1, source_target_pairs={{0,3},{1,0},{2,1},{3,2},{4,7},{5,4},{6,5},{7,6},{8,11},{9,8},{10,9... | collective-permute-start | bytes 221192 | tf_op jit(solution)/shard_map/ppermute | solution.py:435
  14.1 5.2 %collective-permute-start.1 = (bf16[32,1152]{1,0:T(8,128)(2,1)S(1)}, bf16[32,1152]{1,0:T(8,128)(2,1)S(1)}, u32[]{:S(2)}, u32[]{:S(2)}) collective-permute-start(bf16[32,1152]{1,0:T(8,128)(2,1)S(1)} %pad_maximum_fusion.2), channel_id=1, source_target_pairs={{0,2},{1,3},{2,0},{3,1},{4,6},{5,7},{6,4},{7,5},{8,10},{9,11},{10,... | collective-permute-start | bytes 221192 | tf_op jit(solution)/shard_map/ppermute | solution.py:435
  14.1 6.8 %collective-permute-start = (bf16[32,1152]{1,0:T(8,128)(2,1)S(1)}, bf16[32,1152]{1,0:T(8,128)(2,1)S(1)}, u32[]{:S(2)}, u32[]{:S(2)}) collective-permute-start(bf16[32,1152]{1,0:T(8,128)(2,1)S(1)} %pad_maximum_fusion.2), channel_id=1, source_target_pairs={{0,1},{1,2},{2,3},{3,0},{4,5},{5,6},{6,7},{7,4},{8,9},{9,10},{10,1... | collective-permute-start | bytes 221192 | tf_op jit(solution)/shard_map/ppermute | solution.py:435
  21.0 9.5 %collective-permute-start.4 = (bf16[4,32,1152]{2,1,0:T(8,128)(2,1)S(1)}, bf16[4,32,1152]{2,1,0:T(8,128)(2,1)S(1)}, u32[]{:S(2)}, u32[]{:S(2)}) collective-permute-start(bf16[4,32,1152]{2,1,0:T(8,128)(2,1)S(1)} %get-tuple-element.14), channel_id=1, source_target_pairs={{0,8},{1,9},{2,10},{3,11},{4,12},{5,13},{6,14},{7,15},{8,0},{9,1},... | collective-permute-start | bytes 884744 | tf_op jit(solution)/shard_map/ppermute | solution.py:435
  23.8 14.1 %collective-permute-start.3 = (bf16[4,32,1152]{2,1,0:T(8,128)(2,1)S(1)}, bf16[4,32,1152]{2,1,0:T(8,128)(2,1)S(1)}, u32[]{:S(2)}, u32[]{:S(2)}) collective-permute-start(bf16[4,32,1152]{2,1,0:T(8,128)(2,1)S(1)} %get-tuple-element.14), channel_id=1, source_target_pairs={{0,4},{1,5},{2,6},{3,7},{4,8},{5,9},{6,10},{7,11},{8,12},{9,13},{1... | collective-permute-start | bytes 884744 | tf_op jit(solution)/shard_map/ppermute | solution.py:435
  24.1 13.8 %collective-permute-start.5 = (bf16[4,32,1152]{2,1,0:T(8,128)(2,1)S(1)}, bf16[4,32,1152]{2,1,0:T(8,128)(2,1)S(1)}, u32[]{:S(2)}, u32[]{:S(2)}) collective-permute-start(bf16[4,32,1152]{2,1,0:T(8,128)(2,1)S(1)} %get-tuple-element.14), channel_id=1, source_target_pairs={{0,12},{1,13},{2,14},{3,15},{4,0},{5,1},{6,2},{7,3},{8,4},{9,5},{1... | collective-permute-start | bytes 884744 | tf_op jit(solution)/shard_map/ppermute | solution.py:435
  54.7 23.9 %all-to-all-start.1 = ((bf16[16,272,128]{2,1,0:T(8,128)(2,1)}), bf16[16,272,128]{2,1,0:T(8,128)(2,1)S(1)}, u32[]{:S(2)}, u32[]{:S(2)}) async-start(bf16[16,272,128]{2,1,0:T(8,128)(2,1)} %attend.1), calls=%async_computation.1 | async-start | bytes 2228224 | tf_op jit(solution)/shard_map/all_to_all | solution.py:450
  79.9 7.4 %collective-permute-start.8 = (bf16[32,1024]{1,0:T(8,128)(2,1)S(1)}, bf16[32,1024]{1,0:T(8,128)(2,1)S(1)}, u32[]{:S(2)}, u32[]{:S(2)}) collective-permute-start(bf16[32,1024]{1,0:T(8,128)(2,1)S(1)} %finish.1.refs_0_), channel_id=1, source_target_pairs={{0,64},{16,80},{32,96},{48,112},{64,0},{80,16},{96,32},{112,48},{1... | collective-permute-start | bytes 196616 | tf_op jit(solution)/shard_map/ppermute | solution.py:461
  80.5 8.5 %collective-permute-start.7 = (bf16[32,1024]{1,0:T(8,128)(2,1)S(1)}, bf16[32,1024]{1,0:T(8,128)(2,1)S(1)}, u32[]{:S(2)}, u32[]{:S(2)}) collective-permute-start(bf16[32,1024]{1,0:T(8,128)(2,1)S(1)} %finish.1.refs_0_), channel_id=1, source_target_pairs={{0,32},{16,48},{32,64},{48,80},{64,96},{80,112},{96,0},{112,16},{1... | collective-permute-start | bytes 196616 | tf_op jit(solution)/shard_map/ppermute | solution.py:461
  81.4 8.3 %collective-permute-start.6 = (bf16[32,1024]{1,0:T(8,128)(2,1)S(1)}, bf16[32,1024]{1,0:T(8,128)(2,1)S(1)}, u32[]{:S(2)}, u32[]{:S(2)}) collective-permute-start(bf16[32,1024]{1,0:T(8,128)(2,1)S(1)} %finish.1.refs_0_), channel_id=1, source_target_pairs={{0,96},{16,112},{32,0},{48,16},{64,32},{80,48},{96,64},{112,80},{1... | collective-permute-start | bytes 196616 | tf_op jit(solution)/shard_map/ppermute | solution.py:461
  83.2 6.6 %collective-permute-start.9 = (bf16[32,1024]{1,0:T(8,128)(2,1)S(1)}, bf16[32,1024]{1,0:T(8,128)(2,1)S(1)}, u32[]{:S(2)}, u32[]{:S(2)}) collective-permute-start(bf16[32,1024]{1,0:T(8,128)(2,1)S(1)} %finish.1.refs_0_), channel_id=1, source_target_pairs={{0,16},{16,0},{32,48},{48,32},{64,80},{80,64},{96,112},{112,96},{1... | collective-permute-start | bytes 196616 | tf_op jit(solution)/shard_map/ppermute | solution.py:461
  87.3 2.6 %collective-permute-start.12 = (bf16[32,1024]{1,0:T(8,128)(2,1)S(1)}, bf16[32,1024]{1,0:T(8,128)(2,1)S(1)}, u32[]{:S(2)}, u32[]{:S(2)}) collective-permute-start(bf16[32,1024]{1,0:T(8,128)(2,1)S(1)} %collective-permute-done.8.refs_3_), channel_id=1, source_target_pairs={{0,16},{16,0},{32,48},{48,32},{64,80},{80,64},{96,112},{112,96},{1... | collective-permute-start | bytes 196616 | tf_op jit(solution)/shard_map/ppermute | solution.py:461
  89.0 1.6 %collective-permute-start.11 = (bf16[32,1024]{1,0:T(8,128)(2,1)S(1)}, bf16[32,1024]{1,0:T(8,128)(2,1)S(1)}, u32[]{:S(2)}, u32[]{:S(2)}) collective-permute-start(bf16[32,1024]{1,0:T(8,128)(2,1)S(1)} %collective-permute-done.7.refs_2_), channel_id=1, source_target_pairs={{0,16},{16,0},{32,48},{48,32},{64,80},{80,64},{96,112},{112,96},{1... | collective-permute-start | bytes 196616 | tf_op jit(solution)/shard_map/ppermute | solution.py:461
  89.7 1.3 %collective-permute-start.10 = (bf16[32,1024]{1,0:T(8,128)(2,1)S(1)}, bf16[32,1024]{1,0:T(8,128)(2,1)S(1)}, u32[]{:S(2)}, u32[]{:S(2)}) collective-permute-start(bf16[32,1024]{1,0:T(8,128)(2,1)S(1)} %collective-permute-done.6.refs_1_), channel_id=1, source_target_pairs={{0,16},{16,0},{32,48},{48,32},{64,80},{80,64},{96,112},{112,96},{1... | collective-permute-start | bytes 196616 | tf_op jit(solution)/shard_map/ppermute | solution.py:461
